TPU v7x, 32 devices: a whole 2x2x4 slice. The times are simulated.
32 devices in a mesh: dp: 4 (over y, x), ctx: 8 (over z, core).
Axes of the slice: x: 2, y: 2, z: 4, core: 2. Of those that a mesh axis runs over, the one named last changes fastest.
Arguments:
- query_rows: bfloat16 [4, 1024, 2048], P('dp', 'ctx'), may hold values from -6 to 6
- key_rows: bfloat16 [4, 1024, 512], P('dp', 'ctx'), may hold values from -6 to 6
- value_rows: bfloat16 [4, 1024, 512], P('dp', 'ctx'), may hold values from -6 to 6
- out_grad: bfloat16 [4, 1024, 2048], P('dp', 'ctx'), may hold values from -6 to 6
- segment_ids: int32 [4, 1024], P('dp', 'ctx'), may hold values from 0 to 7, never falling along the last dimension, each value on 1 to 256 neighbouring positions
- home_rows: int32 [4, 128], P('dp', 'ctx'), may hold values from 0 to 3, as said below
Outputs:
- routed: bfloat16 [4, 8, 4, 8, 8, 2048], P('dp', 'ctx')
- query_grad: bfloat16 [4, 1024, 2048], P('dp', 'ctx')
- key_grad: bfloat16 [4, 1024, 512], P('dp', 'ctx')
- value_grad: bfloat16 [4, 1024, 512], P('dp', 'ctx')
Inputs may be any that keep to these rules, and one draw needn't show every extreme that they name: `segment_ids`: ids never fall along a sequence; every document holds 1 to 256 tokens, and some document holds exactly 256. `home_rows`: among the 16 stretches of one block, at most 8 name the same dp row; in every block column some dp row is named by exactly 8 stretches of every dp row's block.
All inputs are finite; a program needn't handle non-finite values.
Results may differ from a plain program's by a relative error of at most 0.014.
Values may be sent and summed in bfloat16 or wider, within the bound.
No kernel may reach another device: no remote copies, remote signals or barrier semaphores. Data moves between devices by JAX's collectives and lax.ppermute only.
A program may use at most 64 MiB of HBM per device.

v0:
```python
import math

import jax
import jax.numpy as jnp
from jax import lax
from jax.sharding import PartitionSpec as P

HEAD_DIM = 128
QHEADS = 16
KVHEADS = 4
SPAN = 2
GROUP = 4


def from_behind(value, axis, steps):
    count = lax.axis_size(axis)
    leading, last = (max(0, -steps), min(count, count - steps))
    return lax.ppermute(value, axis, [(source, source + steps) for source in range(leading, last)])


def forward_part(query_block, key_window, value_window, allowed):
    scaling = 1.0 / math.sqrt(HEAD_DIM)
    block_len = query_block.shape[0]
    window = key_window.shape[0]
    query_heads = query_block.reshape(block_len, KVHEADS, GROUP, HEAD_DIM)
    key_heads = key_window.reshape(window, KVHEADS, HEAD_DIM)
    value_heads = value_window.reshape(window, KVHEADS, HEAD_DIM)
    scores = (
        jnp.einsum("qkgd,nkd->kgqn", query_heads, key_heads, preferred_element_type=jnp.float32)
        * scaling
    )
    scores = jnp.where(allowed, scores, -jnp.inf)
    highest = jnp.max(scores, axis=-1, keepdims=True)
    exp_total = jnp.sum(jnp.exp(scores - highest), axis=-1, keepdims=True)
    log_total = highest + jnp.log(exp_total)
    weights = jnp.exp(scores - log_total)
    weights_low = weights.astype(jnp.bfloat16)
    attended = jnp.einsum(
        "kgqn,nkd->qkgd", weights_low, value_heads, preferred_element_type=jnp.float32
    )
    attended = attended.reshape(block_len, QHEADS * HEAD_DIM).astype(jnp.bfloat16)
    return (attended, weights, weights_low)


def backward_part(
    query_block, key_window, value_window, grad_block, attended, weights, weights_low
):
    scaling = 1.0 / math.sqrt(HEAD_DIM)
    block_len = query_block.shape[0]
    window = key_window.shape[0]
    query_heads = query_block.reshape(block_len, KVHEADS, GROUP, HEAD_DIM)
    key_heads = key_window.reshape(window, KVHEADS, HEAD_DIM)
    value_heads = value_window.reshape(window, KVHEADS, HEAD_DIM)
    grad_heads = grad_block.reshape(block_len, KVHEADS, GROUP, HEAD_DIM)
    attended_heads = attended.reshape(block_len, KVHEADS, GROUP, HEAD_DIM)
    row_delta = jnp.einsum(
        "qkgd,qkgd->kgq", grad_heads, attended_heads, preferred_element_type=jnp.float32
    )
    grad_weights = jnp.einsum(
        "qkgd,nkd->kgqn", grad_heads, value_heads, preferred_element_type=jnp.float32
    )
    grad_scores = (weights * (grad_weights - row_delta[..., None]) * scaling).astype(jnp.bfloat16)
    query_grad = jnp.einsum(
        "kgqn,nkd->qkgd", grad_scores, key_heads, preferred_element_type=jnp.float32
    )
    query_grad = query_grad.reshape(block_len, QHEADS * HEAD_DIM).astype(jnp.bfloat16)
    key_terms = jnp.einsum(
        "kgqn,qkgd->nkd", grad_scores, query_heads, preferred_element_type=jnp.float32
    )
    value_terms = jnp.einsum(
        "kgqn,qkgd->nkd", weights_low, grad_heads, preferred_element_type=jnp.float32
    )
    return (
        query_grad,
        key_terms.reshape(window, KVHEADS * HEAD_DIM),
        value_terms.reshape(window, KVHEADS * HEAD_DIM),
    )


def regroup(attended, home_ids):
    sources = lax.axis_size("dp")
    piece_count = home_ids.shape[0]
    capacity = max(2, 2 * piece_count // sources)
    piece_len = attended.shape[0] // piece_count
    flattened = attended.reshape(piece_count, piece_len * attended.shape[1])
    positions = jnp.arange(piece_count, dtype=jnp.int32)
    matching = (home_ids[:, None] == home_ids[None, :]) & (positions[None, :] < positions[:, None])
    slot_index = jnp.sum(matching.astype(jnp.int32), axis=1)
    select = (home_ids[None, None, :] == jnp.arange(sources, dtype=jnp.int32)[:, None, None]) & (
        slot_index[None, None, :] == jnp.arange(capacity, dtype=jnp.int32)[None, :, None]
    )
    select = select.reshape(sources * capacity, piece_count).astype(jnp.bfloat16)
    packed = jnp.dot(select, flattened, preferred_element_type=jnp.float32).astype(jnp.bfloat16)
    packed = packed.reshape(sources, capacity, piece_len * attended.shape[1])
    arrived = lax.all_to_all(packed, "dp", split_axis=0, concat_axis=0, tiled=True)
    return arrived.reshape(1, 1, sources, capacity, piece_len, attended.shape[1])


def on_device(query_rows, key_rows, value_rows, out_grad, segment_ids, home_rows):
    query_block = query_rows[0]
    key_block = key_rows[0]
    value_block = value_rows[0]
    grad_block = out_grad[0]
    seg_block = segment_ids[0].astype(jnp.bfloat16)
    home_ids = home_rows[0]
    block_len = query_block.shape[0]
    column = lax.axis_index("ctx")
    fetched = {}
    current = (key_block, value_block, seg_block)
    for distance in range(1, SPAN + 1):
        current = from_behind((current[0], current[1], current[2]), "ctx", 1)
        fetched[distance] = current
    ordered = [fetched[distance] for distance in range(SPAN, 0, -1)] + [
        (key_block, value_block, seg_block)
    ]
    key_window = jnp.concatenate([piece[0] for piece in ordered], axis=0)
    value_window = jnp.concatenate([piece[1] for piece in ordered], axis=0)
    seg_window = jnp.concatenate([piece[2] for piece in ordered], axis=0)
    window = key_window.shape[0]
    pos_query = column * block_len + jnp.arange(block_len, dtype=jnp.int32)
    pos_key = (column - SPAN) * block_len + jnp.arange(window, dtype=jnp.int32)
    allowed = (
        (seg_block[:, None] == seg_window[None, :])
        & (pos_key[None, :] <= pos_query[:, None])
        & (pos_key[None, :] >= 0)
    )
    attended, weights, weights_low = forward_part(query_block, key_window, value_window, allowed)
    query_grad, key_terms, value_terms = backward_part(
        query_block, key_window, value_window, grad_block, attended, weights, weights_low
    )
    routed = regroup(attended, home_ids)

    def term_rows(terms, distance):
        start = (SPAN - distance) * block_len
        return terms[start : start + block_len]

    carried = (term_rows(key_terms, SPAN), term_rows(value_terms, SPAN))
    for distance in range(SPAN - 1, -1, -1):
        moved = from_behind((carried[0], carried[1]), "ctx", -1)
        carried = (
            moved[0] + term_rows(key_terms, distance),
            moved[1] + term_rows(value_terms, distance),
        )
    key_total, value_total = carried
    return (
        routed,
        query_grad[None],
        key_total.astype(jnp.bfloat16)[None],
        value_total.astype(jnp.bfloat16)[None],
    )


def solution(mesh):
    placed = (
        P("dp", "ctx", None),
        P("dp", "ctx", None),
        P("dp", "ctx", None),
        P("dp", "ctx", None),
        P("dp", "ctx"),
        P("dp", "ctx"),
    )
    return jax.shard_map(
        on_device,
        mesh=mesh,
        in_specs=placed,
        out_specs=(
            P("dp", "ctx", None, None, None, None),
            P("dp", "ctx", None),
            P("dp", "ctx", None),
            P("dp", "ctx", None),
        ),
        check_vma=False,
    )
```

profile of v0, /device:TPU:19, one launch (start us, length us, event | category | flops | bytes accessed | tf_op | source)
XLA Modules:
  0.0 69.4 jit_solution(13405651537208938995)
XLA Ops:
  1.3 3.8 %collective-permute-start.2 = (bf16[128]{0:T(256)(128)(2,1)S(1)}, bf16[128]{0:T(256)(128)(2,1)S(1)}, u32[]{:S(2)}, u32[]{:S(2)}) collective-permute-start(bf16[128]{0:T(256)(128)(2,1)S(1)} %convert_bitcast_fusion), channel_id=1, source_target_pairs={{0,1},{1,2},{2,3},{3,4},{4,5},{5,6},{6,7},{8,9},{9,10},{10,11},{11... | collective-permute-start | bytes 776 | tf_op jit(solution)/shard_map/ppermute | solution.py:18
  5.1 1.0 %copy.59 = bf16[1,128,512]{1,2,0:T(8,128)(2,1)S(1)} copy(bf16[1,128,512]{2,1,0:T(8,128)(2,1)} %param.7) | data formatting | bytes 262144 | tf_op args[1]
  6.1 1.9 %collective-permute-start.4 = (bf16[128,512]{0,1:T(8,128)(2,1)S(1)}, bf16[128,512]{0,1:T(8,128)(2,1)S(1)}, u32[]{:S(2)}, u32[]{:S(2)}) collective-permute-start(bf16[128,512]{0,1:T(8,128)(2,1)S(1)} %bitcast.118), channel_id=1, source_target_pairs={{0,1},{1,2},{2,3},{3,4},{4,5},{5,6},{6,7},{8,9},{9,10},{10,11},{11... | collective-permute-start | bytes 393224 | tf_op jit(solution)/shard_map/ppermute | solution.py:18
  8.0 1.9 %collective-permute-start = (bf16[128,512]{1,0:T(8,128)(2,1)}, bf16[128,512]{1,0:T(8,128)(2,1)S(1)}, u32[]{:S(2)}, u32[]{:S(2)}) collective-permute-start(bf16[128,512]{1,0:T(8,128)(2,1)} %bitcast.120), channel_id=1, source_target_pairs={{0,1},{1,2},{2,3},{3,4},{4,5},{5,6},{6,7},{8,9},{9,10},{10,11},{11... | collective-permute-start | bytes 393224 | tf_op jit(solution)/shard_map/ppermute | solution.py:18
  10.0 0.9 %convert_reduce_fusion = s32[16]{0:T(128)S(1)} fusion(s32[16]{0:T(128)} %bitcast.134), kind=kLoop, calls=%fused_computation.29 | loop fusion | flops 1264 | bytes 128 | tf_op jit(solution)/shard_map/reduce_sum | solution.py:88
  10.9 1.0 %copy.58 = bf16[1,128,512]{1,2,0:T(8,128)(2,1)S(1)} copy(bf16[1,128,512]{2,1,0:T(8,128)(2,1)} %param.8) | data formatting | bytes 262144 | tf_op args[2]
  12.1 1.9 %collective-permute-start.3 = (bf16[128]{0:T(256)(128)(2,1)S(1)}, bf16[128]{0:T(256)(128)(2,1)S(1)}, u32[]{:S(2)}, u32[]{:S(2)}) collective-permute-start(bf16[128]{0:T(256)(128)(2,1)S(1)} %collective-permute-done.2), channel_id=1, source_target_pairs={{0,1},{1,2},{2,3},{3,4},{4,5},{5,6},{6,7},{8,9},{9,10},{10,11},{11... | collective-permute-start | bytes 776 | tf_op jit(solution)/shard_map/ppermute | solution.py:18
  14.0 1.3 %copy.103 = bf16[1,128,2048]{1,2,0:T(8,128)(2,1)S(1)} copy(bf16[1,128,2048]{2,1,0:T(8,128)(2,1)} %param.6) | data formatting | bytes 1048576 | tf_op jit(solution)/shard_map/reshape;squeeze | solution.py:25
  15.3 1.4 %reshape_squeeze.8 = bf16[128,4,4,128]{3,2,1,0:T(4,128)(2,1)S(1)} reshape(bf16[1,128,2048]{2,1,0:T(8,128)(2,1)} %param.9) | data formatting | bytes 1048576 | tf_op jit(solution)/shard_map/reshape;squeeze | solution.py:54
  17.3 1.9 %collective-permute-start.5 = (bf16[128,512]{0,1:T(8,128)(2,1)S(1)}, bf16[128,512]{0,1:T(8,128)(2,1)S(1)}, u32[]{:S(2)}, u32[]{:S(2)}) collective-permute-start(bf16[128,512]{0,1:T(8,128)(2,1)S(1)} %collective-permute-done.4), channel_id=1, source_target_pairs={{0,1},{1,2},{2,3},{3,4},{4,5},{5,6},{6,7},{8,9},{9,10},{10,11},{11... | collective-permute-start | bytes 393224 | tf_op jit(solution)/shard_map/ppermute | solution.py:18
  19.6 1.9 %collective-permute-start.1 = (bf16[128,512]{1,0:T(8,128)(2,1)S(1)}, bf16[128,512]{1,0:T(8,128)(2,1)S(1)}, u32[]{:S(2)}, u32[]{:S(2)}) collective-permute-start(bf16[128,512]{1,0:T(8,128)(2,1)S(1)} %collective-permute-done), channel_id=1, source_target_pairs={{0,1},{1,2},{2,3},{3,4},{4,5},{5,6},{6,7},{8,9},{9,10},{10,11},{11... | collective-permute-start | bytes 393224 | tf_op jit(solution)/shard_map/ppermute | solution.py:18
  23.1 0.9 %convolution_bitcast_fusion = f32[384,4,128]{0,2,1:T(8,128)S(1)} fusion(bf16[128,4,4,128]{0,3,2,1:T(8,128)(2,1)S(1)} %copy.77, f32[4,384,128,4]{2,1,3,0:T(8,128)S(1)} %get-tuple-element.23, f32[4,4,128]{2,1,0:T(4,128)S(1)} %bitcast.131, pred[128,384]{0,1:T(8,128)(4,1)S(1)} %and_and_fusion), kind=kOutput, calls=%fused_computation.11 | convolution fusion | flops 204472320 | bytes 4513792 | tf_op jit(solution)/shard_map/kgqn,qkgd->nkd/dot_general | solution.py:70
  25.6 4.3 %collective-permute-start.8 = (f32[128,512]{1,0:T(8,128)}, f32[128,512]{1,0:T(8,128)}, u32[]{:S(2)}, u32[]{:S(2)}) collective-permute-start(f32[128,512]{1,0:T(8,128)} %copy.78), channel_id=1, source_target_pairs={{1,0},{2,1},{3,2},{4,3},{5,4},{6,5},{7,6},{9,8},{10,9},{11,10},{12... | collective-permute-start | bytes 786440 | tf_op jit(solution)/shard_map/ppermute | solution.py:18
  30.1 3.6 %bitcast_convert_fusion = (f32[4,4,128,128]{2,3,1,0:T(8,128)S(1)}, bf16[4,128,4,128]{3,1,2,0:T(8,128)(2,1)}) fusion(f32[4,384,128,4]{2,1,3,0:T(8,128)} %copy-done, f32[4,4,128]{2,1,0:T(4,128)S(1)} %bitcast.132, pred[128,384]{0,1:T(8,128)(4,1)S(1)} %and_and_fusion, bf16[128,4,128]{0,2,1:T(8,128)(2,1)S(1)} %bitcast.121, ...), kind=kOutput, calls=%fused_computation.17 | convolution fusion | flops 206176256 | bytes 5169152 | tf_op jit(solution)/shard_map/kgqn,nkd->qkgd/dot_general | solution.py:38
  34.4 0.8 %multiply_reduce_fusion = f32[4,4,128]{1,0,2:T(4,128)S(1)} fusion(f32[4,4,128,128]{3,1,0,2:T(4,128)S(1)} %copy.91, bf16[128,4,4,128]{3,2,1,0:T(4,128)(2,1)S(1)} %reshape_squeeze.8), kind=kLoop, calls=%fused_computation.16 | loop fusion | flops 784384 | bytes 1581056
  35.3 3.4 %fusion.3 = bf16[4,4,128,384]{2,3,1,0:T(8,128)(2,1)S(1)} fusion(f32[4,384,128,4]{2,1,3,0:T(8,128)} %copy-done, bf16[128,4,4,128]{0,3,2,1:T(8,128)(2,1)} %copy-done.4, f32[4,4,128]{2,1,0:T(4,128)S(1)} %copy.92, f32[4,4,128]{2,1,0:T(4,128)S(1)} %bitcast.133, pred[128,384]{0,1:T(8,128)(4,1)} %copy-done.6, bf16[128,4,128]{0,2,1:T(8,128)(2,1)} %bitcast.122, ...), kind=kOutput, calls=%fused_computation.5 | convolution fusion | flops 208011264 | bytes 5701632 | tf_op jit(solution)/shard_map/qkgd,nkd->kgqn/dot_general | solution.py:59
  39.3 0.9 %fusion.25 = (f32[128,4,128]{0,2,1:T(8,128)}, f32[128,4,128]{0,2,1:T(8,128)}, f32[128,4,128]{0,2,1:T(8,128)S(1)}) fusion(f32[384,4,128]{0,2,1:T(8,128)S(1)} %convolution_bitcast_fusion.1), kind=kLoop, calls=%fused_computation.50 | loop fusion | bytes 1572864 | tf_op jit(solution)/shard_map/slice | solution.py:135
  40.2 0.8 %copy.73 = f32[128,512]{1,0:T(8,128)} copy(f32[128,512]{0,1:T(8,128)S(1)} %bitcast.116) | data formatting | bytes 524288 | tf_op jit(solution)/shard_map/slice | solution.py:135
  41.1 1.9 %collective-permute-start.6 = (f32[128,512]{1,0:T(8,128)}, f32[128,512]{1,0:T(8,128)}, u32[]{:S(2)}, u32[]{:S(2)}) collective-permute-start(f32[128,512]{1,0:T(8,128)} %copy.73), channel_id=1, source_target_pairs={{1,0},{2,1},{3,2},{4,3},{5,4},{6,5},{7,6},{9,8},{10,9},{11,10},{12... | collective-permute-start | bytes 786440 | tf_op jit(solution)/shard_map/ppermute | solution.py:18
  43.9 1.4 %fusion = bf16[4,8,16384]{2,1,0:T(8,128)(2,1)} fusion(bf16[16,16384]{1,0:T(8,128)(2,1)S(1)} %convert_element_type.62, pred[8,16]{1,0:T(8,128)(4,1)S(1)} %iota_compare_fusion.1, pred[4,16]{1,0:T(4,128)(4,1)S(1)} %iota_compare_fusion.2), kind=kOutput, calls=%fused_computation.1 | convolution fusion | flops 17302016 | bytes 1573056 | tf_op jit(solution)/shard_map/dot_general | solution.py:93
  45.2 3.7 %all-to-all-start = ((bf16[4,8,16384]{2,1,0:T(8,128)(2,1)}), bf16[4,8,16384]{2,1,0:T(8,128)(2,1)S(1)}, u32[]{:S(2)}, u32[]{:S(2)}) async-start(bf16[4,8,16384]{2,1,0:T(8,128)(2,1)} %fusion), calls=%async_computation | async-start | bytes 2097152 | tf_op jit(solution)/shard_map/all_to_all | solution.py:95
  49.1 1.1 %copy.74 = f32[128,512]{1,0:T(8,128)S(1)} copy(f32[128,512]{0,1:T(8,128)} %bitcast.114) | data formatting | bytes 524288 | tf_op jit(solution)/shard_map/slice | solution.py:135
  50.2 1.7 %add.51 = f32[128,512]{1,0:T(8,128)} add(f32[128,512]{1,0:T(8,128)} %collective-permute-done.8, f32[128,512]{1,0:T(8,128)S(1)} %copy.79) | non-fusion elementwise | flops 65536 | bytes 786432 | tf_op jit(solution)/shard_map/add | solution.py:142
  51.9 4.6 %collective-permute-start.9 = (f32[128,512]{1,0:T(8,128)}, f32[128,512]{1,0:T(8,128)}, u32[]{:S(2)}, u32[]{:S(2)}) collective-permute-start(f32[128,512]{1,0:T(8,128)} %add.51), channel_id=1, source_target_pairs={{1,0},{2,1},{3,2},{4,3},{5,4},{6,5},{7,6},{9,8},{10,9},{11,10},{12... | collective-permute-start | bytes 786440 | tf_op jit(solution)/shard_map/ppermute | solution.py:18
  56.6 1.7 %add.49 = f32[128,512]{1,0:T(8,128)} add(f32[128,512]{1,0:T(8,128)} %collective-permute-done.6, f32[128,512]{1,0:T(8,128)S(1)} %copy.74) | non-fusion elementwise | flops 65536 | bytes 786432 | tf_op jit(solution)/shard_map/add | solution.py:141
  58.3 1.9 %collective-permute-start.7 = (f32[128,512]{1,0:T(8,128)}, f32[128,512]{1,0:T(8,128)}, u32[]{:S(2)}, u32[]{:S(2)}) collective-permute-start(f32[128,512]{1,0:T(8,128)} %add.49), channel_id=1, source_target_pairs={{1,0},{2,1},{3,2},{4,3},{5,4},{6,5},{7,6},{9,8},{10,9},{11,10},{12... | collective-permute-start | bytes 786440 | tf_op jit(solution)/shard_map/ppermute | solution.py:18
  60.2 1.5 %convolution_convert_fusion.1 = bf16[4,128,4,128]{3,1,2,0:T(8,128)(2,1)S(1)} fusion(bf16[4,4,128,384]{2,3,1,0:T(8,128)(2,1)S(1)} %fusion.3, bf16[128,4,128]{2,0,1:T(8,128)(2,1)S(1)} %copy.63, bf16[128,4,128]{2,0,1:T(8,128)(2,1)} %copy-done.2, bf16[128,4,128]{2,0,1:T(8,128)(2,1)} %copy-done.3), kind=kOutput, calls=%fused_computation.13 | convolution fusion | flops 202768384 | bytes 2490368 | tf_op jit(solution)/shard_map/kgqn,nkd->qkgd/dot_general | solution.py:63
  61.8 1.1 %copy.75 = f32[128,512]{1,0:T(8,128)S(1)} copy(f32[128,512]{0,1:T(8,128)} %bitcast.113) | data formatting | bytes 524288 | tf_op jit(solution)/shard_map/slice | solution.py:135
  62.9 1.0 %copy.81 = bf16[1,128,2048]{2,1,0:T(8,128)(2,1)} copy(bf16[1,128,2048]{1,2,0:T(8,128)(2,1)S(1)} %bitcast.107) | data formatting | bytes 1048576
  63.9 1.6 %fusion.8 = bf16[1,128,512]{2,1,0:T(8,128)(2,1)} fusion(f32[128,512]{1,0:T(8,128)} %collective-permute-done.9, f32[128,512]{1,0:T(8,128)S(1)} %copy.80), kind=kLoop, calls=%fused_computation.25 | loop fusion | flops 131072 | bytes 655360 | tf_op jit(solution)/shard_map/broadcast_in_dim | solution.py:149
  66.2 1.6 %fusion.7 = bf16[1,128,512]{2,1,0:T(8,128)(2,1)} fusion(f32[128,512]{1,0:T(8,128)} %collective-permute-done.7, f32[128,512]{1,0:T(8,128)S(1)} %copy.75), kind=kLoop, calls=%fused_computation.24 | loop fusion | flops 131072 | bytes 655360 | tf_op jit(solution)/shard_map/broadcast_in_dim | solution.py:148
  67.9 1.6 %copy.106 = bf16[4,8,8,2048]{3,2,1,0:T(8,128)(2,1)} copy(bf16[4,8,8,2048]{3,1,2,0:T(8,128)(2,1)S(1)} %bitcast.106) | data formatting | bytes 2097152
  (59 shorter events, 8.1 us)
Async XLA Ops:
  1.3 10.8 %collective-permute-start.2 = (bf16[128]{0:T(256)(128)(2,1)S(1)}, bf16[128]{0:T(256)(128)(2,1)S(1)}, u32[]{:S(2)}, u32[]{:S(2)}) collective-permute-start(bf16[128]{0:T(256)(128)(2,1)S(1)} %convert_bitcast_fusion), channel_id=1, source_target_pairs={{0,1},{1,2},{2,3},{3,4},{4,5},{5,6},{6,7},{8,9},{9,10},{10,11},{11... | collective-permute-start | bytes 776 | tf_op jit(solution)/shard_map/ppermute | solution.py:18
  6.1 11.2 %collective-permute-start.4 = (bf16[128,512]{0,1:T(8,128)(2,1)S(1)}, bf16[128,512]{0,1:T(8,128)(2,1)S(1)}, u32[]{:S(2)}, u32[]{:S(2)}) collective-permute-start(bf16[128,512]{0,1:T(8,128)(2,1)S(1)} %bitcast.118), channel_id=1, source_target_pairs={{0,1},{1,2},{2,3},{3,4},{4,5},{5,6},{6,7},{8,9},{9,10},{10,11},{11... | collective-permute-start | bytes 393224 | tf_op jit(solution)/shard_map/ppermute | solution.py:18
  8.0 11.6 %collective-permute-start = (bf16[128,512]{1,0:T(8,128)(2,1)}, bf16[128,512]{1,0:T(8,128)(2,1)S(1)}, u32[]{:S(2)}, u32[]{:S(2)}) collective-permute-start(bf16[128,512]{1,0:T(8,128)(2,1)} %bitcast.120), channel_id=1, source_target_pairs={{0,1},{1,2},{2,3},{3,4},{4,5},{5,6},{6,7},{8,9},{9,10},{10,11},{11... | collective-permute-start | bytes 393224 | tf_op jit(solution)/shard_map/ppermute | solution.py:18
  11.9 18.1 %copy-start.7 = (bf16[1,128,512]{1,2,0:T(8,128)(2,1)}, bf16[1,128,512]{1,2,0:T(8,128)(2,1)S(1)}, u32[]{:S(2)}) copy-start(bf16[1,128,512]{1,2,0:T(8,128)(2,1)S(1)} %copy.58) | copy-start | bytes 393220
  12.1 5.1 %collective-permute-start.3 = (bf16[128]{0:T(256)(128)(2,1)S(1)}, bf16[128]{0:T(256)(128)(2,1)S(1)}, u32[]{:S(2)}, u32[]{:S(2)}) collective-permute-start(bf16[128]{0:T(256)(128)(2,1)S(1)} %collective-permute-done.2), channel_id=1, source_target_pairs={{0,1},{1,2},{2,3},{3,4},{4,5},{5,6},{6,7},{8,9},{9,10},{10,11},{11... | collective-permute-start | bytes 776 | tf_op jit(solution)/shard_map/ppermute | solution.py:18
  17.2 5.9 %copy-start.4 = (bf16[128,4,4,128]{0,3,2,1:T(8,128)(2,1)}, bf16[128,4,4,128]{0,3,2,1:T(8,128)(2,1)S(1)}, u32[]{:S(2)}) copy-start(bf16[128,4,4,128]{0,3,2,1:T(8,128)(2,1)S(1)} %copy.77) | copy-start | bytes 1572868
  17.3 4.4 %collective-permute-start.5 = (bf16[128,512]{0,1:T(8,128)(2,1)S(1)}, bf16[128,512]{0,1:T(8,128)(2,1)S(1)}, u32[]{:S(2)}, u32[]{:S(2)}) collective-permute-start(bf16[128,512]{0,1:T(8,128)(2,1)S(1)} %collective-permute-done.4), channel_id=1, source_target_pairs={{0,1},{1,2},{2,3},{3,4},{4,5},{5,6},{6,7},{8,9},{9,10},{10,11},{11... | collective-permute-start | bytes 393224 | tf_op jit(solution)/shard_map/ppermute | solution.py:18
  19.4 10.7 %copy-start.6 = (pred[128,384]{0,1:T(8,128)(4,1)}, pred[128,384]{0,1:T(8,128)(4,1)S(1)}, u32[]{:S(2)}) copy-start(pred[128,384]{0,1:T(8,128)(4,1)S(1)} %and_and_fusion) | copy-start | bytes 147460
  19.6 3.5 %copy-start.2 = (bf16[128,4,128]{2,0,1:T(8,128)(2,1)}, bf16[128,4,128]{2,0,1:T(8,128)(2,1)S(1)}, u32[]{:S(2)}) copy-start(bf16[128,4,128]{2,0,1:T(8,128)(2,1)S(1)} %copy.62) | copy-start | bytes 393220
  19.6 10.3 %collective-permute-start.1 = (bf16[128,512]{1,0:T(8,128)(2,1)S(1)}, bf16[128,512]{1,0:T(8,128)(2,1)S(1)}, u32[]{:S(2)}, u32[]{:S(2)}) collective-permute-start(bf16[128,512]{1,0:T(8,128)(2,1)S(1)} %collective-permute-done), channel_id=1, source_target_pairs={{0,1},{1,2},{2,3},{3,4},{4,5},{5,6},{6,7},{8,9},{9,10},{10,11},{11... | collective-permute-start | bytes 393224 | tf_op jit(solution)/shard_map/ppermute | solution.py:18
  21.6 8.5 %copy-start.8 = (bf16[128,512]{0,1:T(8,128)(2,1)}, bf16[128,512]{0,1:T(8,128)(2,1)S(1)}, u32[]{:S(2)}) copy-start(bf16[128,512]{0,1:T(8,128)(2,1)S(1)} %copy.57) | copy-start | bytes 393220
  21.8 1.3 %copy-start.3 = (bf16[128,4,128]{2,0,1:T(8,128)(2,1)}, bf16[128,4,128]{2,0,1:T(8,128)(2,1)S(1)}, u32[]{:S(2)}) copy-start(bf16[128,4,128]{2,0,1:T(8,128)(2,1)S(1)} %copy.61) | copy-start | bytes 393220
  22.4 1.6 %copy-start = (f32[4,384,128,4]{2,1,3,0:T(8,128)}, f32[4,384,128,4]{2,1,3,0:T(8,128)S(1)}, u32[]{:S(2)}) copy-start(f32[4,384,128,4]{2,1,3,0:T(8,128)S(1)} %get-tuple-element.23) | copy-start | bytes 9437188
  25.6 24.6 %collective-permute-start.8 = (f32[128,512]{1,0:T(8,128)}, f32[128,512]{1,0:T(8,128)}, u32[]{:S(2)}, u32[]{:S(2)}) collective-permute-start(f32[128,512]{1,0:T(8,128)} %copy.78), channel_id=1, source_target_pairs={{1,0},{2,1},{3,2},{4,3},{5,4},{6,5},{7,6},{9,8},{10,9},{11,10},{12... | collective-permute-start | bytes 786440 | tf_op jit(solution)/shard_map/ppermute | solution.py:18
  30.1 3.7 %copy-start.9 = (bf16[128,512]{0,1:T(8,128)(2,1)}, bf16[128,512]{0,1:T(8,128)(2,1)S(1)}, u32[]{:S(2)}) copy-start(bf16[128,512]{0,1:T(8,128)(2,1)S(1)} %copy.56) | copy-start | bytes 393220
  38.7 4.3 %copy-start.10 = (s32[1,16]{1,0:T(1,128)S(1)}, s32[1,16]{1,0:T(1,128)}, u32[]{:S(2)}) copy-start(s32[1,16]{1,0:T(1,128)} %param.11) | copy-start | bytes 196
  38.7 4.3 %copy-start.5 = (bf16[4,128,4,128]{3,1,2,0:T(8,128)(2,1)S(1)}, bf16[4,128,4,128]{3,1,2,0:T(8,128)(2,1)}, u32[]{:S(2)}) copy-start(bf16[4,128,4,128]{3,1,2,0:T(8,128)(2,1)} %get-tuple-element.25) | copy-start | bytes 1572868
  40.2 8.8 %copy-start.1 = (f32[128,4,128]{0,2,1:T(8,128)S(1)}, f32[128,4,128]{0,2,1:T(8,128)}, u32[]{:S(2)}) copy-start(f32[128,4,128]{0,2,1:T(8,128)} %get-tuple-element.17) | copy-start | bytes 786436
  41.1 15.5 %collective-permute-start.6 = (f32[128,512]{1,0:T(8,128)}, f32[128,512]{1,0:T(8,128)}, u32[]{:S(2)}, u32[]{:S(2)}) collective-permute-start(f32[128,512]{1,0:T(8,128)} %copy.73), channel_id=1, source_target_pairs={{1,0},{2,1},{3,2},{4,3},{5,4},{6,5},{7,6},{9,8},{10,9},{11,10},{12... | collective-permute-start | bytes 786440 | tf_op jit(solution)/shard_map/ppermute | solution.py:18
  45.2 22.6 %all-to-all-start = ((bf16[4,8,16384]{2,1,0:T(8,128)(2,1)}), bf16[4,8,16384]{2,1,0:T(8,128)(2,1)S(1)}, u32[]{:S(2)}, u32[]{:S(2)}) async-start(bf16[4,8,16384]{2,1,0:T(8,128)(2,1)} %fusion), calls=%async_computation | async-start | bytes 2097152 | tf_op jit(solution)/shard_map/all_to_all | solution.py:95
  51.9 12.0 %collective-permute-start.9 = (f32[128,512]{1,0:T(8,128)}, f32[128,512]{1,0:T(8,128)}, u32[]{:S(2)}, u32[]{:S(2)}) collective-permute-start(f32[128,512]{1,0:T(8,128)} %add.51), channel_id=1, source_target_pairs={{1,0},{2,1},{3,2},{4,3},{5,4},{6,5},{7,6},{9,8},{10,9},{11,10},{12... | collective-permute-start | bytes 786440 | tf_op jit(solution)/shard_map/ppermute | solution.py:18
  58.3 8.0 %collective-permute-start.7 = (f32[128,512]{1,0:T(8,128)}, f32[128,512]{1,0:T(8,128)}, u32[]{:S(2)}, u32[]{:S(2)}) collective-permute-start(f32[128,512]{1,0:T(8,128)} %add.49), channel_id=1, source_target_pairs={{1,0},{2,1},{3,2},{4,3},{5,4},{6,5},{7,6},{9,8},{10,9},{11,10},{12... | collective-permute-start | bytes 786440 | tf_op jit(solution)/shard_map/ppermute | solution.py:18
where the time goes:
time: 70.3 us; the launch traced here: 69.4 us
  starting transfers between devices  29.8 us (42%)
  local copies, waits for them, and re-layouts  15.8 us (22%)
  matrix products  12 us (17%)
  other arithmetic  10 us (14%)
  between operations  1.11 us (2%)
  waiting for transfers between devices  0.76 us (1%)
    ppermute x10, starting transfers between devices, from_behind(): lax.ppermute(value, axis, [(source, source + steps) for source in range(l...  26.1 us
    slice x8, local copies, waits for them, and re-layouts, term_rows(): return terms[start:start + block_len]  5.74 us
    unnamed x27, local copies, waits for them, and re-layouts  5.32 us
    all_to_all x1, starting transfers between devices, regroup(): lax.all_to_all(packed, 'dp', split_axis=0, concat_axis=0, tiled=True)  3.74 us
    dot_general x1, matrix products, forward_part(): jnp.einsum('kgqn,nkd->qkgd', weights_low, value_heads, preferred_element_...  3.64 us
    dot_general x1, matrix products, backward_part(): jnp.einsum('qkgd,nkd->kgqn', grad_heads, value_heads, preferred_element_t...  3.41 us
    another operation x2, local copies, waits for them, and re-layouts, backward_part(): grad_heads = grad_block.reshape(block_len, KVHEADS, GROUP, HEAD_DIM)  1.87 us
    add x1, other arithmetic, on_device(): moved[0] + term_rows(key_terms, distance)  1.7 us
  transfers between devices with their start and end apart: 11, of which 1 were waited for; matrix products, arithmetic and copies ran while one was open for 51% of the time, Pallas kernels for 0%

commit v1 on v0

v1 whole, which is shorter than its diff:
```python
import functools
import math

import jax
import jax.numpy as jnp
from jax import lax
from jax.experimental import pallas as pl
from jax.experimental.pallas import tpu as pltpu
from jax.sharding import PartitionSpec as P

HEAD_DIM = 128
GROUP = 4
SEG_ROWS = 16
F32 = jnp.float32
BF16 = jnp.bfloat16
NEG = -1e30

NT = (((1,), (1,)), ((), ()))
NN = (((1,), (0,)), ((), ()))
TN = (((0,), (0,)), ((), ()))


def dot(a, b, dims):
    return lax.dot_general(a, b, dims, preferred_element_type=F32)


def stacked(ref, g):
    heads = [
        ref[:, (g * GROUP + h) * HEAD_DIM : (g * GROUP + h + 1) * HEAD_DIM] for h in range(GROUP)
    ]
    return jnp.concatenate(heads, axis=0)


def window(g, block, own_ref, r_ref, near):
    cols = slice(g * HEAD_DIM, (g + 1) * HEAD_DIM)
    keys = (own_ref[0:block, cols], near[0:block, cols], r_ref[0:block, cols])
    values = (
        own_ref[block : 2 * block, cols],
        near[block : 2 * block, cols],
        r_ref[block : 2 * block, cols],
    )
    return keys, values


def near_block(column, b_ref, c_ref):
    return jnp.where(lax.rem(column, 2) == 0, c_ref[...], b_ref[...])


def triangle(block, copies):
    key_pos = lax.broadcasted_iota(jnp.int32, (block, copies * block), 0)
    query_pos = lax.broadcasted_iota(jnp.int32, (block, copies * block), 1)
    return key_pos <= lax.rem(query_pos, block)


def repartner(index, k, count):
    if count & (count - 1) == 0:
        return index ^ k
    return lax.rem(index + k, count)


def fwd_kernel(n_dp, capacity, info_ref, home_ref, q_ref, own_ref, r_ref, b_ref, c_ref, *rest):
    p_ref = rest[0]
    sends = rest[1 : 1 + n_dp]
    packed, counts, sems = rest[1 + n_dp :]
    block = q_ref.shape[0]
    column, row = info_ref[0], info_ref[1]
    pieces = home_ref.shape[0]
    piece_len = block // pieces
    packed[...] = jnp.zeros_like(packed)
    near = near_block(column, b_ref, c_ref)

    def seg_of(value):
        return value[2 * block : 2 * block + SEG_ROWS, 0:block].astype(F32)[0:1]

    seg_own, seg_near, seg_far = seg_of(own_ref), seg_of(near), seg_of(r_ref)
    first = seg_own[:, 0:1]
    reach = jnp.where(column >= 1, jnp.sum((seg_near == first).astype(F32), axis=1, keepdims=True), 0.0)
    reach = reach + jnp.where(
        column >= 2, jnp.sum((seg_far == first).astype(F32), axis=1, keepdims=True), 0.0
    )
    key_pos = lax.broadcasted_iota(jnp.int32, (block, block), 0).astype(F32)
    tri = triangle(block, 1)
    seg_rows = jnp.broadcast_to(seg_own, (block, block))
    joined = seg_rows == first
    own_ok = seg_rows == seg_rows.T
    far_ok = (key_pos >= 2 * block - reach) & joined
    near_ok = (key_pos >= block - reach) & joined
    bias_x = jnp.where((tri & own_ok) | (~tri & far_ok), 0.0, NEG)
    bias_n = jnp.where(near_ok, 0.0, NEG)
    bias_x = jnp.concatenate([bias_x] * GROUP, axis=1)
    bias_n = jnp.concatenate([bias_n] * GROUP, axis=1)
    tri_g = triangle(block, GROUP)
    scaling = math.log2(math.e) / math.sqrt(HEAD_DIM)

    for d in range(n_dp):
        counts[d] = 0
    place = []
    for m in range(pieces):
        home = home_ref[m]
        slot = counts[home]
        counts[home] = slot + 1
        place.append(((home ^ row) if n_dp & (n_dp - 1) == 0 else lax.rem(home - row + n_dp, n_dp), slot))

    for g in range(own_ref.shape[1] // HEAD_DIM):
        keys, values = window(g, block, own_ref, r_ref, near)
        queries = stacked(q_ref, g)
        s_x = jnp.where(tri_g, dot(keys[0], queries, NT), dot(keys[2], queries, NT))
        s_x = s_x * scaling + bias_x
        s_n = dot(keys[1], queries, NT) * scaling + bias_n
        highest = jnp.max(jnp.maximum(s_x, s_n), axis=0, keepdims=True)
        e_x = jnp.exp2(s_x - highest)
        e_n = jnp.exp2(s_n - highest)
        inverse = 1.0 / jnp.sum(e_x + e_n, axis=0, keepdims=True)
        w_x = e_x * inverse
        w_n = (e_n * inverse).astype(BF16)
        p_ref[g, 0:block] = w_x.astype(BF16)
        p_ref[g, block : 2 * block] = w_n
        w_0 = jnp.where(tri_g, w_x, 0.0).astype(BF16)
        w_2 = jnp.where(tri_g, 0.0, w_x).astype(BF16)
        weights = jnp.concatenate([w_0, w_n, w_2], axis=0)
        attended = dot(weights, jnp.concatenate(values, axis=0), TN)
        for h in range(GROUP):
            cols = slice((g * GROUP + h) * HEAD_DIM, (g * GROUP + h + 1) * HEAD_DIM)
            tile = attended[h * block : (h + 1) * block].reshape(pieces, piece_len, HEAD_DIM)
            for m in range(pieces):
                packed[place[m][0], place[m][1], :, cols] = tile[m].astype(BF16)
    copies = [pltpu.make_async_copy(packed.at[k], sends[k], sems.at[k]) for k in range(n_dp)]
    for copy in copies:
        copy.start()
    for copy in copies:
        copy.wait()


def bwd_kernel(info_ref, q_ref, do_ref, own_ref, r_ref, b_ref, c_ref, p_ref, dq_ref, d0_ref, d1_ref, d2_ref):
    block = q_ref.shape[0]
    column = info_ref[0]
    near = near_block(column, b_ref, c_ref)
    tri_g = triangle(block, GROUP)
    scaling = 1.0 / math.sqrt(HEAD_DIM)
    for g in range(own_ref.shape[1] // HEAD_DIM):
        keys, values = window(g, block, own_ref, r_ref, near)
        queries, grads = stacked(q_ref, g), stacked(do_ref, g)
        w_x = p_ref[g, 0:block].astype(F32)
        w_n = p_ref[g, block : 2 * block]
        w_nf = w_n.astype(F32)
        gw_x = jnp.where(tri_g, dot(values[0], grads, NT), dot(values[2], grads, NT))
        gw_n = dot(values[1], grads, NT)
        delta = jnp.sum(w_x * gw_x + w_nf * gw_n, axis=0, keepdims=True)
        gs_x = w_x * (gw_x - delta) * scaling
        gs_n = (w_nf * (gw_n - delta) * scaling).astype(BF16)
        gs_0 = jnp.where(tri_g, gs_x, 0.0).astype(BF16)
        gs_2 = jnp.where(tri_g, 0.0, gs_x).astype(BF16)
        w_0 = jnp.where(tri_g, w_x, 0.0).astype(BF16)
        w_2 = jnp.where(tri_g, 0.0, w_x).astype(BF16)
        cols = slice(g * HEAD_DIM, (g + 1) * HEAD_DIM)
        d2_ref[0:block, cols] = dot(gs_2, queries, NN).astype(d2_ref.dtype)
        d2_ref[block : 2 * block, cols] = dot(w_2, grads, NN).astype(d2_ref.dtype)
        d1_ref[0:block, cols] = dot(gs_n, queries, NN).astype(d1_ref.dtype)
        d1_ref[block : 2 * block, cols] = dot(w_n, grads, NN).astype(d1_ref.dtype)
        d0_ref[0:block, cols] = dot(gs_0, queries, NN)
        d0_ref[block : 2 * block, cols] = dot(w_0, grads, NN)
        dq = dot(jnp.concatenate([gs_0, gs_n, gs_2], axis=0), jnp.concatenate(keys, axis=0), TN)
        for h in range(GROUP):
            heads = slice((g * GROUP + h) * HEAD_DIM, (g * GROUP + h + 1) * HEAD_DIM)
            dq_ref[:, heads] = dq[h * block : (h + 1) * block].astype(dq_ref.dtype)


def final_kernel(n_ctx, info_ref, d0_ref, b_ref, r_ref, dk_ref, dv_ref):
    block = dk_ref.shape[0]
    column = info_ref[0]
    total = d0_ref[...]
    total = total + jnp.where(lax.rem(column, 2) == 0, b_ref[...].astype(F32), 0.0)
    total = total + jnp.where(column + 2 < n_ctx, r_ref[...].astype(F32), 0.0)
    dk_ref[...] = total[0:block].astype(dk_ref.dtype)
    dv_ref[...] = total[block : 2 * block].astype(dv_ref.dtype)


def join_kernel(n_dp, info_ref, *rest):
    pieces, out_ref, sems = rest[:n_dp], rest[n_dp], rest[n_dp + 1]
    row = info_ref[1]
    copies = []
    for k in range(n_dp):
        source = row ^ k if n_dp & (n_dp - 1) == 0 else lax.rem(row - k + n_dp, n_dp)
        copies.append(pltpu.make_async_copy(pieces[k], out_ref.at[0, 0, source], sems.at[k]))
    for copy in copies:
        copy.start()
    for copy in copies:
        copy.wait()


VMEM = pl.BlockSpec(memory_space=pltpu.VMEM)
SMEM = pl.BlockSpec(memory_space=pltpu.SMEM)
HBM = pl.BlockSpec(memory_space=pl.ANY)


def params():
    return pltpu.CompilerParams(vmem_limit_bytes=32 * 1024 * 1024)


def cost(flops, nbytes):
    return pl.CostEstimate(flops=flops, bytes_accessed=nbytes, transcendentals=0)


def swap(value):
    count = lax.axis_size("ctx")
    return lax.ppermute(value, "ctx", [(i, i ^ 1) for i in range(count)])


def ring(value, steps):
    count = lax.axis_size("ctx")
    return lax.ppermute(value, "ctx", [(i, (i + steps) % count) for i in range(count)])


def exchange(value, k):
    count = lax.axis_size("dp")
    if count & (count - 1) == 0:
        pairs = [(i, i ^ k) for i in range(count)]
    else:
        pairs = [(i, (i + k) % count) for i in range(count)]
    return lax.ppermute(value, "dp", pairs)


def on_device(query_rows, key_rows, value_rows, out_grad, segment_ids, home_rows):
    n_dp, n_ctx = lax.axis_size("dp"), lax.axis_size("ctx")
    query, grad = query_rows[0], out_grad[0]
    block, width = query.shape
    kv_width = key_rows.shape[2]
    heads = kv_width // HEAD_DIM
    home = home_rows[0]
    pieces = home.shape[0]
    capacity = max(2, 2 * pieces // n_dp)
    piece_len = block // pieces
    column = lax.axis_index("ctx")
    info = jnp.stack([column, lax.axis_index("dp")]).astype(jnp.int32)
    seg = jnp.pad(segment_ids.astype(BF16), ((0, SEG_ROWS - 1), (0, kv_width - block)))
    own = jnp.concatenate([key_rows[0], value_rows[0], seg], axis=0)
    far = ring(own, 2)
    beside = swap(own)
    crossed = swap(far)

    pairs = 2 * block * block * GROUP * heads * HEAD_DIM
    outs = pl.pallas_call(
        functools.partial(fwd_kernel, n_dp, capacity),
        out_shape=[jax.ShapeDtypeStruct((heads, 2 * block, GROUP * block), BF16)]
        + [jax.ShapeDtypeStruct((capacity, piece_len, width), BF16)] * n_dp,
        in_specs=[SMEM, SMEM] + [VMEM] * 5,
        out_specs=[VMEM] + [HBM] * n_dp,
        scratch_shapes=[
            pltpu.VMEM((n_dp, capacity, piece_len, width), BF16),
            pltpu.SMEM((n_dp,), jnp.int32),
            pltpu.SemaphoreType.DMA((n_dp,)),
        ],
        compiler_params=params(),
        cost_estimate=cost(6 * pairs, 4 << 20),
        name="attend",
    )(info, home, query, own, far, beside, crossed)
    weights, sends = outs[0], outs[1:]
    arrived = [sends[0]] + [exchange(sends[k], k) for k in range(1, n_dp)]
    dq, d0, d1, d2 = pl.pallas_call(
        bwd_kernel,
        out_shape=[
            jax.ShapeDtypeStruct((block, width), BF16),
            jax.ShapeDtypeStruct((2 * block, kv_width), F32),
            jax.ShapeDtypeStruct((2 * block, kv_width), BF16),
            jax.ShapeDtypeStruct((2 * block, kv_width), BF16),
        ],
        in_specs=[SMEM] + [VMEM] * 7,
        out_specs=[VMEM] * 4,
        compiler_params=params(),
        cost_estimate=cost(12 * pairs, 4 << 20),
        name="gradients",
    )(info, query, grad, own, far, beside, crossed, weights)
    d1_in = swap(d1)
    d2_sum = (d2.astype(F32) + jnp.where(column % 2 == 1, d1_in.astype(F32), 0.0)).astype(BF16)
    d2_in = ring(d2_sum, -2)
    dk, dv = pl.pallas_call(
        functools.partial(final_kernel, n_ctx),
        out_shape=[jax.ShapeDtypeStruct((block, kv_width), BF16)] * 2,
        in_specs=[SMEM] + [VMEM] * 3,
        out_specs=[VMEM] * 2,
        compiler_params=params(),
        cost_estimate=cost(0, 2 << 20),
        name="total",
    )(info, d0, d1_in, d2_in)
    routed = pl.pallas_call(
        functools.partial(join_kernel, n_dp),
        out_shape=jax.ShapeDtypeStruct((1, 1, n_dp, capacity, piece_len, width), BF16),
        in_specs=[SMEM] + [HBM] * n_dp,
        out_specs=HBM,
        scratch_shapes=[pltpu.SemaphoreType.DMA((n_dp,))],
        compiler_params=params(),
        cost_estimate=cost(0, 2 << 20),
        name="join",
    )(info, *arrived)
    return routed, dq[None], dk[None], dv[None]


def solution(mesh):
    rows = P("dp", "ctx", None)
    return jax.shard_map(
        on_device,
        mesh=mesh,
        in_specs=(rows, rows, rows, rows, P("dp", "ctx"), P("dp", "ctx")),
        out_specs=(P("dp", "ctx", None, None, None, None), rows, rows, rows),
        check_vma=False,
    )
```

time: 70.3 us -> 41.8 us (0.59)
  the two profiles are of different devices: /device:TPU:19 before, /device:TPU:0 now
where the time goes in v1:
time: 41.8 us; the launch traced here: 41.6 us
  waiting for transfers between devices  20.2 us (48%)
  Pallas kernels  9.68 us (23%)
  starting transfers between devices  8.52 us (20%)
  other arithmetic  1.86 us (4%)
  between operations  0.69 us (2%)
  local copies, waits for them, and re-layouts  0.66 us (2%)
    ppermute x3, waiting for transfers between devices, exchange(): return lax.ppermute(value, 'dp', pairs)  10 us
    ppermute x2, waiting for transfers between devices, ring(): lax.ppermute(value, 'ctx', [(i, (i + steps) % count) for i in range(count)])  8.68 us
    ppermute x2, starting transfers between devices, ring(): lax.ppermute(value, 'ctx', [(i, (i + steps) % count) for i in range(count)])  4.87 us
    pallas_call x1, Pallas kernels, on_device(): pl.pallas_call(bwd_kernel, out_shape=[jax.ShapeDtypeStruct((block, width)...  4.06 us
    ppermute x3, starting transfers between devices, exchange(): return lax.ppermute(value, 'dp', pairs)  3.5 us
    pallas_call x1, Pallas kernels, on_device(): pl.pallas_call(functools.partial(fwd_kernel, n_dp, capacity), out_shape=[...  2.76 us
    pallas_call x1, Pallas kernels, on_device(): pl.pallas_call(functools.partial(join_kernel, n_dp), out_shape=jax.ShapeD...  1.54 us
    ppermute x3, waiting for transfers between devices, swap(): return lax.ppermute(value, 'ctx', [(i, i ^ 1) for i in range(count)])  1.48 us
  transfers between devices with their start and end apart: 8, of which 4 were waited for; matrix products, arithmetic and copies ran while one was open for 0% of the time, Pallas kernels for 4%

profile of v1, /device:TPU:0, one launch (start us, length us, event | category | flops | bytes accessed | tf_op | source)
XLA Modules:
  0.0 41.6 jit_solution(2477298258319297073)
XLA Ops:
  0.6 0.0 copy-start
  0.6 0.7 %convert_element_type.14 = bf16[1,128]{1,0:T(2,128)(2,1)S(1)} convert(s32[1,128]{1,0:T(1,128)} %param.10) | non-fusion elementwise | flops 128 | bytes 768 | tf_op jit(solution)/shard_map/convert_element_type | solution.py:235
  1.4 1.0 %fusion.1.own_ref = bf16[272,512]{1,0:T(8,128)(2,1)S(1)} fusion(bf16[1,128]{1,0:T(2,128)(2,1)S(1)} %convert_element_type.14, bf16[128,512]{1,0:T(8,128)(2,1)} %bitcast.14, bf16[128,512]{1,0:T(8,128)(2,1)} %bitcast.15), kind=kLoop, calls=%fused_computation.3 | loop fusion | flops 1114112 | bytes 540928 | tf_op jit(solution)/shard_map/concatenate | solution.py:236
  2.3 3.1 %collective-permute-start = (bf16[272,512]{1,0:T(8,128)(2,1)S(1)}, bf16[272,512]{1,0:T(8,128)(2,1)S(1)}, u32[]{:S(2)}, u32[]{:S(2)}) collective-permute-start(bf16[272,512]{1,0:T(8,128)(2,1)S(1)} %fusion.1.own_ref), channel_id=1, source_target_pairs={{0,2},{1,3},{2,4},{3,5},{4,6},{5,7},{6,0},{7,1},{8,10},{9,11},{10,... | collective-permute-start | bytes 835592 | tf_op jit(solution)/shard_map/ppermute | solution.py:211
  5.4 0.0 collective-permute-start.1
  5.4 8.7 %collective-permute-done.r_ref = bf16[272,512]{1,0:T(8,128)(2,1)S(1)} collective-permute-done((bf16[272,512]{1,0:T(8,128)(2,1)S(1)}, bf16[272,512]{1,0:T(8,128)(2,1)S(1)}, u32[]{:S(2)}, u32[]{:S(2)}) %collective-permute-start) | collective-permute-done | bytes 278560 | tf_op jit(solution)/shard_map/ppermute | solution.py:211
  14.1 0.0 collective-permute-start.2
  14.1 0.1 pad_add_fusion.info_ref
  14.2 0.0 collective-permute-done.1.b_ref
  14.2 1.5 %collective-permute-done.2.c_ref = bf16[272,512]{1,0:T(8,128)(2,1)S(1)} collective-permute-done((bf16[272,512]{1,0:T(8,128)(2,1)S(1)}, bf16[272,512]{1,0:T(8,128)(2,1)S(1)}, u32[]{:S(2)}, u32[]{:S(2)}) %collective-permute-start.2) | collective-permute-done | bytes 278560 | tf_op jit(solution)/shard_map/ppermute | solution.py:206
  15.7 0.0 copy-start.2
  15.7 0.0 copy-done
  15.7 0.7 %copy-done.2 = s32[1,16]{1,0:T(1,128)S(1)} copy-done((s32[1,16]{1,0:T(1,128)S(1)}, s32[1,16]{1,0:T(1,128)}, u32[]{:S(2)}) %copy-start.2) | copy-done | bytes 88
  16.3 0.0 copy-start.1
  16.3 2.8 %attend.1 = (bf16[4,256,512]{2,1,0:T(8,128)(2,1)S(1)}, bf16[8,8,2048]{2,1,0:T(8,128)(2,1)S(1)}, bf16[8,8,2048]{2,1,0:T(8,128)(2,1)S(1)}, bf16[8,8,2048]{2,1,0:T(8,128)(2,1)S(1)}, bf16[8,8,2048]{2,1,0:T(8,128)(2,1)S(1)}) custom-call(s32[2]{0:T(128)S(1)} %pad_add_fusion.info_ref, s32[16]{0:T(128)S(1)} %bitcast.13, bf16[128,2048]{1,0:T(8,128)(2,1)S(1)} %bitcast.10, ...), custom_call_target="tpu_custom_call" | custom-call | flops 402653184 | bytes 4194304 | tf_op jit(solution)/shard_map/attend/pallas_call | solution.py:242
  19.1 0.0 copy-done.1
  19.1 4.1 %gradients.1 = (bf16[128,2048]{1,0:T(8,128)(2,1)}, f32[256,512]{1,0:T(8,128)S(1)}, bf16[256,512]{1,0:T(8,128)(2,1)}, bf16[256,512]{1,0:T(8,128)(2,1)S(1)}) custom-call(s32[2]{0:T(128)S(1)} %pad_add_fusion.info_ref, bf16[128,2048]{1,0:T(8,128)(2,1)S(1)} %bitcast.11, bf16[128,2048]{1,0:T(8,128)(2,1)S(1)} %bitcast.12, bf16[272,512]{1,0:T(8,128)(2,1)S(1)} %fusion.1.own_ref, ...), custom_call_target="tpu_custom_call" | custom-call | flops 805306368 | bytes 4194304 | tf_op jit(solution)/shard_map/gradients/pallas_call | solution.py:259
  23.2 0.1 collective-permute-start.6
  23.3 1.5 %collective-permute-start.3 = (bf16[8,8,2048]{2,1,0:T(8,128)(2,1)S(1)}, bf16[8,8,2048]{2,1,0:T(8,128)(2,1)S(1)}, u32[]{:S(2)}, u32[]{:S(2)}) collective-permute-start(bf16[8,8,2048]{2,1,0:T(8,128)(2,1)S(1)} %get-tuple-element.16), channel_id=1, source_target_pairs={{0,8},{8,0},{16,24},{24,16},{1,9},{9,1},{17,25},{25,17},{2,10},{10... | collective-permute-start | bytes 786440 | tf_op jit(solution)/shard_map/ppermute | solution.py:220
  24.8 1.5 %collective-permute-start.4 = (bf16[8,8,2048]{2,1,0:T(8,128)(2,1)S(1)}, bf16[8,8,2048]{2,1,0:T(8,128)(2,1)S(1)}, u32[]{:S(2)}, u32[]{:S(2)}) collective-permute-start(bf16[8,8,2048]{2,1,0:T(8,128)(2,1)S(1)} %get-tuple-element.17), channel_id=1, source_target_pairs={{0,16},{8,24},{16,0},{24,8},{1,17},{9,25},{17,1},{25,9},{2,18},{10... | collective-permute-start | bytes 786440 | tf_op jit(solution)/shard_map/ppermute | solution.py:220
  26.3 0.5 %collective-permute-start.5 = (bf16[8,8,2048]{2,1,0:T(8,128)(2,1)S(1)}, bf16[8,8,2048]{2,1,0:T(8,128)(2,1)S(1)}, u32[]{:S(2)}, u32[]{:S(2)}) collective-permute-start(bf16[8,8,2048]{2,1,0:T(8,128)(2,1)S(1)} %get-tuple-element.18), channel_id=1, source_target_pairs={{0,24},{8,16},{16,8},{24,0},{1,25},{9,17},{17,9},{25,1},{2,26},{10... | collective-permute-start | bytes 786440 | tf_op jit(solution)/shard_map/ppermute | solution.py:220
  26.8 0.0 collective-permute-done.6.b_ref
  26.8 0.1 add_convert_fusion
  26.9 1.8 %collective-permute-start.7 = (bf16[256,512]{1,0:T(8,128)(2,1)S(1)}, bf16[256,512]{1,0:T(8,128)(2,1)S(1)}, u32[]{:S(2)}, u32[]{:S(2)}) collective-permute-start(bf16[256,512]{1,0:T(8,128)(2,1)S(1)} %add_convert_fusion), channel_id=1, source_target_pairs={{0,6},{1,7},{2,0},{3,1},{4,2},{5,3},{6,4},{7,5},{8,14},{9,15},{10,... | collective-permute-start | bytes 786440 | tf_op jit(solution)/shard_map/ppermute | solution.py:211
  28.7 3.7 %collective-permute-done.3.rest_1_ = bf16[8,8,2048]{2,1,0:T(8,128)(2,1)S(1)} collective-permute-done((bf16[8,8,2048]{2,1,0:T(8,128)(2,1)S(1)}, bf16[8,8,2048]{2,1,0:T(8,128)(2,1)S(1)}, u32[]{:S(2)}, u32[]{:S(2)}) %collective-permute-start.3) | collective-permute-done | bytes 262176 | tf_op jit(solution)/shard_map/ppermute | solution.py:220
  32.4 6.3 %collective-permute-done.4.rest_2_ = bf16[8,8,2048]{2,1,0:T(8,128)(2,1)S(1)} collective-permute-done((bf16[8,8,2048]{2,1,0:T(8,128)(2,1)S(1)}, bf16[8,8,2048]{2,1,0:T(8,128)(2,1)S(1)}, u32[]{:S(2)}, u32[]{:S(2)}) %collective-permute-start.4) | collective-permute-done | bytes 262176 | tf_op jit(solution)/shard_map/ppermute | solution.py:220
  38.7 0.0 collective-permute-done.5.rest_3_
  38.7 1.5 %join.1 = bf16[1,1,4,8,8,2048]{5,4,3,2,1,0:T(8,128)(2,1)} custom-call(s32[2]{0:T(128)S(1)} %pad_add_fusion.info_ref, bf16[8,8,2048]{2,1,0:T(8,128)(2,1)S(1)} %get-tuple-element.15.rest_0_, bf16[8,8,2048]{2,1,0:T(8,128)(2,1)S(1)} %collective-permute-done.3.rest_1_, bf16[8,8,2048]{2,1,0:T(8,128)(2,1)S(1)} %collective-permute-done.4.rest_2_, ...), custom_call_target="tpu_custom_call" | custom-call | bytes 2097152 | tf_op jit(solution)/shard_map/join/pallas_call | solution.py:285
  40.3 0.0 collective-permute-done.7.r_ref
  40.3 1.3 %total.1 = (bf16[128,512]{1,0:T(8,128)(2,1)}, bf16[128,512]{1,0:T(8,128)(2,1)}) custom-call(s32[2]{0:T(128)S(1)} %pad_add_fusion.info_ref, f32[256,512]{1,0:T(8,128)S(1)} %get-tuple-element.21.d0_ref, bf16[256,512]{1,0:T(8,128)(2,1)S(1)} %collective-permute-done.6.b_ref, bf16[256,512]{1,0:T(8,128)(2,1)S(1)} %collective-permute-done.7.r_ref), custom_call_target="tpu_custom_call" | custom-call | bytes 2097152 | tf_op jit(solution)/shard_map/total/pallas_call | solution.py:276
Async XLA Ops:
  0.6 15.0 %copy-start = (bf16[1,128,2048]{2,1,0:T(8,128)(2,1)S(1)}, bf16[1,128,2048]{2,1,0:T(8,128)(2,1)}, u32[]{:S(2)}) copy-start(bf16[1,128,2048]{2,1,0:T(8,128)(2,1)} %param.6) | copy-start | bytes 1572868
  2.3 11.8 %collective-permute-start = (bf16[272,512]{1,0:T(8,128)(2,1)S(1)}, bf16[272,512]{1,0:T(8,128)(2,1)S(1)}, u32[]{:S(2)}, u32[]{:S(2)}) collective-permute-start(bf16[272,512]{1,0:T(8,128)(2,1)S(1)} %fusion.1.own_ref), channel_id=1, source_target_pairs={{0,2},{1,3},{2,4},{3,5},{4,6},{5,7},{6,0},{7,1},{8,10},{9,11},{10,... | collective-permute-start | bytes 835592 | tf_op jit(solution)/shard_map/ppermute | solution.py:211
  5.4 8.8 %collective-permute-start.1 = (bf16[272,512]{1,0:T(8,128)(2,1)S(1)}, bf16[272,512]{1,0:T(8,128)(2,1)S(1)}, u32[]{:S(2)}, u32[]{:S(2)}) collective-permute-start(bf16[272,512]{1,0:T(8,128)(2,1)S(1)} %fusion.1.own_ref), channel_id=1, source_target_pairs={{0,1},{1,0},{2,3},{3,2},{4,5},{5,4},{6,7},{7,6},{8,9},{9,8},{10,11... | collective-permute-start | bytes 835592 | tf_op jit(solution)/shard_map/ppermute | solution.py:206
  14.1 1.6 %collective-permute-start.2 = (bf16[272,512]{1,0:T(8,128)(2,1)S(1)}, bf16[272,512]{1,0:T(8,128)(2,1)S(1)}, u32[]{:S(2)}, u32[]{:S(2)}) collective-permute-start(bf16[272,512]{1,0:T(8,128)(2,1)S(1)} %collective-permute-done.r_ref), channel_id=1, source_target_pairs={{0,1},{1,0},{2,3},{3,2},{4,5},{5,4},{6,7},{7,6},{8,9},{9,8},{10,11... | collective-permute-start | bytes 835592 | tf_op jit(solution)/shard_map/ppermute | solution.py:206
  15.7 0.7 %copy-start.2 = (s32[1,16]{1,0:T(1,128)S(1)}, s32[1,16]{1,0:T(1,128)}, u32[]{:S(2)}) copy-start(s32[1,16]{1,0:T(1,128)} %param.11) | copy-start | bytes 196
  16.3 2.8 %copy-start.1 = (bf16[1,128,2048]{2,1,0:T(8,128)(2,1)S(1)}, bf16[1,128,2048]{2,1,0:T(8,128)(2,1)}, u32[]{:S(2)}) copy-start(bf16[1,128,2048]{2,1,0:T(8,128)(2,1)} %param.9) | copy-start | bytes 1572868
  23.2 3.6 %collective-permute-start.6 = (bf16[256,512]{1,0:T(8,128)(2,1)}, bf16[256,512]{1,0:T(8,128)(2,1)S(1)}, u32[]{:S(2)}, u32[]{:S(2)}) collective-permute-start(bf16[256,512]{1,0:T(8,128)(2,1)} %get-tuple-element.22), channel_id=1, source_target_pairs={{0,1},{1,0},{2,3},{3,2},{4,5},{5,4},{6,7},{7,6},{8,9},{9,8},{10,11... | collective-permute-start | bytes 786440 | tf_op jit(solution)/shard_map/ppermute | solution.py:206
  23.3 9.1 %collective-permute-start.3 = (bf16[8,8,2048]{2,1,0:T(8,128)(2,1)S(1)}, bf16[8,8,2048]{2,1,0:T(8,128)(2,1)S(1)}, u32[]{:S(2)}, u32[]{:S(2)}) collective-permute-start(bf16[8,8,2048]{2,1,0:T(8,128)(2,1)S(1)} %get-tuple-element.16), channel_id=1, source_target_pairs={{0,8},{8,0},{16,24},{24,16},{1,9},{9,1},{17,25},{25,17},{2,10},{10... | collective-permute-start | bytes 786440 | tf_op jit(solution)/shard_map/ppermute | solution.py:220
  24.8 13.9 %collective-permute-start.4 = (bf16[8,8,2048]{2,1,0:T(8,128)(2,1)S(1)}, bf16[8,8,2048]{2,1,0:T(8,128)(2,1)S(1)}, u32[]{:S(2)}, u32[]{:S(2)}) collective-permute-start(bf16[8,8,2048]{2,1,0:T(8,128)(2,1)S(1)} %get-tuple-element.17), channel_id=1, source_target_pairs={{0,16},{8,24},{16,0},{24,8},{1,17},{9,25},{17,1},{25,9},{2,18},{10... | collective-permute-start | bytes 786440 | tf_op jit(solution)/shard_map/ppermute | solution.py:220
  26.3 12.4 %collective-permute-start.5 = (bf16[8,8,2048]{2,1,0:T(8,128)(2,1)S(1)}, bf16[8,8,2048]{2,1,0:T(8,128)(2,1)S(1)}, u32[]{:S(2)}, u32[]{:S(2)}) collective-permute-start(bf16[8,8,2048]{2,1,0:T(8,128)(2,1)S(1)} %get-tuple-element.18), channel_id=1, source_target_pairs={{0,24},{8,16},{16,8},{24,0},{1,25},{9,17},{17,9},{25,1},{2,26},{10... | collective-permute-start | bytes 786440 | tf_op jit(solution)/shard_map/ppermute | solution.py:220
  26.9 13.4 %collective-permute-start.7 = (bf16[256,512]{1,0:T(8,128)(2,1)S(1)}, bf16[256,512]{1,0:T(8,128)(2,1)S(1)}, u32[]{:S(2)}, u32[]{:S(2)}) collective-permute-start(bf16[256,512]{1,0:T(8,128)(2,1)S(1)} %add_convert_fusion), channel_id=1, source_target_pairs={{0,6},{1,7},{2,0},{3,1},{4,2},{5,3},{6,4},{7,5},{8,14},{9,15},{10,... | collective-permute-start | bytes 786440 | tf_op jit(solution)/shard_map/ppermute | solution.py:211

commit v2 on v1

--- a/solution.py
+++ b/solution.py
@@ -52,21 +52,22 @@
     return key_pos <= lax.rem(query_pos, block)
 
 
-def repartner(index, k, count):
-    if count & (count - 1) == 0:
-        return index ^ k
-    return lax.rem(index + k, count)
-
-
-def fwd_kernel(n_dp, capacity, info_ref, home_ref, q_ref, own_ref, r_ref, b_ref, c_ref, *rest):
+def step_between(home, row, count):
+    return home ^ row if count & (count - 1) == 0 else lax.rem(home - row + count, count)
+
+
+def fwd_kernel(n_dp, home_hbm, q_ref, own_ref, r_ref, b_ref, c_ref, *rest):
     p_ref = rest[0]
     sends = rest[1 : 1 + n_dp]
-    packed, counts, sems = rest[1 + n_dp :]
+    held, counts, filled, home_ref, sem = rest[1 + n_dp :]
+    fetch = pltpu.make_async_copy(home_hbm, home_ref, sem)
+    fetch.start()
     block = q_ref.shape[0]
-    column, row = info_ref[0], info_ref[1]
-    pieces = home_ref.shape[0]
+    column, row = lax.axis_index("ctx"), lax.axis_index("dp")
+    pieces = home_ref.shape[1]
     piece_len = block // pieces
-    packed[...] = jnp.zeros_like(packed)
+    capacity = sends[0].shape[0]
+    held[pieces] = jnp.zeros(held.shape[1:], held.dtype)
     near = near_block(column, b_ref, c_ref)
 
     def seg_of(value):
@@ -91,15 +92,6 @@
     bias_n = jnp.concatenate([bias_n] * GROUP, axis=1)
     tri_g = triangle(block, GROUP)
     scaling = math.log2(math.e) / math.sqrt(HEAD_DIM)
-
-    for d in range(n_dp):
-        counts[d] = 0
-    place = []
-    for m in range(pieces):
-        home = home_ref[m]
-        slot = counts[home]
-        counts[home] = slot + 1
-        place.append(((home ^ row) if n_dp & (n_dp - 1) == 0 else lax.rem(home - row + n_dp, n_dp), slot))
 
     for g in range(own_ref.shape[1] // HEAD_DIM):
         keys, values = window(g, block, own_ref, r_ref, near)
@@ -121,20 +113,26 @@
         attended = dot(weights, jnp.concatenate(values, axis=0), TN)
         for h in range(GROUP):
             cols = slice((g * GROUP + h) * HEAD_DIM, (g * GROUP + h + 1) * HEAD_DIM)
-            tile = attended[h * block : (h + 1) * block].reshape(pieces, piece_len, HEAD_DIM)
-            for m in range(pieces):
-                packed[place[m][0], place[m][1], :, cols] = tile[m].astype(BF16)
-    copies = [pltpu.make_async_copy(packed.at[k], sends[k], sems.at[k]) for k in range(n_dp)]
-    for copy in copies:
-        copy.start()
-    for copy in copies:
-        copy.wait()
-
-
-def bwd_kernel(info_ref, q_ref, do_ref, own_ref, r_ref, b_ref, c_ref, p_ref, dq_ref, d0_ref, d1_ref, d2_ref):
+            tile = attended[h * block : (h + 1) * block].astype(BF16)
+            held[0:pieces, :, cols] = tile.reshape(pieces, piece_len, HEAD_DIM)
+    fetch.wait()
+    for d in range(n_dp):
+        counts[d] = 0
+        for slot in range(capacity):
+            filled[d * capacity + slot] = pieces
+    for m in range(pieces):
+        step = step_between(home_ref[0, m], row, n_dp)
+        slot = counts[step]
+        counts[step] = slot + 1
+        filled[step * capacity + slot] = m
+    for d in range(n_dp):
+        for slot in range(capacity):
+            sends[d][slot] = held[filled[d * capacity + slot]]
+
+
+def bwd_kernel(q_ref, do_ref, own_ref, r_ref, b_ref, c_ref, p_ref, dq_ref, d0_ref, d1_ref, d2_ref):
     block = q_ref.shape[0]
-    column = info_ref[0]
-    near = near_block(column, b_ref, c_ref)
+    near = near_block(lax.axis_index("ctx"), b_ref, c_ref)
     tri_g = triangle(block, GROUP)
     scaling = 1.0 / math.sqrt(HEAD_DIM)
     for g in range(own_ref.shape[1] // HEAD_DIM):
@@ -165,40 +163,61 @@
             dq_ref[:, heads] = dq[h * block : (h + 1) * block].astype(dq_ref.dtype)
 
 
-def final_kernel(n_ctx, info_ref, d0_ref, b_ref, r_ref, dk_ref, dv_ref):
-    block = dk_ref.shape[0]
-    column = info_ref[0]
-    total = d0_ref[...]
-    total = total + jnp.where(lax.rem(column, 2) == 0, b_ref[...].astype(F32), 0.0)
-    total = total + jnp.where(column + 2 < n_ctx, r_ref[...].astype(F32), 0.0)
-    dk_ref[...] = total[0:block].astype(dk_ref.dtype)
-    dv_ref[...] = total[block : 2 * block].astype(dv_ref.dtype)
-
-
-def join_kernel(n_dp, info_ref, *rest):
-    pieces, out_ref, sems = rest[:n_dp], rest[n_dp], rest[n_dp + 1]
-    row = info_ref[1]
+def prep_kernel(seg_hbm, k_hbm, v_hbm, own_ref, seg_ref, sems):
+    block = k_hbm.shape[0]
+    copies = [
+        pltpu.make_async_copy(seg_hbm, seg_ref, sems.at[0]),
+        pltpu.make_async_copy(k_hbm, own_ref.at[0:block], sems.at[1]),
+        pltpu.make_async_copy(v_hbm, own_ref.at[block : 2 * block], sems.at[2]),
+    ]
+    for copy in copies:
+        copy.start()
+    tail = slice(2 * block, 2 * block + SEG_ROWS)
+    own_ref[tail, block:] = jnp.zeros((SEG_ROWS, own_ref.shape[1] - block), BF16)
+    copies[0].wait()
+    ids = jnp.broadcast_to(seg_ref[...].astype(F32), (SEG_ROWS, block))
+    own_ref[tail, 0:block] = ids.astype(BF16)
+    for copy in copies[1:]:
+        copy.wait()
+
+
+def final_kernel(n_dp, n_ctx, *rest):
+    pieces = rest[:n_dp]
+    d1_ref, d2_ref, d0_ref, out_ref, dk_ref, dv_ref, total_ref, sems = rest[n_dp:]
+    row, column = lax.axis_index("dp"), lax.axis_index("ctx")
     copies = []
     for k in range(n_dp):
         source = row ^ k if n_dp & (n_dp - 1) == 0 else lax.rem(row - k + n_dp, n_dp)
         copies.append(pltpu.make_async_copy(pieces[k], out_ref.at[0, 0, source], sems.at[k]))
     for copy in copies:
         copy.start()
+    block = dk_ref.shape[0]
+    for part, target in ((0, dk_ref), (1, dv_ref)):
+        rows = slice(part * block, (part + 1) * block)
+        total = d0_ref[rows]
+        total = total + jnp.where(column + 1 < n_ctx, d1_ref[rows].astype(F32), 0.0)
+        total = total + jnp.where(column + 2 < n_ctx, d2_ref[rows].astype(F32), 0.0)
+        total_ref[rows] = total.astype(total_ref.dtype)
+        copies.append(pltpu.make_async_copy(total_ref.at[rows], target, sems.at[n_dp + part]))
+        copies[-1].start()
     for copy in copies:
         copy.wait()
 
 
 VMEM = pl.BlockSpec(memory_space=pltpu.VMEM)
-SMEM = pl.BlockSpec(memory_space=pltpu.SMEM)
 HBM = pl.BlockSpec(memory_space=pl.ANY)
 
 
-def params():
-    return pltpu.CompilerParams(vmem_limit_bytes=32 * 1024 * 1024)
+def params(kib=32 * 1024):
+    return pltpu.CompilerParams(vmem_limit_bytes=kib * 1024)
 
 
 def cost(flops, nbytes):
     return pl.CostEstimate(flops=flops, bytes_accessed=nbytes, transcendentals=0)
+
+
+def pinned(*arrays):
+    return [pltpu.with_memory_space_constraint(array, pltpu.HBM) for array in arrays]
 
 
 def swap(value):
@@ -226,34 +245,42 @@
     block, width = query.shape
     kv_width = key_rows.shape[2]
     heads = kv_width // HEAD_DIM
-    home = home_rows[0]
-    pieces = home.shape[0]
+    pieces = home_rows.shape[1]
     capacity = max(2, 2 * pieces // n_dp)
     piece_len = block // pieces
     column = lax.axis_index("ctx")
-    info = jnp.stack([column, lax.axis_index("dp")]).astype(jnp.int32)
-    seg = jnp.pad(segment_ids.astype(BF16), ((0, SEG_ROWS - 1), (0, kv_width - block)))
-    own = jnp.concatenate([key_rows[0], value_rows[0], seg], axis=0)
+    own = pl.pallas_call(
+        prep_kernel,
+        out_shape=jax.ShapeDtypeStruct((2 * block + SEG_ROWS, kv_width), BF16),
+        in_specs=[HBM] * 3,
+        out_specs=VMEM,
+        scratch_shapes=[pltpu.VMEM((1, block), jnp.int32), pltpu.SemaphoreType.DMA((3,))],
+        compiler_params=params(),
+        cost_estimate=cost(0, 1 << 19),
+        name="bundle",
+    )(*pinned(segment_ids, key_rows[0], value_rows[0]))
     far = ring(own, 2)
     beside = swap(own)
     crossed = swap(far)
 
     pairs = 2 * block * block * GROUP * heads * HEAD_DIM
     outs = pl.pallas_call(
-        functools.partial(fwd_kernel, n_dp, capacity),
+        functools.partial(fwd_kernel, n_dp),
         out_shape=[jax.ShapeDtypeStruct((heads, 2 * block, GROUP * block), BF16)]
         + [jax.ShapeDtypeStruct((capacity, piece_len, width), BF16)] * n_dp,
-        in_specs=[SMEM, SMEM] + [VMEM] * 5,
-        out_specs=[VMEM] + [HBM] * n_dp,
+        in_specs=[HBM] + [VMEM] * 5,
+        out_specs=[VMEM] * (1 + n_dp),
         scratch_shapes=[
-            pltpu.VMEM((n_dp, capacity, piece_len, width), BF16),
+            pltpu.VMEM((pieces + 1, piece_len, width), BF16),
             pltpu.SMEM((n_dp,), jnp.int32),
-            pltpu.SemaphoreType.DMA((n_dp,)),
+            pltpu.SMEM((n_dp * capacity,), jnp.int32),
+            pltpu.SMEM((1, pieces), jnp.int32),
+            pltpu.SemaphoreType.DMA,
         ],
         compiler_params=params(),
         cost_estimate=cost(6 * pairs, 4 << 20),
         name="attend",
-    )(info, home, query, own, far, beside, crossed)
+    )(home_rows, query, own, far, beside, crossed)
     weights, sends = outs[0], outs[1:]
     arrived = [sends[0]] + [exchange(sends[k], k) for k in range(1, n_dp)]
     dq, d0, d1, d2 = pl.pallas_call(
@@ -264,34 +291,27 @@
             jax.ShapeDtypeStruct((2 * block, kv_width), BF16),
             jax.ShapeDtypeStruct((2 * block, kv_width), BF16),
         ],
-        in_specs=[SMEM] + [VMEM] * 7,
+        in_specs=[VMEM] * 7,
         out_specs=[VMEM] * 4,
         compiler_params=params(),
         cost_estimate=cost(12 * pairs, 4 << 20),
         name="gradients",
-    )(info, query, grad, own, far, beside, crossed, weights)
-    d1_in = swap(d1)
-    d2_sum = (d2.astype(F32) + jnp.where(column % 2 == 1, d1_in.astype(F32), 0.0)).astype(BF16)
-    d2_in = ring(d2_sum, -2)
-    dk, dv = pl.pallas_call(
-        functools.partial(final_kernel, n_ctx),
-        out_shape=[jax.ShapeDtypeStruct((block, kv_width), BF16)] * 2,
-        in_specs=[SMEM] + [VMEM] * 3,
-        out_specs=[VMEM] * 2,
+    )(query, grad, own, far, beside, crossed, weights)
+    d1_in, d2_in = ring(d1, -1), ring(d2, -2)
+    routed, dk, dv = pl.pallas_call(
+        functools.partial(final_kernel, n_dp, n_ctx),
+        out_shape=[jax.ShapeDtypeStruct((1, 1, n_dp, capacity, piece_len, width), BF16)]
+        + [jax.ShapeDtypeStruct((block, kv_width), BF16)] * 2,
+        in_specs=[HBM] * n_dp + [VMEM] * 3,
+        out_specs=[HBM] * 3,
+        scratch_shapes=[
+            pltpu.VMEM((2 * block, kv_width), BF16),
+            pltpu.SemaphoreType.DMA((n_dp + 2,)),
+        ],
         compiler_params=params(),
-        cost_estimate=cost(0, 2 << 20),
-        name="total",
-    )(info, d0, d1_in, d2_in)
-    routed = pl.pallas_call(
-        functools.partial(join_kernel, n_dp),
-        out_shape=jax.ShapeDtypeStruct((1, 1, n_dp, capacity, piece_len, width), BF16),
-        in_specs=[SMEM] + [HBM] * n_dp,
-        out_specs=HBM,
-        scratch_shapes=[pltpu.SemaphoreType.DMA((n_dp,))],
-        compiler_params=params(),
-        cost_estimate=cost(0, 2 << 20),
-        name="join",
-    )(info, *arrived)
+        cost_estimate=cost(0, 4 << 20),
+        name="finish",
+    )(*arrived, d1_in, d2_in, d0)
     return routed, dq[None], dk[None], dv[None]
 
 

time: 41.8 us -> 36.5 us (0.87)
  other arithmetic: 1.86 us -> 0 us
  Pallas kernels: 9.68 us -> 7.95 us
  waiting for transfers between devices: 20.2 us -> 19.4 us
  local copies, waits for them, and re-layouts: 0.66 us -> 0.01 us
    ppermute x3, waiting for transfers between devices: 10 us -> 6.43 us  [exchange(): return lax.ppermute(value, 'dp', pairs)]
    ppermute x2 -> x3, waiting for transfers between devices: 8.68 us -> 11.4 us  [ring(): lax.ppermute(value, 'ctx', [(i, (i + steps) % count) for i in range(count)])]
    pallas_call x3, Pallas kernels: 5.62 us -> 4.44 us  [the longest x1 2.27 us: on_device(): pl.pallas_call(functools.partial(fwd_kernel, n_dp), out_shape=[jax.ShapeD...]
    concatenate x1 -> x0, other arithmetic: 0.99 us -> none  [on_device(): own = jnp.concatenate([key_rows[0], value_rows[0], seg], axis=0)]
    convert_element_type x2 -> x0, other arithmetic: 0.8 us -> none  [the longest x1 0.72 us: on_device(): segment_ids.astype(BF16)]
    unnamed x6, local copies, waits for them, and re-layouts: 0.66 us -> 0.01 us
    pallas_call x1, Pallas kernels: 4.06 us -> 3.51 us  [on_device(): pl.pallas_call(bwd_kernel, out_shape=[jax.ShapeDtypeStruct((block, width)...]
    ppermute x3 -> x2, waiting for transfers between devices: 1.48 us -> 1.56 us  [swap(): return lax.ppermute(value, 'ctx', [(i, i ^ 1) for i in range(count)])]
  transfers between devices with their start and end apart: 8 -> 8, of which waited for: 4 -> 5; matrix products, arithmetic and copies ran while one was open for 0% -> 0% of each run, Pallas kernels for 4% -> 10%
where the time goes in v2:
time: 36.5 us; the launch traced here: 36.4 us
  waiting for transfers between devices  19.4 us (53%)
  starting transfers between devices  8.38 us (23%)
  Pallas kernels  7.95 us (22%)
  between operations  0.67 us (2%)
    ppermute x3, waiting for transfers between devices, ring(): lax.ppermute(value, 'ctx', [(i, (i + steps) % count) for i in range(count)])  11.4 us
    ppermute x3, waiting for transfers between devices, exchange(): return lax.ppermute(value, 'dp', pairs)  6.43 us
    ppermute x3, starting transfers between devices, ring(): lax.ppermute(value, 'ctx', [(i, (i + steps) % count) for i in range(count)])  4.82 us
    ppermute x3, starting transfers between devices, exchange(): return lax.ppermute(value, 'dp', pairs)  3.55 us
    pallas_call x1, Pallas kernels, on_device(): pl.pallas_call(bwd_kernel, out_shape=[jax.ShapeDtypeStruct((block, width)...  3.51 us
    pallas_call x1, Pallas kernels, on_device(): pl.pallas_call(functools.partial(fwd_kernel, n_dp), out_shape=[jax.ShapeD...  2.27 us
    ppermute x2, waiting for transfers between devices, swap(): return lax.ppermute(value, 'ctx', [(i, i ^ 1) for i in range(count)])  1.56 us
    pallas_call x1, Pallas kernels, on_device(): pl.pallas_call(functools.partial(final_kernel, n_dp, n_ctx), out_shape=[j...  1.1 us
  transfers between devices with their start and end apart: 8, of which 5 were waited for; matrix products, arithmetic and copies ran while one was open for 0% of the time, Pallas kernels for 10%

profile of v2, /device:TPU:0, one launch (start us, length us, event | category | flops | bytes accessed | tf_op | source)
XLA Modules:
  0.0 36.4 jit_solution(5311267768613012072)
XLA Ops:
  0.6 0.0 copy-start
  0.6 1.1 %bundle.1.own_ref = bf16[272,512]{1,0:T(8,128)(2,1)S(1)} custom-call(s32[1,128]{1,0:T(1,128)} %seg_hbm.1, bf16[128,512]{1,0:T(8,128)(2,1)} %bitcast.10, bf16[128,512]{1,0:T(8,128)(2,1)} %bitcast.11), custom_call_target="tpu_custom_call" | custom-call | bytes 524288 | tf_op jit(solution)/shard_map/bundle/pallas_call | solution.py:252
  1.7 0.0 copy-start.2
  1.7 3.1 %collective-permute-start = (bf16[272,512]{1,0:T(8,128)(2,1)S(1)}, bf16[272,512]{1,0:T(8,128)(2,1)S(1)}, u32[]{:S(2)}, u32[]{:S(2)}) collective-permute-start(bf16[272,512]{1,0:T(8,128)(2,1)S(1)} %bundle.1.own_ref), channel_id=1, source_target_pairs={{0,2},{1,3},{2,4},{3,5},{4,6},{5,7},{6,0},{7,1},{8,10},{9,11},{10,... | collective-permute-start | bytes 835592 | tf_op jit(solution)/shard_map/ppermute | solution.py:230
  4.8 0.0 collective-permute-start.1
  4.8 8.7 %collective-permute-done.r_ref = bf16[272,512]{1,0:T(8,128)(2,1)S(1)} collective-permute-done((bf16[272,512]{1,0:T(8,128)(2,1)S(1)}, bf16[272,512]{1,0:T(8,128)(2,1)S(1)}, u32[]{:S(2)}, u32[]{:S(2)}) %collective-permute-start) | collective-permute-done | bytes 278560 | tf_op jit(solution)/shard_map/ppermute | solution.py:230
  13.5 0.0 collective-permute-start.2
  13.5 0.0 collective-permute-done.1.b_ref
  13.5 1.6 %collective-permute-done.2.c_ref = bf16[272,512]{1,0:T(8,128)(2,1)S(1)} collective-permute-done((bf16[272,512]{1,0:T(8,128)(2,1)S(1)}, bf16[272,512]{1,0:T(8,128)(2,1)S(1)}, u32[]{:S(2)}, u32[]{:S(2)}) %collective-permute-start.2) | collective-permute-done | bytes 278560 | tf_op jit(solution)/shard_map/ppermute | solution.py:225
  15.0 0.0 copy-done
  15.0 0.0 copy-done.2
  15.1 0.0 copy-start.1
  15.1 2.3 %attend.1 = (bf16[4,256,512]{2,1,0:T(8,128)(2,1)S(1)}, bf16[8,8,2048]{2,1,0:T(8,128)(2,1)S(1)}, bf16[8,8,2048]{2,1,0:T(8,128)(2,1)S(1)}, bf16[8,8,2048]{2,1,0:T(8,128)(2,1)S(1)}, bf16[8,8,2048]{2,1,0:T(8,128)(2,1)S(1)}) custom-call(s32[1,16]{1,0:T(1,128)S(1)} %copy-done.2, bf16[128,2048]{1,0:T(8,128)(2,1)S(1)} %bitcast.7, ...), custom_call_target="tpu_custom_call" | custom-call | flops 402653184 | bytes 4194304 | tf_op jit(solution)/shard_map/attend/pallas_call | solution.py:267
  17.3 1.6 %collective-permute-start.3 = (bf16[8,8,2048]{2,1,0:T(8,128)(2,1)S(1)}, bf16[8,8,2048]{2,1,0:T(8,128)(2,1)S(1)}, u32[]{:S(2)}, u32[]{:S(2)}) collective-permute-start(bf16[8,8,2048]{2,1,0:T(8,128)(2,1)S(1)} %get-tuple-element.17), channel_id=1, source_target_pairs={{0,8},{8,0},{16,24},{24,16},{1,9},{9,1},{17,25},{25,17},{2,10},{10... | collective-permute-start | bytes 786440 | tf_op jit(solution)/shard_map/ppermute | solution.py:239
  18.9 1.5 %collective-permute-start.4 = (bf16[8,8,2048]{2,1,0:T(8,128)(2,1)S(1)}, bf16[8,8,2048]{2,1,0:T(8,128)(2,1)S(1)}, u32[]{:S(2)}, u32[]{:S(2)}) collective-permute-start(bf16[8,8,2048]{2,1,0:T(8,128)(2,1)S(1)} %get-tuple-element.18), channel_id=1, source_target_pairs={{0,16},{8,24},{16,0},{24,8},{1,17},{9,25},{17,1},{25,9},{2,18},{10... | collective-permute-start | bytes 786440 | tf_op jit(solution)/shard_map/ppermute | solution.py:239
  20.4 0.5 %collective-permute-start.5 = (bf16[8,8,2048]{2,1,0:T(8,128)(2,1)S(1)}, bf16[8,8,2048]{2,1,0:T(8,128)(2,1)S(1)}, u32[]{:S(2)}, u32[]{:S(2)}) collective-permute-start(bf16[8,8,2048]{2,1,0:T(8,128)(2,1)S(1)} %get-tuple-element.19), channel_id=1, source_target_pairs={{0,24},{8,16},{16,8},{24,0},{1,25},{9,17},{17,9},{25,1},{2,26},{10... | collective-permute-start | bytes 786440 | tf_op jit(solution)/shard_map/ppermute | solution.py:239
  20.9 0.0 copy-done.1
  20.9 3.5 %gradients.1 = (bf16[128,2048]{1,0:T(8,128)(2,1)}, f32[256,512]{1,0:T(8,128)S(1)}, bf16[256,512]{1,0:T(8,128)(2,1)S(1)}, bf16[256,512]{1,0:T(8,128)(2,1)S(1)}) custom-call(bf16[128,2048]{1,0:T(8,128)(2,1)S(1)} %bitcast.8, bf16[128,2048]{1,0:T(8,128)(2,1)S(1)} %bitcast.9, bf16[272,512]{1,0:T(8,128)(2,1)S(1)} %bundle.1.own_ref, ...), custom_call_target="tpu_custom_call" | custom-call | flops 805306368 | bytes 4194304 | tf_op jit(solution)/shard_map/gradients/pallas_call | solution.py:286
  24.4 0.7 %collective-permute-start.6 = (bf16[256,512]{1,0:T(8,128)(2,1)S(1)}, bf16[256,512]{1,0:T(8,128)(2,1)S(1)}, u32[]{:S(2)}, u32[]{:S(2)}) collective-permute-start(bf16[256,512]{1,0:T(8,128)(2,1)S(1)} %get-tuple-element.21), channel_id=1, source_target_pairs={{0,7},{1,0},{2,1},{3,2},{4,3},{5,4},{6,5},{7,6},{8,15},{9,8},{10,9... | collective-permute-start | bytes 786440 | tf_op jit(solution)/shard_map/ppermute | solution.py:230
  25.1 1.1 %collective-permute-start.7 = (bf16[256,512]{1,0:T(8,128)(2,1)S(1)}, bf16[256,512]{1,0:T(8,128)(2,1)S(1)}, u32[]{:S(2)}, u32[]{:S(2)}) collective-permute-start(bf16[256,512]{1,0:T(8,128)(2,1)S(1)} %get-tuple-element.22), channel_id=1, source_target_pairs={{0,6},{1,7},{2,0},{3,1},{4,2},{5,3},{6,4},{7,5},{8,14},{9,15},{10,... | collective-permute-start | bytes 786440 | tf_op jit(solution)/shard_map/ppermute | solution.py:230
  26.1 0.4 %collective-permute-done.3.rest_1_ = bf16[8,8,2048]{2,1,0:T(8,128)(2,1)S(1)} collective-permute-done((bf16[8,8,2048]{2,1,0:T(8,128)(2,1)S(1)}, bf16[8,8,2048]{2,1,0:T(8,128)(2,1)S(1)}, u32[]{:S(2)}, u32[]{:S(2)}) %collective-permute-start.3) | collective-permute-done | bytes 262176 | tf_op jit(solution)/shard_map/ppermute | solution.py:239
  26.5 6.0 %collective-permute-done.4.rest_2_ = bf16[8,8,2048]{2,1,0:T(8,128)(2,1)S(1)} collective-permute-done((bf16[8,8,2048]{2,1,0:T(8,128)(2,1)S(1)}, bf16[8,8,2048]{2,1,0:T(8,128)(2,1)S(1)}, u32[]{:S(2)}, u32[]{:S(2)}) %collective-permute-start.4) | collective-permute-done | bytes 262176 | tf_op jit(solution)/shard_map/ppermute | solution.py:239
  32.6 0.0 collective-permute-done.5.rest_3_
  32.6 0.0 collective-permute-done.6.rest_4_
  32.6 2.7 %collective-permute-done.7.rest_5_ = bf16[256,512]{1,0:T(8,128)(2,1)S(1)} collective-permute-done((bf16[256,512]{1,0:T(8,128)(2,1)S(1)}, bf16[256,512]{1,0:T(8,128)(2,1)S(1)}, u32[]{:S(2)}, u32[]{:S(2)}) %collective-permute-start.7) | collective-permute-done | bytes 262176 | tf_op jit(solution)/shard_map/ppermute | solution.py:230
  35.3 1.1 %finish.1 = (bf16[1,1,4,8,8,2048]{5,4,3,2,1,0:T(8,128)(2,1)}, bf16[128,512]{1,0:T(8,128)(2,1)}, bf16[128,512]{1,0:T(8,128)(2,1)}) custom-call(bf16[8,8,2048]{2,1,0:T(8,128)(2,1)S(1)} %get-tuple-element.16.rest_0_, bf16[8,8,2048]{2,1,0:T(8,128)(2,1)S(1)} %collective-permute-done.3.rest_1_, bf16[8,8,2048]{2,1,0:T(8,128)(2,1)S(1)} %collective-permute-done.4.rest_2_, ...), custom_call_target="tpu_custom_call" | custom-call | bytes 4194304 | tf_op jit(solution)/shard_map/finish/pallas_call | solution.py:301
Async XLA Ops:
  0.6 14.4 %copy-start = (bf16[1,128,2048]{2,1,0:T(8,128)(2,1)S(1)}, bf16[1,128,2048]{2,1,0:T(8,128)(2,1)}, u32[]{:S(2)}) copy-start(bf16[1,128,2048]{2,1,0:T(8,128)(2,1)} %param.6) | copy-start | bytes 1572868
  1.7 13.3 %copy-start.2 = (s32[1,16]{1,0:T(1,128)S(1)}, s32[1,16]{1,0:T(1,128)}, u32[]{:S(2)}) copy-start(s32[1,16]{1,0:T(1,128)} %home_hbm.1) | copy-start | bytes 196
  1.7 11.8 %collective-permute-start = (bf16[272,512]{1,0:T(8,128)(2,1)S(1)}, bf16[272,512]{1,0:T(8,128)(2,1)S(1)}, u32[]{:S(2)}, u32[]{:S(2)}) collective-permute-start(bf16[272,512]{1,0:T(8,128)(2,1)S(1)} %bundle.1.own_ref), channel_id=1, source_target_pairs={{0,2},{1,3},{2,4},{3,5},{4,6},{5,7},{6,0},{7,1},{8,10},{9,11},{10,... | collective-permute-start | bytes 835592 | tf_op jit(solution)/shard_map/ppermute | solution.py:230
  4.8 8.7 %collective-permute-start.1 = (bf16[272,512]{1,0:T(8,128)(2,1)S(1)}, bf16[272,512]{1,0:T(8,128)(2,1)S(1)}, u32[]{:S(2)}, u32[]{:S(2)}) collective-permute-start(bf16[272,512]{1,0:T(8,128)(2,1)S(1)} %bundle.1.own_ref), channel_id=1, source_target_pairs={{0,1},{1,0},{2,3},{3,2},{4,5},{5,4},{6,7},{7,6},{8,9},{9,8},{10,11... | collective-permute-start | bytes 835592 | tf_op jit(solution)/shard_map/ppermute | solution.py:225
  13.5 1.6 %collective-permute-start.2 = (bf16[272,512]{1,0:T(8,128)(2,1)S(1)}, bf16[272,512]{1,0:T(8,128)(2,1)S(1)}, u32[]{:S(2)}, u32[]{:S(2)}) collective-permute-start(bf16[272,512]{1,0:T(8,128)(2,1)S(1)} %collective-permute-done.r_ref), channel_id=1, source_target_pairs={{0,1},{1,0},{2,3},{3,2},{4,5},{5,4},{6,7},{7,6},{8,9},{9,8},{10,11... | collective-permute-start | bytes 835592 | tf_op jit(solution)/shard_map/ppermute | solution.py:225
  15.1 5.8 %copy-start.1 = (bf16[1,128,2048]{2,1,0:T(8,128)(2,1)S(1)}, bf16[1,128,2048]{2,1,0:T(8,128)(2,1)}, u32[]{:S(2)}) copy-start(bf16[1,128,2048]{2,1,0:T(8,128)(2,1)} %param.9) | copy-start | bytes 1572868
  17.3 9.2 %collective-permute-start.3 = (bf16[8,8,2048]{2,1,0:T(8,128)(2,1)S(1)}, bf16[8,8,2048]{2,1,0:T(8,128)(2,1)S(1)}, u32[]{:S(2)}, u32[]{:S(2)}) collective-permute-start(bf16[8,8,2048]{2,1,0:T(8,128)(2,1)S(1)} %get-tuple-element.17), channel_id=1, source_target_pairs={{0,8},{8,0},{16,24},{24,16},{1,9},{9,1},{17,25},{25,17},{2,10},{10... | collective-permute-start | bytes 786440 | tf_op jit(solution)/shard_map/ppermute | solution.py:239
  18.9 13.7 %collective-permute-start.4 = (bf16[8,8,2048]{2,1,0:T(8,128)(2,1)S(1)}, bf16[8,8,2048]{2,1,0:T(8,128)(2,1)S(1)}, u32[]{:S(2)}, u32[]{:S(2)}) collective-permute-start(bf16[8,8,2048]{2,1,0:T(8,128)(2,1)S(1)} %get-tuple-element.18), channel_id=1, source_target_pairs={{0,16},{8,24},{16,0},{24,8},{1,17},{9,25},{17,1},{25,9},{2,18},{10... | collective-permute-start | bytes 786440 | tf_op jit(solution)/shard_map/ppermute | solution.py:239
  20.4 12.2 %collective-permute-start.5 = (bf16[8,8,2048]{2,1,0:T(8,128)(2,1)S(1)}, bf16[8,8,2048]{2,1,0:T(8,128)(2,1)S(1)}, u32[]{:S(2)}, u32[]{:S(2)}) collective-permute-start(bf16[8,8,2048]{2,1,0:T(8,128)(2,1)S(1)} %get-tuple-element.19), channel_id=1, source_target_pairs={{0,24},{8,16},{16,8},{24,0},{1,25},{9,17},{17,9},{25,1},{2,26},{10... | collective-permute-start | bytes 786440 | tf_op jit(solution)/shard_map/ppermute | solution.py:239
  24.4 8.2 %collective-permute-start.6 = (bf16[256,512]{1,0:T(8,128)(2,1)S(1)}, bf16[256,512]{1,0:T(8,128)(2,1)S(1)}, u32[]{:S(2)}, u32[]{:S(2)}) collective-permute-start(bf16[256,512]{1,0:T(8,128)(2,1)S(1)} %get-tuple-element.21), channel_id=1, source_target_pairs={{0,7},{1,0},{2,1},{3,2},{4,3},{5,4},{6,5},{7,6},{8,15},{9,8},{10,9... | collective-permute-start | bytes 786440 | tf_op jit(solution)/shard_map/ppermute | solution.py:230
  25.1 10.2 %collective-permute-start.7 = (bf16[256,512]{1,0:T(8,128)(2,1)S(1)}, bf16[256,512]{1,0:T(8,128)(2,1)S(1)}, u32[]{:S(2)}, u32[]{:S(2)}) collective-permute-start(bf16[256,512]{1,0:T(8,128)(2,1)S(1)} %get-tuple-element.22), channel_id=1, source_target_pairs={{0,6},{1,7},{2,0},{3,1},{4,2},{5,3},{6,4},{7,5},{8,14},{9,15},{10,... | collective-permute-start | bytes 786440 | tf_op jit(solution)/shard_map/ppermute | solution.py:230

commit v3 on v2

--- a/solution.py
+++ b/solution.py
@@ -31,13 +31,13 @@
     return jnp.concatenate(heads, axis=0)
 
 
-def window(g, block, own_ref, r_ref, near):
+def window(g, block, own_ref, far, near):
     cols = slice(g * HEAD_DIM, (g + 1) * HEAD_DIM)
-    keys = (own_ref[0:block, cols], near[0:block, cols], r_ref[0:block, cols])
+    keys = (own_ref[0:block, cols], near[0:block, cols], far[0:block, cols])
     values = (
         own_ref[block : 2 * block, cols],
         near[block : 2 * block, cols],
-        r_ref[block : 2 * block, cols],
+        far[block : 2 * block, cols],
     )
     return keys, values
 
@@ -130,13 +130,19 @@
             sends[d][slot] = held[filled[d * capacity + slot]]
 
 
-def bwd_kernel(q_ref, do_ref, own_ref, r_ref, b_ref, c_ref, p_ref, dq_ref, d0_ref, d1_ref, d2_ref):
+def split(tri, packed):
+    own = jnp.where(tri, packed, 0.0).astype(BF16)
+    far = jnp.where(tri, 0.0, packed).astype(BF16)
+    return own, far
+
+
+def sent_kernel(q_ref, do_ref, own_ref, r_ref, b_ref, c_ref, p_ref, gs_ref, d2_ref, dk1_ref, dv1_ref):
     block = q_ref.shape[0]
     near = near_block(lax.axis_index("ctx"), b_ref, c_ref)
     tri_g = triangle(block, GROUP)
     scaling = 1.0 / math.sqrt(HEAD_DIM)
     for g in range(own_ref.shape[1] // HEAD_DIM):
-        keys, values = window(g, block, own_ref, r_ref, near)
+        _, values = window(g, block, own_ref, r_ref, near)
         queries, grads = stacked(q_ref, g), stacked(do_ref, g)
         w_x = p_ref[g, 0:block].astype(F32)
         w_n = p_ref[g, block : 2 * block]
@@ -146,15 +152,29 @@
         delta = jnp.sum(w_x * gw_x + w_nf * gw_n, axis=0, keepdims=True)
         gs_x = w_x * (gw_x - delta) * scaling
         gs_n = (w_nf * (gw_n - delta) * scaling).astype(BF16)
-        gs_0 = jnp.where(tri_g, gs_x, 0.0).astype(BF16)
-        gs_2 = jnp.where(tri_g, 0.0, gs_x).astype(BF16)
-        w_0 = jnp.where(tri_g, w_x, 0.0).astype(BF16)
-        w_2 = jnp.where(tri_g, 0.0, w_x).astype(BF16)
+        gs_ref[g, 0:block] = gs_x.astype(BF16)
+        gs_ref[g, block : 2 * block] = gs_n
+        _, gs_2 = split(tri_g, gs_x)
+        _, w_2 = split(tri_g, w_x)
         cols = slice(g * HEAD_DIM, (g + 1) * HEAD_DIM)
+        dk1_ref[:, cols] = dot(gs_n, queries, NN).astype(dk1_ref.dtype)
+        dv1_ref[:, cols] = dot(w_n, grads, NN).astype(dv1_ref.dtype)
         d2_ref[0:block, cols] = dot(gs_2, queries, NN).astype(d2_ref.dtype)
         d2_ref[block : 2 * block, cols] = dot(w_2, grads, NN).astype(d2_ref.dtype)
-        d1_ref[0:block, cols] = dot(gs_n, queries, NN).astype(d1_ref.dtype)
-        d1_ref[block : 2 * block, cols] = dot(w_n, grads, NN).astype(d1_ref.dtype)
+
+
+def kept_kernel(q_ref, do_ref, own_ref, r_ref, b_ref, c_ref, p_ref, gs_ref, dq_ref, d0_ref, mark_ref):
+    mark_ref[...] = jnp.zeros_like(mark_ref)
+    block = q_ref.shape[0]
+    near = near_block(lax.axis_index("ctx"), b_ref, c_ref)
+    tri_g = triangle(block, GROUP)
+    for g in range(own_ref.shape[1] // HEAD_DIM):
+        keys, _ = window(g, block, own_ref, r_ref, near)
+        queries, grads = stacked(q_ref, g), stacked(do_ref, g)
+        gs_0, gs_2 = split(tri_g, gs_ref[g, 0:block].astype(F32))
+        w_0, _ = split(tri_g, p_ref[g, 0:block].astype(F32))
+        gs_n = gs_ref[g, block : 2 * block]
+        cols = slice(g * HEAD_DIM, (g + 1) * HEAD_DIM)
         d0_ref[0:block, cols] = dot(gs_0, queries, NN)
         d0_ref[block : 2 * block, cols] = dot(w_0, grads, NN)
         dq = dot(jnp.concatenate([gs_0, gs_n, gs_2], axis=0), jnp.concatenate(keys, axis=0), TN)
@@ -181,24 +201,41 @@
         copy.wait()
 
 
-def final_kernel(n_dp, n_ctx, *rest):
-    pieces = rest[:n_dp]
-    d1_ref, d2_ref, d0_ref, out_ref, dk_ref, dv_ref, total_ref, sems = rest[n_dp:]
-    row, column = lax.axis_index("dp"), lax.axis_index("ctx")
+def merge_kernel(d2_ref, dk1_ref, dv1_ref, out_ref):
+    block = dk1_ref.shape[0]
+    odd = lax.rem(lax.axis_index("ctx"), 2) == 1
+    for part, d1_ref in enumerate((dk1_ref, dv1_ref)):
+        rows = slice(part * block, (part + 1) * block)
+        other = jnp.where(odd, d1_ref[...].astype(F32), 0.0)
+        out_ref[rows] = (d2_ref[rows].astype(F32) + other).astype(out_ref.dtype)
+
+
+def join_kernel(n_dp, *rest):
+    pieces, (_, out_ref, mark_ref, sems) = rest[:n_dp], rest[n_dp:]
+    row = lax.axis_index("dp")
     copies = []
     for k in range(n_dp):
         source = row ^ k if n_dp & (n_dp - 1) == 0 else lax.rem(row - k + n_dp, n_dp)
-        copies.append(pltpu.make_async_copy(pieces[k], out_ref.at[0, 0, source], sems.at[k]))
+        copies.append(pltpu.make_async_copy(pieces[n_dp - 1 - k], out_ref.at[0, 0, source], sems.at[k]))
     for copy in copies:
         copy.start()
+    mark_ref[...] = jnp.zeros_like(mark_ref)
+    for copy in copies:
+        copy.wait()
+
+
+def total_kernel(n_ctx, d0_ref, dk1_ref, dv1_ref, uneven_ref, even_ref, _, dk_ref, dv_ref, total_ref, sems):
+    column = lax.axis_index("ctx")
     block = dk_ref.shape[0]
-    for part, target in ((0, dk_ref), (1, dv_ref)):
+    copies = []
+    for part, (d1_ref, target) in enumerate(((dk1_ref, dk_ref), (dv1_ref, dv_ref))):
         rows = slice(part * block, (part + 1) * block)
         total = d0_ref[rows]
-        total = total + jnp.where(column + 1 < n_ctx, d1_ref[rows].astype(F32), 0.0)
-        total = total + jnp.where(column + 2 < n_ctx, d2_ref[rows].astype(F32), 0.0)
+        total = total + jnp.where(lax.rem(column, 2) == 0, d1_ref[...].astype(F32), 0.0)
+        d2 = jnp.where(lax.rem(column // 2, 2) == 0, even_ref[rows], uneven_ref[rows])
+        total = total + jnp.where(column + 2 < n_ctx, d2.astype(F32), 0.0)
         total_ref[rows] = total.astype(total_ref.dtype)
-        copies.append(pltpu.make_async_copy(total_ref.at[rows], target, sems.at[n_dp + part]))
+        copies.append(pltpu.make_async_copy(total_ref.at[rows], target, sems.at[part]))
         copies[-1].start()
     for copy in copies:
         copy.wait()
@@ -225,9 +262,18 @@
     return lax.ppermute(value, "ctx", [(i, i ^ 1) for i in range(count)])
 
 
-def ring(value, steps):
+def from_chip(value):
     count = lax.axis_size("ctx")
-    return lax.ppermute(value, "ctx", [(i, (i + steps) % count) for i in range(count)])
+
+    def pairs(first):
+        found = []
+        for i in range(count):
+            chip = i // 2
+            other = chip + 1 if (chip - first) % 2 == 0 else chip - 1
+            found.append((i, 2 * other + i % 2 if 0 <= other < count // 2 else i ^ 1))
+        return found
+
+    return lax.ppermute(value, "ctx", pairs(0)), lax.ppermute(value, "ctx", pairs(1))
 
 
 def exchange(value, k):
@@ -259,7 +305,8 @@
         cost_estimate=cost(0, 1 << 19),
         name="bundle",
     )(*pinned(segment_ids, key_rows[0], value_rows[0]))
-    far = ring(own, 2)
+    even, uneven = from_chip(own)
+    far = jnp.where(lax.rem(column // 2, 2) == 0, uneven, even)
     beside = swap(own)
     crossed = swap(far)
 
@@ -282,36 +329,66 @@
         name="attend",
     )(home_rows, query, own, far, beside, crossed)
     weights, sends = outs[0], outs[1:]
-    arrived = [sends[0]] + [exchange(sends[k], k) for k in range(1, n_dp)]
-    dq, d0, d1, d2 = pl.pallas_call(
-        bwd_kernel,
+    arrived = [exchange(sends[k], k) for k in range(n_dp - 1, 0, -1)] + [sends[0]]
+    terms = jax.ShapeDtypeStruct((2 * block, kv_width), BF16)
+    half = jax.ShapeDtypeStruct((block, kv_width), BF16)
+    mark = jax.ShapeDtypeStruct((8, HEAD_DIM), F32)
+    score_grads, d2, dk1, dv1 = pl.pallas_call(
+        sent_kernel,
+        out_shape=[jax.ShapeDtypeStruct(weights.shape, BF16), terms, half, half],
+        in_specs=[VMEM] * 7,
+        out_specs=[VMEM] * 4,
+        compiler_params=params(),
+        cost_estimate=cost(7 * pairs, 4 << 20),
+        name="sent_terms",
+    )(query, grad, own, far, beside, crossed, weights)
+    dq, d0, after_kept = pl.pallas_call(
+        kept_kernel,
         out_shape=[
             jax.ShapeDtypeStruct((block, width), BF16),
             jax.ShapeDtypeStruct((2 * block, kv_width), F32),
-            jax.ShapeDtypeStruct((2 * block, kv_width), BF16),
-            jax.ShapeDtypeStruct((2 * block, kv_width), BF16),
+            mark,
         ],
-        in_specs=[VMEM] * 7,
-        out_specs=[VMEM] * 4,
-        compiler_params=params(),
-        cost_estimate=cost(12 * pairs, 4 << 20),
-        name="gradients",
-    )(query, grad, own, far, beside, crossed, weights)
-    d1_in, d2_in = ring(d1, -1), ring(d2, -2)
-    routed, dk, dv = pl.pallas_call(
-        functools.partial(final_kernel, n_dp, n_ctx),
-        out_shape=[jax.ShapeDtypeStruct((1, 1, n_dp, capacity, piece_len, width), BF16)]
-        + [jax.ShapeDtypeStruct((block, kv_width), BF16)] * 2,
-        in_specs=[HBM] * n_dp + [VMEM] * 3,
-        out_specs=[HBM] * 3,
+        in_specs=[VMEM] * 8,
+        out_specs=[VMEM] * 3,
+        compiler_params=params(),
+        cost_estimate=cost(1073741824, 0),
+        name="kept_terms",
+    )(query, grad, own, far, beside, crossed, weights, score_grads)
+    dk1_in, dv1_in = swap(dk1), swap(dv1)
+    d2_sum = pl.pallas_call(
+        merge_kernel,
+        out_shape=terms,
+        in_specs=[VMEM] * 3,
+        out_specs=VMEM,
+        compiler_params=params(),
+        cost_estimate=cost(0, 0),
+        name="merge",
+    )(d2, dk1_in, dv1_in)
+    d2_even, d2_uneven = from_chip(d2_sum)
+    routed, after_join = pl.pallas_call(
+        functools.partial(join_kernel, n_dp),
+        out_shape=[jax.ShapeDtypeStruct((1, 1, n_dp, capacity, piece_len, width), BF16), mark],
+        in_specs=[HBM] * (n_dp + 1),
+        out_specs=[HBM, VMEM],
+        scratch_shapes=[pltpu.SemaphoreType.DMA((n_dp,))],
+        compiler_params=params(),
+        cost_estimate=cost(2147483648, 0),
+        name="join",
+    )(*arrived, after_kept)
+    dk, dv = pl.pallas_call(
+        functools.partial(total_kernel, n_ctx),
+        out_shape=[jax.ShapeDtypeStruct((block, kv_width), BF16)] * 2,
+        in_specs=[VMEM] * 5 + [HBM],
+        out_specs=[HBM] * 2,
         scratch_shapes=[
             pltpu.VMEM((2 * block, kv_width), BF16),
-            pltpu.SemaphoreType.DMA((n_dp + 2,)),
+            pltpu.SemaphoreType.DMA((2,)),
         ],
         compiler_params=params(),
-        cost_estimate=cost(0, 4 << 20),
-        name="finish",
-    )(*arrived, d1_in, d2_in, d0)
+        cost_estimate=cost(0, 1 << 20),
+        name="total",
+    )(d0, dk1_in, dv1_in, d2_uneven, d2_even, after_join)
     return routed, dq[None], dk[None], dv[None]
 
 

time: 36.5 us -> 33.5 us (0.918)
  waiting for transfers between devices: 19.4 us -> 12.7 us
  starting transfers between devices: 8.38 us -> 10.8 us
  Pallas kernels: 7.95 us -> 9.08 us
    ppermute x3 -> x4, waiting for transfers between devices: 11.4 us -> 7.14 us  [the longest x2 7.13 us: from_chip(): lax.ppermute(value, 'ctx', pairs(0))]
    ppermute x3, waiting for transfers between devices: 6.43 us -> 3.04 us  [exchange(): return lax.ppermute(value, 'dp', pairs)]
    ppermute x3 -> x4, starting transfers between devices: 4.82 us -> 6.07 us  [the longest x2 6.02 us: from_chip(): lax.ppermute(value, 'ctx', pairs(0))]
    pallas_call x2 -> x5, Pallas kernels: 4.62 us -> 5.8 us  [the longest x1 2.2 us: on_device(): pl.pallas_call(sent_kernel, out_shape=[jax.ShapeDtypeStruct(weights.shape...]
    ppermute x2 -> x4, starting transfers between devices: 0.01 us -> 1.15 us  [swap(): return lax.ppermute(value, 'ctx', [(i, i ^ 1) for i in range(count)])]
    ppermute x2 -> x4, waiting for transfers between devices: 1.56 us -> 2.56 us  [swap(): return lax.ppermute(value, 'ctx', [(i, i ^ 1) for i in range(count)])]
  transfers between devices with their start and end apart: 8 -> 11, of which waited for: 5 -> 7; matrix products, arithmetic and copies ran while one was open for 0% -> 0% of each run, Pallas kernels for 10% -> 15%
where the time goes in v3:
time: 33.5 us; the launch traced here: 33.4 us
  waiting for transfers between devices  12.7 us (38%)
  starting transfers between devices  10.8 us (32%)
  Pallas kernels  9.08 us (27%)
  between operations  0.72 us (2%)
    ppermute x2, waiting for transfers between devices, from_chip(): lax.ppermute(value, 'ctx', pairs(0))  7.13 us
    ppermute x2, starting transfers between devices, from_chip(): lax.ppermute(value, 'ctx', pairs(0))  6.02 us
    ppermute x3, starting transfers between devices, exchange(): return lax.ppermute(value, 'dp', pairs)  3.55 us
    ppermute x3, waiting for transfers between devices, exchange(): return lax.ppermute(value, 'dp', pairs)  3.04 us
    ppermute x4, waiting for transfers between devices, swap(): return lax.ppermute(value, 'ctx', [(i, i ^ 1) for i in range(count)])  2.56 us
    pallas_call x1, Pallas kernels, on_device(): pl.pallas_call(functools.partial(fwd_kernel, n_dp), out_shape=[jax.ShapeD...  2.27 us
    pallas_call x1, Pallas kernels, on_device(): pl.pallas_call(sent_kernel, out_shape=[jax.ShapeDtypeStruct(weights.shape...  2.2 us
    pallas_call x1, Pallas kernels, on_device(): pl.pallas_call(kept_kernel, out_shape=[jax.ShapeDtypeStruct((block, width...  1.72 us
  transfers between devices with their start and end apart: 11, of which 7 were waited for; matrix products, arithmetic and copies ran while one was open for 0% of the time, Pallas kernels for 15%

profile of v3, /device:TPU:0, one launch (start us, length us, event | category | flops | bytes accessed | tf_op | source)
XLA Modules:
  0.0 33.4 jit_solution(15677730975146519652)
XLA Ops:
  0.6 1.0 %bundle.1.own_ref = bf16[272,512]{1,0:T(8,128)(2,1)S(1)} custom-call(s32[1,128]{1,0:T(1,128)} %seg_hbm.1, bf16[128,512]{1,0:T(8,128)(2,1)} %bitcast.12, bf16[128,512]{1,0:T(8,128)(2,1)} %bitcast.13), custom_call_target="tpu_custom_call" | custom-call | bytes 524288 | tf_op jit(solution)/shard_map/bundle/pallas_call | solution.py:298
  1.6 0.0 copy-start
  1.7 3.1 %collective-permute-start.1 = (bf16[272,512]{1,0:T(8,128)(2,1)S(1)}, bf16[272,512]{1,0:T(8,128)(2,1)S(1)}, u32[]{:S(2)}, u32[]{:S(2)}) collective-permute-start(bf16[272,512]{1,0:T(8,128)(2,1)S(1)} %bundle.1.own_ref), channel_id=1, source_target_pairs={{0,2},{1,3},{2,0},{3,1},{4,6},{5,7},{6,4},{7,5},{8,10},{9,11},{10,... | collective-permute-start | bytes 835592 | tf_op jit(solution)/shard_map/ppermute | solution.py:276
  4.8 0.0 collective-permute-start
  4.8 0.5 %collective-permute-start.2 = (bf16[272,512]{1,0:T(8,128)(2,1)S(1)}, bf16[272,512]{1,0:T(8,128)(2,1)S(1)}, u32[]{:S(2)}, u32[]{:S(2)}) collective-permute-start(bf16[272,512]{1,0:T(8,128)(2,1)S(1)} %bundle.1.own_ref), channel_id=1, source_target_pairs={{0,1},{1,0},{2,3},{3,2},{4,5},{5,4},{6,7},{7,6},{8,9},{9,8},{10,11... | collective-permute-start | bytes 835592 | tf_op jit(solution)/shard_map/ppermute | solution.py:262
  5.3 6.1 %collective-permute-done.1 = bf16[272,512]{1,0:T(8,128)(2,1)S(1)} collective-permute-done((bf16[272,512]{1,0:T(8,128)(2,1)S(1)}, bf16[272,512]{1,0:T(8,128)(2,1)S(1)}, u32[]{:S(2)}, u32[]{:S(2)}) %collective-permute-start.1) | collective-permute-done | bytes 278560 | tf_op jit(solution)/shard_map/ppermute | solution.py:276
  11.4 0.0 collective-permute-done
  11.4 0.0 copy-start.2
  11.5 0.1 collective-permute-start.3
  11.5 0.0 collective-permute-done.2.b_ref
  11.5 1.5 %collective-permute-done.3.c_ref = bf16[272,512]{1,0:T(8,128)(2,1)S(1)} collective-permute-done((bf16[272,512]{1,0:T(8,128)(2,1)S(1)}, bf16[272,512]{1,0:T(8,128)(2,1)S(1)}, u32[]{:S(2)}, u32[]{:S(2)}) %collective-permute-start.3) | collective-permute-done | bytes 278560 | tf_op jit(solution)/shard_map/ppermute | solution.py:262
  13.1 0.0 copy-done
  13.1 2.3 %attend.1 = (bf16[4,256,512]{2,1,0:T(8,128)(2,1)S(1)}, bf16[8,8,2048]{2,1,0:T(8,128)(2,1)S(1)}, bf16[8,8,2048]{2,1,0:T(8,128)(2,1)S(1)}, bf16[8,8,2048]{2,1,0:T(8,128)(2,1)S(1)}, bf16[8,8,2048]{2,1,0:T(8,128)(2,1)S(1)}) custom-call(s32[1,16]{1,0:T(1,128)S(1)} %copy-done.2, bf16[128,2048]{1,0:T(8,128)(2,1)S(1)} %bitcast.7, ...), custom_call_target="tpu_custom_call" | custom-call | flops 402653184 | bytes 4194304 | tf_op jit(solution)/shard_map/attend/pallas_call | solution.py:314
  15.4 2.7 %collective-permute-start.4 = (bf16[8,8,2048]{2,1,0:T(8,128)(2,1)S(1)}, bf16[8,8,2048]{2,1,0:T(8,128)(2,1)S(1)}, u32[]{:S(2)}, u32[]{:S(2)}) collective-permute-start(bf16[8,8,2048]{2,1,0:T(8,128)(2,1)S(1)} %get-tuple-element.20), channel_id=1, source_target_pairs={{0,24},{8,16},{16,8},{24,0},{1,25},{9,17},{17,9},{25,1},{2,26},{10... | collective-permute-start | bytes 786440 | tf_op jit(solution)/shard_map/ppermute | solution.py:285
  18.1 0.5 %collective-permute-start.5 = (bf16[8,8,2048]{2,1,0:T(8,128)(2,1)S(1)}, bf16[8,8,2048]{2,1,0:T(8,128)(2,1)S(1)}, u32[]{:S(2)}, u32[]{:S(2)}) collective-permute-start(bf16[8,8,2048]{2,1,0:T(8,128)(2,1)S(1)} %get-tuple-element.21), channel_id=1, source_target_pairs={{0,16},{8,24},{16,0},{24,8},{1,17},{9,25},{17,1},{25,9},{2,18},{10... | collective-permute-start | bytes 786440 | tf_op jit(solution)/shard_map/ppermute | solution.py:285
  18.6 0.4 %collective-permute-start.6 = (bf16[8,8,2048]{2,1,0:T(8,128)(2,1)S(1)}, bf16[8,8,2048]{2,1,0:T(8,128)(2,1)S(1)}, u32[]{:S(2)}, u32[]{:S(2)}) collective-permute-start(bf16[8,8,2048]{2,1,0:T(8,128)(2,1)S(1)} %get-tuple-element.22), channel_id=1, source_target_pairs={{0,8},{8,0},{16,24},{24,16},{1,9},{9,1},{17,25},{25,17},{2,10},{10... | collective-permute-start | bytes 786440 | tf_op jit(solution)/shard_map/ppermute | solution.py:285
  18.9 2.2 %sent_terms.1 = (bf16[4,256,512]{2,1,0:T(8,128)(2,1)S(1)}, bf16[256,512]{1,0:T(8,128)(2,1)S(1)}, bf16[128,512]{1,0:T(8,128)(2,1)S(1)}, bf16[128,512]{1,0:T(8,128)(2,1)S(1)}) custom-call(bf16[128,2048]{1,0:T(8,128)(2,1)S(1)} %bitcast.8, bf16[128,2048]{1,0:T(8,128)(2,1)S(1)} %bitcast.10, bf16[272,512]{1,0:T(8,128)(2,1)S(1)} %bundle.1.own_ref, ...), custom_call_target="tpu_custom_call" | custom-call | flops 469762048 | bytes 4194304 | tf_op jit(solution)/shard_map/sent_terms/pallas_call | solution.py:336
  21.1 0.1 collective-permute-start.7
  21.2 0.5 %collective-permute-start.8 = (bf16[128,512]{1,0:T(8,128)(2,1)S(1)}, bf16[128,512]{1,0:T(8,128)(2,1)S(1)}, u32[]{:S(2)}, u32[]{:S(2)}) collective-permute-start(bf16[128,512]{1,0:T(8,128)(2,1)S(1)} %get-tuple-element.31), channel_id=1, source_target_pairs={{0,1},{1,0},{2,3},{3,2},{4,5},{5,4},{6,7},{7,6},{8,9},{9,8},{10,11... | collective-permute-start | bytes 393224 | tf_op jit(solution)/shard_map/ppermute | solution.py:262
  21.7 0.8 %collective-permute-done.7.dk1_ref = bf16[128,512]{1,0:T(8,128)(2,1)S(1)} collective-permute-done((bf16[128,512]{1,0:T(8,128)(2,1)S(1)}, bf16[128,512]{1,0:T(8,128)(2,1)S(1)}, u32[]{:S(2)}, u32[]{:S(2)}) %collective-permute-start.7) | collective-permute-done | bytes 131104 | tf_op jit(solution)/shard_map/ppermute | solution.py:262
  22.5 0.2 collective-permute-done.8.dv1_ref
  22.7 0.1 merge.1
  22.8 2.9 %collective-permute-start.10 = (bf16[256,512]{1,0:T(8,128)(2,1)S(1)}, bf16[256,512]{1,0:T(8,128)(2,1)S(1)}, u32[]{:S(2)}, u32[]{:S(2)}) collective-permute-start(bf16[256,512]{1,0:T(8,128)(2,1)S(1)} %merge.1), channel_id=1, source_target_pairs={{0,2},{1,3},{2,0},{3,1},{4,6},{5,7},{6,4},{7,5},{8,10},{9,11},{10,... | collective-permute-start | bytes 786440 | tf_op jit(solution)/shard_map/ppermute | solution.py:276
  25.8 0.0 collective-permute-start.9
  25.8 1.7 %kept_terms.1 = (bf16[128,2048]{1,0:T(8,128)(2,1)}, f32[256,512]{1,0:T(8,128)S(1)}, f32[8,128]{1,0:T(8,128)S(1)}) custom-call(bf16[128,2048]{1,0:T(8,128)(2,1)S(1)} %bitcast.9, bf16[128,2048]{1,0:T(8,128)(2,1)S(1)} %bitcast.11, bf16[272,512]{1,0:T(8,128)(2,1)S(1)} %bundle.1.own_ref, bf16[272,512]{1,0:T(8,128)(2,1)S(1)} %broadcast_select_fusion.r_ref, ...), custom_call_target="tpu_custom_call" | custom-call | flops 1073741824 | tf_op jit(solution)/shard_map/kept_terms/pallas_call | solution.py:345
  27.5 0.0 collective-permute-done.4.rest_0_
  27.5 2.8 %collective-permute-done.5.rest_1_ = bf16[8,8,2048]{2,1,0:T(8,128)(2,1)S(1)} collective-permute-done((bf16[8,8,2048]{2,1,0:T(8,128)(2,1)S(1)}, bf16[8,8,2048]{2,1,0:T(8,128)(2,1)S(1)}, u32[]{:S(2)}, u32[]{:S(2)}) %collective-permute-start.5) | collective-permute-done | bytes 262176 | tf_op jit(solution)/shard_map/ppermute | solution.py:285
  30.3 0.3 collective-permute-done.6.rest_2_
  30.6 1.0 %join.1 = (bf16[1,1,4,8,8,2048]{5,4,3,2,1,0:T(8,128)(2,1)}, f32[8,128]{1,0:T(8,128)S(1)}) custom-call(bf16[8,8,2048]{2,1,0:T(8,128)(2,1)S(1)} %collective-permute-done.4.rest_0_, bf16[8,8,2048]{2,1,0:T(8,128)(2,1)S(1)} %collective-permute-done.5.rest_1_, bf16[8,8,2048]{2,1,0:T(8,128)(2,1)S(1)} %collective-permute-done.6.rest_2_, ...), custom_call_target="tpu_custom_call" | custom-call | flops 2147483648 | tf_op jit(solution)/shard_map/join/pallas_call | solution.py:369
  31.6 1.0 %collective-permute-done.10.even_ref = bf16[256,512]{1,0:T(8,128)(2,1)S(1)} collective-permute-done((bf16[256,512]{1,0:T(8,128)(2,1)S(1)}, bf16[256,512]{1,0:T(8,128)(2,1)S(1)}, u32[]{:S(2)}, u32[]{:S(2)}) %collective-permute-start.10) | collective-permute-done | bytes 262176 | tf_op jit(solution)/shard_map/ppermute | solution.py:276
  32.6 0.0 collective-permute-done.9.uneven_ref
  32.6 0.8 %total.1 = (bf16[128,512]{1,0:T(8,128)(2,1)}, bf16[128,512]{1,0:T(8,128)(2,1)}) custom-call(f32[256,512]{1,0:T(8,128)S(1)} %get-tuple-element.29.d0_ref, bf16[128,512]{1,0:T(8,128)(2,1)S(1)} %collective-permute-done.7.dk1_ref, bf16[128,512]{1,0:T(8,128)(2,1)S(1)} %collective-permute-done.8.dv1_ref, bf16[256,512]{1,0:T(8,128)(2,1)S(1)} %collective-permute-done.9.uneven_ref, ...), custom_call_target="tpu_custom_call" | custom-call | bytes 1048576 | tf_op jit(solution)/shard_map/total/pallas_call | solution.py:379
  (4 shorter events, 0.0 us)
Async XLA Ops:
  1.6 11.4 %copy-start = (bf16[1,128,2048]{2,1,0:T(8,128)(2,1)S(1)}, bf16[1,128,2048]{2,1,0:T(8,128)(2,1)}, u32[]{:S(2)}) copy-start(bf16[1,128,2048]{2,1,0:T(8,128)(2,1)} %param.6) | copy-start | bytes 1572868
  1.7 9.7 %collective-permute-start.1 = (bf16[272,512]{1,0:T(8,128)(2,1)S(1)}, bf16[272,512]{1,0:T(8,128)(2,1)S(1)}, u32[]{:S(2)}, u32[]{:S(2)}) collective-permute-start(bf16[272,512]{1,0:T(8,128)(2,1)S(1)} %bundle.1.own_ref), channel_id=1, source_target_pairs={{0,2},{1,3},{2,0},{3,1},{4,6},{5,7},{6,4},{7,5},{8,10},{9,11},{10,... | collective-permute-start | bytes 835592 | tf_op jit(solution)/shard_map/ppermute | solution.py:276
  4.8 6.7 %collective-permute-start = (bf16[272,512]{1,0:T(8,128)(2,1)S(1)}, bf16[272,512]{1,0:T(8,128)(2,1)S(1)}, u32[]{:S(2)}, u32[]{:S(2)}) collective-permute-start(bf16[272,512]{1,0:T(8,128)(2,1)S(1)} %bundle.1.own_ref), channel_id=1, source_target_pairs={{0,1},{1,0},{2,4},{3,5},{4,2},{5,3},{6,7},{7,6},{8,9},{9,8},{10,12... | collective-permute-start | bytes 835592 | tf_op jit(solution)/shard_map/ppermute | solution.py:276
  4.8 6.8 %collective-permute-start.2 = (bf16[272,512]{1,0:T(8,128)(2,1)S(1)}, bf16[272,512]{1,0:T(8,128)(2,1)S(1)}, u32[]{:S(2)}, u32[]{:S(2)}) collective-permute-start(bf16[272,512]{1,0:T(8,128)(2,1)S(1)} %bundle.1.own_ref), channel_id=1, source_target_pairs={{0,1},{1,0},{2,3},{3,2},{4,5},{5,4},{6,7},{7,6},{8,9},{9,8},{10,11... | collective-permute-start | bytes 835592 | tf_op jit(solution)/shard_map/ppermute | solution.py:262
  11.4 1.6 %copy-start.2 = (s32[1,16]{1,0:T(1,128)S(1)}, s32[1,16]{1,0:T(1,128)}, u32[]{:S(2)}) copy-start(s32[1,16]{1,0:T(1,128)} %home_hbm.1) | copy-start | bytes 196
  11.5 1.6 %collective-permute-start.3 = (bf16[272,512]{1,0:T(8,128)(2,1)S(1)}, bf16[272,512]{1,0:T(8,128)(2,1)S(1)}, u32[]{:S(2)}, u32[]{:S(2)}) collective-permute-start(bf16[272,512]{1,0:T(8,128)(2,1)S(1)} %broadcast_select_fusion.r_ref), channel_id=1, source_target_pairs={{0,1},{1,0},{2,3},{3,2},{4,5},{5,4},{6,7},{7,6},{8,9},{9,8},{10,11... | collective-permute-start | bytes 835592 | tf_op jit(solution)/shard_map/ppermute | solution.py:262
  13.1 5.8 %copy-start.1 = (bf16[1,128,2048]{2,1,0:T(8,128)(2,1)S(1)}, bf16[1,128,2048]{2,1,0:T(8,128)(2,1)}, u32[]{:S(2)}) copy-start(bf16[1,128,2048]{2,1,0:T(8,128)(2,1)} %param.9) | copy-start | bytes 1572868
  15.4 12.2 %collective-permute-start.4 = (bf16[8,8,2048]{2,1,0:T(8,128)(2,1)S(1)}, bf16[8,8,2048]{2,1,0:T(8,128)(2,1)S(1)}, u32[]{:S(2)}, u32[]{:S(2)}) collective-permute-start(bf16[8,8,2048]{2,1,0:T(8,128)(2,1)S(1)} %get-tuple-element.20), channel_id=1, source_target_pairs={{0,24},{8,16},{16,8},{24,0},{1,25},{9,17},{17,9},{25,1},{2,26},{10... | collective-permute-start | bytes 786440 | tf_op jit(solution)/shard_map/ppermute | solution.py:285
  18.1 12.2 %collective-permute-start.5 = (bf16[8,8,2048]{2,1,0:T(8,128)(2,1)S(1)}, bf16[8,8,2048]{2,1,0:T(8,128)(2,1)S(1)}, u32[]{:S(2)}, u32[]{:S(2)}) collective-permute-start(bf16[8,8,2048]{2,1,0:T(8,128)(2,1)S(1)} %get-tuple-element.21), channel_id=1, source_target_pairs={{0,16},{8,24},{16,0},{24,8},{1,17},{9,25},{17,1},{25,9},{2,18},{10... | collective-permute-start | bytes 786440 | tf_op jit(solution)/shard_map/ppermute | solution.py:285
  18.6 12.0 %collective-permute-start.6 = (bf16[8,8,2048]{2,1,0:T(8,128)(2,1)S(1)}, bf16[8,8,2048]{2,1,0:T(8,128)(2,1)S(1)}, u32[]{:S(2)}, u32[]{:S(2)}) collective-permute-start(bf16[8,8,2048]{2,1,0:T(8,128)(2,1)S(1)} %get-tuple-element.22), channel_id=1, source_target_pairs={{0,8},{8,0},{16,24},{24,16},{1,9},{9,1},{17,25},{25,17},{2,10},{10... | collective-permute-start | bytes 786440 | tf_op jit(solution)/shard_map/ppermute | solution.py:285
  21.1 1.4 %collective-permute-start.7 = (bf16[128,512]{1,0:T(8,128)(2,1)S(1)}, bf16[128,512]{1,0:T(8,128)(2,1)S(1)}, u32[]{:S(2)}, u32[]{:S(2)}) collective-permute-start(bf16[128,512]{1,0:T(8,128)(2,1)S(1)} %get-tuple-element.30), channel_id=1, source_target_pairs={{0,1},{1,0},{2,3},{3,2},{4,5},{5,4},{6,7},{7,6},{8,9},{9,8},{10,11... | collective-permute-start | bytes 393224 | tf_op jit(solution)/shard_map/ppermute | solution.py:262
  21.2 1.5 %collective-permute-start.8 = (bf16[128,512]{1,0:T(8,128)(2,1)S(1)}, bf16[128,512]{1,0:T(8,128)(2,1)S(1)}, u32[]{:S(2)}, u32[]{:S(2)}) collective-permute-start(bf16[128,512]{1,0:T(8,128)(2,1)S(1)} %get-tuple-element.31), channel_id=1, source_target_pairs={{0,1},{1,0},{2,3},{3,2},{4,5},{5,4},{6,7},{7,6},{8,9},{9,8},{10,11... | collective-permute-start | bytes 393224 | tf_op jit(solution)/shard_map/ppermute | solution.py:262
  22.8 9.7 %collective-permute-start.10 = (bf16[256,512]{1,0:T(8,128)(2,1)S(1)}, bf16[256,512]{1,0:T(8,128)(2,1)S(1)}, u32[]{:S(2)}, u32[]{:S(2)}) collective-permute-start(bf16[256,512]{1,0:T(8,128)(2,1)S(1)} %merge.1), channel_id=1, source_target_pairs={{0,2},{1,3},{2,0},{3,1},{4,6},{5,7},{6,4},{7,5},{8,10},{9,11},{10,... | collective-permute-start | bytes 786440 | tf_op jit(solution)/shard_map/ppermute | solution.py:276
  25.8 6.8 %collective-permute-start.9 = (bf16[256,512]{1,0:T(8,128)(2,1)S(1)}, bf16[256,512]{1,0:T(8,128)(2,1)S(1)}, u32[]{:S(2)}, u32[]{:S(2)}) collective-permute-start(bf16[256,512]{1,0:T(8,128)(2,1)S(1)} %merge.1), channel_id=1, source_target_pairs={{0,1},{1,0},{2,4},{3,5},{4,2},{5,3},{6,7},{7,6},{8,9},{9,8},{10,12... | collective-permute-start | bytes 786440 | tf_op jit(solution)/shard_map/ppermute | solution.py:276

commit v4 on v3

--- a/solution.py
+++ b/solution.py
@@ -31,19 +31,15 @@
     return jnp.concatenate(heads, axis=0)
 
 
-def window(g, block, own_ref, far, near):
+def window(g, block, own_ref, far_ref, near_ref):
     cols = slice(g * HEAD_DIM, (g + 1) * HEAD_DIM)
-    keys = (own_ref[0:block, cols], near[0:block, cols], far[0:block, cols])
+    keys = (own_ref[0:block, cols], near_ref[0:block, cols], far_ref[0:block, cols])
     values = (
         own_ref[block : 2 * block, cols],
-        near[block : 2 * block, cols],
-        far[block : 2 * block, cols],
+        near_ref[block : 2 * block, cols],
+        far_ref[block : 2 * block, cols],
     )
     return keys, values
-
-
-def near_block(column, b_ref, c_ref):
-    return jnp.where(lax.rem(column, 2) == 0, c_ref[...], b_ref[...])
 
 
 def triangle(block, copies):
@@ -56,24 +52,23 @@
     return home ^ row if count & (count - 1) == 0 else lax.rem(home - row + count, count)
 
 
-def fwd_kernel(n_dp, home_hbm, q_ref, own_ref, r_ref, b_ref, c_ref, *rest):
+def fwd_kernel(n_dp, home_hbm, qt_ref, s0_ref, own_ref, far_ref, near_ref, *rest):
     p_ref = rest[0]
     sends = rest[1 : 1 + n_dp]
     held, counts, filled, home_ref, sem = rest[1 + n_dp :]
     fetch = pltpu.make_async_copy(home_hbm, home_ref, sem)
     fetch.start()
-    block = q_ref.shape[0]
+    block = s0_ref.shape[1]
     column, row = lax.axis_index("ctx"), lax.axis_index("dp")
     pieces = home_ref.shape[1]
     piece_len = block // pieces
     capacity = sends[0].shape[0]
     held[pieces] = jnp.zeros(held.shape[1:], held.dtype)
-    near = near_block(column, b_ref, c_ref)
 
     def seg_of(value):
         return value[2 * block : 2 * block + SEG_ROWS, 0:block].astype(F32)[0:1]
 
-    seg_own, seg_near, seg_far = seg_of(own_ref), seg_of(near), seg_of(r_ref)
+    seg_own, seg_near, seg_far = seg_of(own_ref), seg_of(near_ref), seg_of(far_ref)
     first = seg_own[:, 0:1]
     reach = jnp.where(column >= 1, jnp.sum((seg_near == first).astype(F32), axis=1, keepdims=True), 0.0)
     reach = reach + jnp.where(
@@ -90,30 +85,28 @@
     bias_n = jnp.where(near_ok, 0.0, NEG)
     bias_x = jnp.concatenate([bias_x] * GROUP, axis=1)
     bias_n = jnp.concatenate([bias_n] * GROUP, axis=1)
-    tri_g = triangle(block, GROUP)
+    tri_g, lower = triangle(block, GROUP), lower_mask(block)
     scaling = math.log2(math.e) / math.sqrt(HEAD_DIM)
 
     for g in range(own_ref.shape[1] // HEAD_DIM):
-        keys, values = window(g, block, own_ref, r_ref, near)
-        queries = stacked(q_ref, g)
-        s_x = jnp.where(tri_g, dot(keys[0], queries, NT), dot(keys[2], queries, NT))
-        s_x = s_x * scaling + bias_x
-        s_n = dot(keys[1], queries, NT) * scaling + bias_n
+        keys, values = window(g, block, own_ref, far_ref, near_ref)
+        scores = dot(jnp.concatenate(keys[1:], axis=0), qt_ref[g], NN)
+        s_x = jnp.where(tri_g, s0_ref[g], scores[block:]) * scaling + bias_x
+        s_n = scores[0:block] * scaling + bias_n
         highest = jnp.max(jnp.maximum(s_x, s_n), axis=0, keepdims=True)
         e_x = jnp.exp2(s_x - highest)
         e_n = jnp.exp2(s_n - highest)
         inverse = 1.0 / jnp.sum(e_x + e_n, axis=0, keepdims=True)
-        w_x = e_x * inverse
+        w_x = (e_x * inverse).astype(BF16)
         w_n = (e_n * inverse).astype(BF16)
-        p_ref[g, 0:block] = w_x.astype(BF16)
+        p_ref[g, 0:block] = w_x
         p_ref[g, block : 2 * block] = w_n
-        w_0 = jnp.where(tri_g, w_x, 0.0).astype(BF16)
-        w_2 = jnp.where(tri_g, 0.0, w_x).astype(BF16)
+        w_0, w_2 = split(lower, w_x)
         weights = jnp.concatenate([w_0, w_n, w_2], axis=0)
-        attended = dot(weights, jnp.concatenate(values, axis=0), TN)
+        attended = dot(jnp.concatenate(values, axis=0), weights, TN).astype(BF16)
         for h in range(GROUP):
             cols = slice((g * GROUP + h) * HEAD_DIM, (g * GROUP + h + 1) * HEAD_DIM)
-            tile = attended[h * block : (h + 1) * block].astype(BF16)
+            tile = attended[:, h * block : (h + 1) * block].T
             held[0:pieces, :, cols] = tile.reshape(pieces, piece_len, HEAD_DIM)
     fetch.wait()
     for d in range(n_dp):
@@ -130,49 +123,67 @@
             sends[d][slot] = held[filled[d * capacity + slot]]
 
 
-def split(tri, packed):
-    own = jnp.where(tri, packed, 0.0).astype(BF16)
-    far = jnp.where(tri, 0.0, packed).astype(BF16)
-    return own, far
-
-
-def sent_kernel(q_ref, do_ref, own_ref, r_ref, b_ref, c_ref, p_ref, gs_ref, d2_ref, dk1_ref, dv1_ref):
+def split(lower, packed):
+    own = packed * lower
+    return own, packed - own
+
+
+def lower_mask(block):
+    return jnp.where(triangle(block, GROUP), 1.0, 0.0).astype(BF16)
+
+
+def ahead_kernel(home_ref, q_ref, do_ref, own_ref, plan_ref, qt_ref, gt_ref, s0_ref, gw0_ref):
+    plan_ref[...] = home_ref[...]
     block = q_ref.shape[0]
-    near = near_block(lax.axis_index("ctx"), b_ref, c_ref)
-    tri_g = triangle(block, GROUP)
+    for g in range(own_ref.shape[1] // HEAD_DIM):
+        cols = slice(g * HEAD_DIM, (g + 1) * HEAD_DIM)
+        for source, turned, product, rows in (
+            (q_ref, qt_ref, s0_ref, slice(0, block)),
+            (do_ref, gt_ref, gw0_ref, slice(block, 2 * block)),
+        ):
+            turned[g] = stacked(source, g).T
+            product[g] = dot(own_ref[rows, cols], turned[g], NN)
+
+
+def sent_kernel(q_ref, do_ref, gt_ref, gw0_ref, own_ref, far_ref, near_ref, p_ref, gs_ref, d2_ref, dk1_ref, dv1_ref):
+    block = q_ref.shape[0]
+    tri_g, lower = triangle(block, GROUP), lower_mask(block)
     scaling = 1.0 / math.sqrt(HEAD_DIM)
     for g in range(own_ref.shape[1] // HEAD_DIM):
-        _, values = window(g, block, own_ref, r_ref, near)
+        _, values = window(g, block, own_ref, far_ref, near_ref)
         queries, grads = stacked(q_ref, g), stacked(do_ref, g)
-        w_x = p_ref[g, 0:block].astype(F32)
+        w_xb = p_ref[g, 0:block]
+        w_x = w_xb.astype(F32)
         w_n = p_ref[g, block : 2 * block]
         w_nf = w_n.astype(F32)
-        gw_x = jnp.where(tri_g, dot(values[0], grads, NT), dot(values[2], grads, NT))
-        gw_n = dot(values[1], grads, NT)
+        score_terms = dot(jnp.concatenate(values[1:], axis=0), gt_ref[g], NN)
+        gw_x = jnp.where(tri_g, gw0_ref[g], score_terms[block:])
+        gw_n = score_terms[0:block]
         delta = jnp.sum(w_x * gw_x + w_nf * gw_n, axis=0, keepdims=True)
-        gs_x = w_x * (gw_x - delta) * scaling
+        gs_x = (w_x * (gw_x - delta) * scaling).astype(BF16)
         gs_n = (w_nf * (gw_n - delta) * scaling).astype(BF16)
-        gs_ref[g, 0:block] = gs_x.astype(BF16)
+        gs_ref[g, 0:block] = gs_x
         gs_ref[g, block : 2 * block] = gs_n
-        _, gs_2 = split(tri_g, gs_x)
-        _, w_2 = split(tri_g, w_x)
+        _, gs_2 = split(lower, gs_x)
+        _, w_2 = split(lower, w_xb)
         cols = slice(g * HEAD_DIM, (g + 1) * HEAD_DIM)
-        dk1_ref[:, cols] = dot(gs_n, queries, NN).astype(dk1_ref.dtype)
-        dv1_ref[:, cols] = dot(w_n, grads, NN).astype(dv1_ref.dtype)
-        d2_ref[0:block, cols] = dot(gs_2, queries, NN).astype(d2_ref.dtype)
-        d2_ref[block : 2 * block, cols] = dot(w_2, grads, NN).astype(d2_ref.dtype)
-
-
-def kept_kernel(q_ref, do_ref, own_ref, r_ref, b_ref, c_ref, p_ref, gs_ref, dq_ref, d0_ref, mark_ref):
+        dk = dot(jnp.concatenate([gs_n, gs_2], axis=0), queries, NN).astype(d2_ref.dtype)
+        dv = dot(jnp.concatenate([w_n, w_2], axis=0), grads, NN).astype(d2_ref.dtype)
+        dk1_ref[:, cols] = dk[0:block]
+        dv1_ref[:, cols] = dv[0:block]
+        d2_ref[0:block, cols] = dk[block:]
+        d2_ref[block : 2 * block, cols] = dv[block:]
+
+
+def kept_kernel(q_ref, do_ref, own_ref, far_ref, near_ref, p_ref, gs_ref, dq_ref, d0_ref, mark_ref):
     mark_ref[...] = jnp.zeros_like(mark_ref)
     block = q_ref.shape[0]
-    near = near_block(lax.axis_index("ctx"), b_ref, c_ref)
-    tri_g = triangle(block, GROUP)
+    lower = lower_mask(block)
     for g in range(own_ref.shape[1] // HEAD_DIM):
-        keys, _ = window(g, block, own_ref, r_ref, near)
+        keys, _ = window(g, block, own_ref, far_ref, near_ref)
         queries, grads = stacked(q_ref, g), stacked(do_ref, g)
-        gs_0, gs_2 = split(tri_g, gs_ref[g, 0:block].astype(F32))
-        w_0, _ = split(tri_g, p_ref[g, 0:block].astype(F32))
+        gs_0, gs_2 = split(lower, gs_ref[g, 0:block])
+        w_0, _ = split(lower, p_ref[g, 0:block])
         gs_n = gs_ref[g, block : 2 * block]
         cols = slice(g * HEAD_DIM, (g + 1) * HEAD_DIM)
         d0_ref[0:block, cols] = dot(gs_0, queries, NN)
@@ -210,24 +221,34 @@
         out_ref[rows] = (d2_ref[rows].astype(F32) + other).astype(out_ref.dtype)
 
 
-def join_kernel(n_dp, *rest):
-    pieces, (_, out_ref, mark_ref, sems) = rest[:n_dp], rest[n_dp:]
+def source_row(row, step, count):
+    return row ^ step if count & (count - 1) == 0 else lax.rem(row - step + count, count)
+
+
+def early_kernel(n_dp, kept_ref, far_ref, own_ref, out_ref, sems):
     row = lax.axis_index("dp")
-    copies = []
-    for k in range(n_dp):
-        source = row ^ k if n_dp & (n_dp - 1) == 0 else lax.rem(row - k + n_dp, n_dp)
-        copies.append(pltpu.make_async_copy(pieces[n_dp - 1 - k], out_ref.at[0, 0, source], sems.at[k]))
+    copies = [
+        pltpu.make_async_copy(own_ref, out_ref.at[0, 0, row], sems.at[0]),
+        pltpu.make_async_copy(
+            far_ref, out_ref.at[0, 0, source_row(row, n_dp - 1, n_dp)], sems.at[1]
+        ),
+    ]
     for copy in copies:
         copy.start()
-    mark_ref[...] = jnp.zeros_like(mark_ref)
     for copy in copies:
         copy.wait()
 
 
-def total_kernel(n_ctx, d0_ref, dk1_ref, dv1_ref, uneven_ref, even_ref, _, dk_ref, dv_ref, total_ref, sems):
-    column = lax.axis_index("ctx")
+def finish_kernel(n_dp, n_ctx, *rest):
+    pieces, rest = rest[: n_dp - 2], rest[n_dp - 2 :]
+    uneven_ref, even_ref, dk1_ref, dv1_ref, d0_ref, _, out_ref, dk_ref, dv_ref, total_ref, sems = rest
+    row, column = lax.axis_index("dp"), lax.axis_index("ctx")
     block = dk_ref.shape[0]
     copies = []
+    for i in range(n_dp - 2):
+        target = out_ref.at[0, 0, source_row(row, n_dp - 2 - i, n_dp)]
+        copies.append(pltpu.make_async_copy(pieces[i], target, sems.at[i]))
+        copies[-1].start()
     for part, (d1_ref, target) in enumerate(((dk1_ref, dk_ref), (dv1_ref, dv_ref))):
         rows = slice(part * block, (part + 1) * block)
         total = d0_ref[rows]
@@ -235,7 +256,7 @@
         d2 = jnp.where(lax.rem(column // 2, 2) == 0, even_ref[rows], uneven_ref[rows])
         total = total + jnp.where(column + 2 < n_ctx, d2.astype(F32), 0.0)
         total_ref[rows] = total.astype(total_ref.dtype)
-        copies.append(pltpu.make_async_copy(total_ref.at[rows], target, sems.at[part]))
+        copies.append(pltpu.make_async_copy(total_ref.at[rows], target, sems.at[n_dp - 2 + part]))
         copies[-1].start()
     for copy in copies:
         copy.wait()
@@ -308,9 +329,22 @@
     even, uneven = from_chip(own)
     far = jnp.where(lax.rem(column // 2, 2) == 0, uneven, even)
     beside = swap(own)
-    crossed = swap(far)
+    near = jnp.where(lax.rem(column, 2) == 0, swap(far), beside)
 
     pairs = 2 * block * block * GROUP * heads * HEAD_DIM
+    turned = jax.ShapeDtypeStruct((heads, HEAD_DIM, GROUP * block), BF16)
+    product = jax.ShapeDtypeStruct((heads, block, GROUP * block), F32)
+    plan, turned_query, turned_grad, own_scores, own_terms = pl.pallas_call(
+        ahead_kernel,
+        out_shape=[
+            jax.ShapeDtypeStruct(home_rows.shape, jnp.int32), turned, turned, product, product
+        ],
+        in_specs=[VMEM] * 4,
+        out_specs=[VMEM] * 5,
+        compiler_params=params(),
+        cost_estimate=cost(2 * pairs, 4 << 20),
+        name="ahead",
+    )(home_rows, query, grad, own)
     outs = pl.pallas_call(
         functools.partial(fwd_kernel, n_dp),
         out_shape=[jax.ShapeDtypeStruct((heads, 2 * block, GROUP * block), BF16)]
@@ -327,7 +361,7 @@
         compiler_params=params(),
         cost_estimate=cost(6 * pairs, 4 << 20),
         name="attend",
-    )(home_rows, query, own, far, beside, crossed)
+    )(plan, turned_query, own_scores, own, far, near)
     weights, sends = outs[0], outs[1:]
     arrived = [exchange(sends[k], k) for k in range(n_dp - 1, 0, -1)] + [sends[0]]
     terms = jax.ShapeDtypeStruct((2 * block, kv_width), BF16)
@@ -336,12 +370,12 @@
     score_grads, d2, dk1, dv1 = pl.pallas_call(
         sent_kernel,
         out_shape=[jax.ShapeDtypeStruct(weights.shape, BF16), terms, half, half],
-        in_specs=[VMEM] * 7,
+        in_specs=[VMEM] * 8,
         out_specs=[VMEM] * 4,
         compiler_params=params(),
-        cost_estimate=cost(7 * pairs, 4 << 20),
+        cost_estimate=cost(0, 0),
         name="sent_terms",
-    )(query, grad, own, far, beside, crossed, weights)
+    )(query, grad, turned_grad, own_terms, own, far, near, weights)
     dq, d0, after_kept = pl.pallas_call(
         kept_kernel,
         out_shape=[
@@ -349,12 +383,12 @@
             jax.ShapeDtypeStruct((2 * block, kv_width), F32),
             mark,
         ],
-        in_specs=[VMEM] * 8,
+        in_specs=[VMEM] * 7,
         out_specs=[VMEM] * 3,
         compiler_params=params(),
         cost_estimate=cost(1073741824, 0),
         name="kept_terms",
-    )(query, grad, own, far, beside, crossed, weights, score_grads)
+    )(query, grad, own, far, near, weights, score_grads)
     dk1_in, dv1_in = swap(dk1), swap(dv1)
     d2_sum = pl.pallas_call(
         merge_kernel,
@@ -366,29 +400,31 @@
         name="merge",
     )(d2, dk1_in, dv1_in)
     d2_even, d2_uneven = from_chip(d2_sum)
-    routed, after_join = pl.pallas_call(
-        functools.partial(join_kernel, n_dp),
-        out_shape=[jax.ShapeDtypeStruct((1, 1, n_dp, capacity, piece_len, width), BF16), mark],
-        in_specs=[HBM] * (n_dp + 1),
-        out_specs=[HBM, VMEM],
-        scratch_shapes=[pltpu.SemaphoreType.DMA((n_dp,))],
+    routed_shape = jax.ShapeDtypeStruct((1, 1, n_dp, capacity, piece_len, width), BF16)
+    routed = pl.pallas_call(
+        functools.partial(early_kernel, n_dp),
+        out_shape=routed_shape,
+        in_specs=[HBM] * 3,
+        out_specs=HBM,
+        scratch_shapes=[pltpu.SemaphoreType.DMA((2,))],
         compiler_params=params(),
         cost_estimate=cost(2147483648, 0),
-        name="join",
-    )(*arrived, after_kept)
-    dk, dv = pl.pallas_call(
-        functools.partial(total_kernel, n_ctx),
-        out_shape=[jax.ShapeDtypeStruct((block, kv_width), BF16)] * 2,
-        in_specs=[VMEM] * 5 + [HBM],
-        out_specs=[HBM] * 2,
+        name="place_early",
+    )(after_kept, arrived[0], arrived[-1])
+    routed, dk, dv = pl.pallas_call(
+        functools.partial(finish_kernel, n_dp, n_ctx),
+        out_shape=[routed_shape] + [jax.ShapeDtypeStruct((block, kv_width), BF16)] * 2,
+        in_specs=[HBM] * (n_dp - 2) + [VMEM] * 5 + [HBM],
+        out_specs=[HBM] * 3,
+        input_output_aliases={n_dp + 3: 0},
         scratch_shapes=[
             pltpu.VMEM((2 * block, kv_width), BF16),
-            pltpu.SemaphoreType.DMA((2,)),
+            pltpu.SemaphoreType.DMA((n_dp,)),
         ],
         compiler_params=params(),
         cost_estimate=cost(0, 1 << 20),
-        name="total",
-    )(d0, dk1_in, dv1_in, d2_uneven, d2_even, after_join)
+        name="finish",
+    )(*arrived[1:-1], d2_uneven, d2_even, dk1_in, dv1_in, d0, *pinned(routed))
     return routed, dq[None], dk[None], dv[None]
 
 

time: 33.5 us -> 32.3 us (0.964)
  waiting for transfers between devices: 12.7 us -> 11 us
  local copies, waits for them, and re-layouts: 0.02 us -> 0.64 us
    ppermute x4, waiting for transfers between devices: 2.56 us -> 0.53 us  [swap(): return lax.ppermute(value, 'ctx', [(i, i ^ 1) for i in range(count)])]
    unnamed x6, local copies, waits for them, and re-layouts: 0.02 us -> 0.64 us
    ppermute x3, waiting for transfers between devices: 3.04 us -> 3.45 us  [exchange(): return lax.ppermute(value, 'dp', pairs)]
    pallas_call x2 -> x3, Pallas kernels: 1.79 us -> 2.21 us  [the longest x1 0.91 us: on_device(): pl.pallas_call(functools.partial(finish_kernel, n_dp, n_ctx), out_shape=[...]
  transfers between devices with their start and end apart: 11 -> 11, of which waited for: 7 -> 6; matrix products, arithmetic and copies ran while one was open for 0% -> 0% of each run, Pallas kernels for 15% -> 16%
where the time goes in v4:
time: 32.3 us; the launch traced here: 32.2 us
  waiting for transfers between devices  11 us (34%)
  starting transfers between devices  10.6 us (33%)
  Pallas kernels  9.19 us (28%)
  between operations  0.75 us (2%)
  local copies, waits for them, and re-layouts  0.64 us (2%)
    ppermute x2, waiting for transfers between devices, from_chip(): lax.ppermute(value, 'ctx', pairs(0))  6.98 us
    ppermute x2, starting transfers between devices, from_chip(): lax.ppermute(value, 'ctx', pairs(0))  5.88 us
    ppermute x3, starting transfers between devices, exchange(): return lax.ppermute(value, 'dp', pairs)  3.55 us
    ppermute x3, waiting for transfers between devices, exchange(): return lax.ppermute(value, 'dp', pairs)  3.45 us
    pallas_call x1, Pallas kernels, on_device(): pl.pallas_call(functools.partial(fwd_kernel, n_dp), out_shape=[jax.ShapeD...  2.1 us
    pallas_call x1, Pallas kernels, on_device(): pl.pallas_call(sent_kernel, out_shape=[jax.ShapeDtypeStruct(weights.shape...  2.08 us
    pallas_call x1, Pallas kernels, on_device(): pl.pallas_call(kept_kernel, out_shape=[jax.ShapeDtypeStruct((block, width...  1.65 us
    ppermute x4, starting transfers between devices, swap(): return lax.ppermute(value, 'ctx', [(i, i ^ 1) for i in range(count)])  1.15 us
  transfers between devices with their start and end apart: 11, of which 6 were waited for; matrix products, arithmetic and copies ran while one was open for 0% of the time, Pallas kernels for 16%

profile of v4, /device:TPU:0, one launch (start us, length us, event | category | flops | bytes accessed | tf_op | source)
XLA Modules:
  0.0 32.2 jit_solution(11689997980864217108)
XLA Ops:
  0.6 1.1 %bundle.1.own_ref = bf16[272,512]{1,0:T(8,128)(2,1)S(1)} custom-call(s32[1,128]{1,0:T(1,128)} %seg_hbm.1, bf16[128,512]{1,0:T(8,128)(2,1)} %bitcast.13, bf16[128,512]{1,0:T(8,128)(2,1)} %bitcast.14), custom_call_target="tpu_custom_call" | custom-call | bytes 524288 | tf_op jit(solution)/shard_map/bundle/pallas_call | solution.py:319
  1.7 0.0 copy-start
  1.7 3.1 %collective-permute-start.1 = (bf16[272,512]{1,0:T(8,128)(2,1)S(1)}, bf16[272,512]{1,0:T(8,128)(2,1)S(1)}, u32[]{:S(2)}, u32[]{:S(2)}) collective-permute-start(bf16[272,512]{1,0:T(8,128)(2,1)S(1)} %bundle.1.own_ref), channel_id=1, source_target_pairs={{0,2},{1,3},{2,0},{3,1},{4,6},{5,7},{6,4},{7,5},{8,10},{9,11},{10,... | collective-permute-start | bytes 835592 | tf_op jit(solution)/shard_map/ppermute | solution.py:297
  4.8 0.0 collective-permute-start
  4.8 0.5 %collective-permute-start.3 = (bf16[272,512]{1,0:T(8,128)(2,1)S(1)}, bf16[272,512]{1,0:T(8,128)(2,1)S(1)}, u32[]{:S(2)}, u32[]{:S(2)}) collective-permute-start(bf16[272,512]{1,0:T(8,128)(2,1)S(1)} %bundle.1.own_ref), channel_id=1, source_target_pairs={{0,1},{1,0},{2,3},{3,2},{4,5},{5,4},{6,7},{7,6},{8,9},{9,8},{10,11... | collective-permute-start | bytes 835592 | tf_op jit(solution)/shard_map/ppermute | solution.py:283
  5.3 6.1 %collective-permute-done.1 = bf16[272,512]{1,0:T(8,128)(2,1)S(1)} collective-permute-done((bf16[272,512]{1,0:T(8,128)(2,1)S(1)}, bf16[272,512]{1,0:T(8,128)(2,1)S(1)}, u32[]{:S(2)}, u32[]{:S(2)}) %collective-permute-start.1) | collective-permute-done | bytes 278560 | tf_op jit(solution)/shard_map/ppermute | solution.py:297
  11.5 0.0 collective-permute-done
  11.5 0.1 collective-permute-start.2
  11.6 0.0 copy-start.2
  11.6 0.6 %copy-done.2 = s32[1,16]{1,0:T(1,128)S(1)} copy-done((s32[1,16]{1,0:T(1,128)S(1)}, s32[1,16]{1,0:T(1,128)}, u32[]{:S(2)}) %copy-start.2) | copy-done | bytes 88
  12.3 0.5 %ahead.1 = (s32[1,16]{1,0:T(1,128)S(1)}, bf16[4,128,512]{2,1,0:T(8,128)(2,1)S(1)}, bf16[4,128,512]{2,1,0:T(8,128)(2,1)S(1)}, f32[4,128,512]{2,1,0:T(8,128)S(1)}, f32[4,128,512]{2,1,0:T(8,128)S(1)}) custom-call(s32[1,16]{1,0:T(1,128)S(1)} %copy-done.2, bf16[128,2048]{1,0:T(8,128)(2,1)S(1)} %bitcast.7, bf16[128,2048]{1,0:T(8,128)(2,1)S(1)} %bitcast.10, ...), custom_call_target="tpu_custom_call" | custom-call | flops 134217728 | bytes 4194304 | tf_op jit(solution)/shard_map/ahead/pallas_call | solution.py:337
  12.7 0.0 collective-permute-done.3
  12.8 0.4 %collective-permute-done.2 = bf16[272,512]{1,0:T(8,128)(2,1)S(1)} collective-permute-done((bf16[272,512]{1,0:T(8,128)(2,1)S(1)}, bf16[272,512]{1,0:T(8,128)(2,1)S(1)}, u32[]{:S(2)}, u32[]{:S(2)}) %collective-permute-start.2) | collective-permute-done | bytes 278560 | tf_op jit(solution)/shard_map/ppermute | solution.py:283
  13.2 2.1 %attend.1 = (bf16[4,256,512]{2,1,0:T(8,128)(2,1)S(1)}, bf16[8,8,2048]{2,1,0:T(8,128)(2,1)S(1)}, bf16[8,8,2048]{2,1,0:T(8,128)(2,1)S(1)}, bf16[8,8,2048]{2,1,0:T(8,128)(2,1)S(1)}, bf16[8,8,2048]{2,1,0:T(8,128)(2,1)S(1)}) custom-call(s32[1,16]{1,0:T(1,128)S(1)} %get-tuple-element.24.home_hbm, bf16[4,128,512]{2,1,0:T(8,128)(2,1)S(1)} %get-tuple-element.25.qt_ref, ...), custom_call_target="tpu_custom_call" | custom-call | flops 402653184 | bytes 4194304 | tf_op jit(solution)/shard_map/attend/pallas_call | solution.py:348
  15.3 2.7 %collective-permute-start.10 = (bf16[8,8,2048]{2,1,0:T(8,128)(2,1)S(1)}, bf16[8,8,2048]{2,1,0:T(8,128)(2,1)S(1)}, u32[]{:S(2)}, u32[]{:S(2)}) collective-permute-start(bf16[8,8,2048]{2,1,0:T(8,128)(2,1)S(1)} %get-tuple-element.38), channel_id=1, source_target_pairs={{0,24},{8,16},{16,8},{24,0},{1,25},{9,17},{17,9},{25,1},{2,26},{10... | collective-permute-start | bytes 786440 | tf_op jit(solution)/shard_map/ppermute | solution.py:306
  18.0 2.1 %sent_terms.1 = (bf16[4,256,512]{2,1,0:T(8,128)(2,1)S(1)}, bf16[256,512]{1,0:T(8,128)(2,1)S(1)}, bf16[128,512]{1,0:T(8,128)(2,1)S(1)}, bf16[128,512]{1,0:T(8,128)(2,1)S(1)}) custom-call(bf16[128,2048]{1,0:T(8,128)(2,1)S(1)} %bitcast.8, bf16[128,2048]{1,0:T(8,128)(2,1)S(1)} %bitcast.11, bf16[4,128,512]{2,1,0:T(8,128)(2,1)S(1)} %get-tuple-element.29.gt_ref, ...), custom_call_target="tpu_custom_call" | custom-call | tf_op jit(solution)/shard_map/sent_terms/pallas_call | solution.py:370
  20.0 0.1 collective-permute-start.6
  20.1 0.5 %collective-permute-start.7 = (bf16[128,512]{1,0:T(8,128)(2,1)S(1)}, bf16[128,512]{1,0:T(8,128)(2,1)S(1)}, u32[]{:S(2)}, u32[]{:S(2)}) collective-permute-start(bf16[128,512]{1,0:T(8,128)(2,1)S(1)} %get-tuple-element.34), channel_id=1, source_target_pairs={{0,1},{1,0},{2,3},{3,2},{4,5},{5,4},{6,7},{7,6},{8,9},{9,8},{10,11... | collective-permute-start | bytes 393224 | tf_op jit(solution)/shard_map/ppermute | solution.py:283
  20.6 0.5 %collective-permute-start.4 = (bf16[8,8,2048]{2,1,0:T(8,128)(2,1)S(1)}, bf16[8,8,2048]{2,1,0:T(8,128)(2,1)S(1)}, u32[]{:S(2)}, u32[]{:S(2)}) collective-permute-start(bf16[8,8,2048]{2,1,0:T(8,128)(2,1)S(1)} %get-tuple-element.27), channel_id=1, source_target_pairs={{0,16},{8,24},{16,0},{24,8},{1,17},{9,25},{17,1},{25,9},{2,18},{10... | collective-permute-start | bytes 786440 | tf_op jit(solution)/shard_map/ppermute | solution.py:306
  21.1 0.4 %collective-permute-start.5 = (bf16[8,8,2048]{2,1,0:T(8,128)(2,1)S(1)}, bf16[8,8,2048]{2,1,0:T(8,128)(2,1)S(1)}, u32[]{:S(2)}, u32[]{:S(2)}) collective-permute-start(bf16[8,8,2048]{2,1,0:T(8,128)(2,1)S(1)} %get-tuple-element.28), channel_id=1, source_target_pairs={{0,8},{8,0},{16,24},{24,16},{1,9},{9,1},{17,25},{25,17},{2,10},{10... | collective-permute-start | bytes 786440 | tf_op jit(solution)/shard_map/ppermute | solution.py:306
  21.5 0.0 collective-permute-done.6.dk1_ref.rest_4_
  21.5 0.1 collective-permute-done.7.dv1_ref.rest_5_
  21.6 0.1 merge.1
  21.7 2.8 %collective-permute-start.9 = (bf16[256,512]{1,0:T(8,128)(2,1)S(1)}, bf16[256,512]{1,0:T(8,128)(2,1)S(1)}, u32[]{:S(2)}, u32[]{:S(2)}) collective-permute-start(bf16[256,512]{1,0:T(8,128)(2,1)S(1)} %merge.1), channel_id=1, source_target_pairs={{0,2},{1,3},{2,0},{3,1},{4,6},{5,7},{6,4},{7,5},{8,10},{9,11},{10,... | collective-permute-start | bytes 786440 | tf_op jit(solution)/shard_map/ppermute | solution.py:297
  24.5 0.0 collective-permute-start.8
  24.5 1.6 %kept_terms.1 = (bf16[128,2048]{1,0:T(8,128)(2,1)}, f32[256,512]{1,0:T(8,128)S(1)}, f32[8,128]{1,0:T(8,128)S(1)}) custom-call(bf16[128,2048]{1,0:T(8,128)(2,1)S(1)} %bitcast.9, bf16[128,2048]{1,0:T(8,128)(2,1)S(1)} %bitcast.12, bf16[272,512]{1,0:T(8,128)(2,1)S(1)} %bundle.1.own_ref, bf16[272,512]{1,0:T(8,128)(2,1)S(1)} %broadcast_select_fusion.1.far_ref, ...), custom_call_target="tpu_custom_call" | custom-call | flops 1073741824 | tf_op jit(solution)/shard_map/kept_terms/pallas_call | solution.py:379
  26.2 0.0 collective-permute-done.10.far_ref
  26.2 0.8 %place_early.1.rest_7_ = bf16[1,1,4,8,8,2048]{5,4,3,2,1,0:T(8,128)(2,1)} custom-call(f32[8,128]{1,0:T(8,128)S(1)} %get-tuple-element.37.kept_ref, bf16[8,8,2048]{2,1,0:T(8,128)(2,1)S(1)} %collective-permute-done.10.far_ref, bf16[8,8,2048]{2,1,0:T(8,128)(2,1)S(1)} %get-tuple-element.39.own_ref), custom_call_target="tpu_custom_call" | custom-call | flops 2147483648 | tf_op jit(solution)/shard_map/place_early/pallas_call | solution.py:404
  27.0 3.2 %collective-permute-done.4.rest_0_ = bf16[8,8,2048]{2,1,0:T(8,128)(2,1)S(1)} collective-permute-done((bf16[8,8,2048]{2,1,0:T(8,128)(2,1)S(1)}, bf16[8,8,2048]{2,1,0:T(8,128)(2,1)S(1)}, u32[]{:S(2)}, u32[]{:S(2)}) %collective-permute-start.4) | collective-permute-done | bytes 262176 | tf_op jit(solution)/shard_map/ppermute | solution.py:306
  30.2 0.2 collective-permute-done.5.rest_1_
  30.5 0.8 %collective-permute-done.9.rest_3_ = bf16[256,512]{1,0:T(8,128)(2,1)S(1)} collective-permute-done((bf16[256,512]{1,0:T(8,128)(2,1)S(1)}, bf16[256,512]{1,0:T(8,128)(2,1)S(1)}, u32[]{:S(2)}, u32[]{:S(2)}) %collective-permute-start.9) | collective-permute-done | bytes 262176 | tf_op jit(solution)/shard_map/ppermute | solution.py:297
  31.3 0.9 %finish.1 = (bf16[1,1,4,8,8,2048]{5,4,3,2,1,0:T(8,128)(2,1)}, bf16[128,512]{1,0:T(8,128)(2,1)}, bf16[128,512]{1,0:T(8,128)(2,1)}) custom-call(bf16[8,8,2048]{2,1,0:T(8,128)(2,1)S(1)} %collective-permute-done.4.rest_0_, bf16[8,8,2048]{2,1,0:T(8,128)(2,1)S(1)} %collective-permute-done.5.rest_1_, ...), custom_call_target="tpu_custom_call", output_to_operand_aliasing={{0}: (7, {})} | custom-call | bytes 1048576 | tf_op jit(solution)/shard_map/finish/pallas_call | solution.py:414
  (6 shorter events, 0.1 us)
Async XLA Ops:
  0.6 11.0 %copy-start.1 = (bf16[1,128,2048]{2,1,0:T(8,128)(2,1)S(1)}, bf16[1,128,2048]{2,1,0:T(8,128)(2,1)}, u32[]{:S(2)}) copy-start(bf16[1,128,2048]{2,1,0:T(8,128)(2,1)} %param.9) | copy-start | bytes 1572868
  1.7 9.9 %copy-start = (bf16[1,128,2048]{2,1,0:T(8,128)(2,1)S(1)}, bf16[1,128,2048]{2,1,0:T(8,128)(2,1)}, u32[]{:S(2)}) copy-start(bf16[1,128,2048]{2,1,0:T(8,128)(2,1)} %param.6) | copy-start | bytes 1572868
  1.7 9.7 %collective-permute-start.1 = (bf16[272,512]{1,0:T(8,128)(2,1)S(1)}, bf16[272,512]{1,0:T(8,128)(2,1)S(1)}, u32[]{:S(2)}, u32[]{:S(2)}) collective-permute-start(bf16[272,512]{1,0:T(8,128)(2,1)S(1)} %bundle.1.own_ref), channel_id=1, source_target_pairs={{0,2},{1,3},{2,0},{3,1},{4,6},{5,7},{6,4},{7,5},{8,10},{9,11},{10,... | collective-permute-start | bytes 835592 | tf_op jit(solution)/shard_map/ppermute | solution.py:297
  4.8 6.7 %collective-permute-start = (bf16[272,512]{1,0:T(8,128)(2,1)S(1)}, bf16[272,512]{1,0:T(8,128)(2,1)S(1)}, u32[]{:S(2)}, u32[]{:S(2)}) collective-permute-start(bf16[272,512]{1,0:T(8,128)(2,1)S(1)} %bundle.1.own_ref), channel_id=1, source_target_pairs={{0,1},{1,0},{2,4},{3,5},{4,2},{5,3},{6,7},{7,6},{8,9},{9,8},{10,12... | collective-permute-start | bytes 835592 | tf_op jit(solution)/shard_map/ppermute | solution.py:297
  4.8 7.9 %collective-permute-start.3 = (bf16[272,512]{1,0:T(8,128)(2,1)S(1)}, bf16[272,512]{1,0:T(8,128)(2,1)S(1)}, u32[]{:S(2)}, u32[]{:S(2)}) collective-permute-start(bf16[272,512]{1,0:T(8,128)(2,1)S(1)} %bundle.1.own_ref), channel_id=1, source_target_pairs={{0,1},{1,0},{2,3},{3,2},{4,5},{5,4},{6,7},{7,6},{8,9},{9,8},{10,11... | collective-permute-start | bytes 835592 | tf_op jit(solution)/shard_map/ppermute | solution.py:283
  11.5 1.6 %collective-permute-start.2 = (bf16[272,512]{1,0:T(8,128)(2,1)S(1)}, bf16[272,512]{1,0:T(8,128)(2,1)S(1)}, u32[]{:S(2)}, u32[]{:S(2)}) collective-permute-start(bf16[272,512]{1,0:T(8,128)(2,1)S(1)} %broadcast_select_fusion.1.far_ref), channel_id=1, source_target_pairs={{0,1},{1,0},{2,3},{3,2},{4,5},{5,4},{6,7},{7,6},{8,9},{9,8},{10,11... | collective-permute-start | bytes 835592 | tf_op jit(solution)/shard_map/ppermute | solution.py:283
  11.6 0.7 %copy-start.2 = (s32[1,16]{1,0:T(1,128)S(1)}, s32[1,16]{1,0:T(1,128)}, u32[]{:S(2)}) copy-start(s32[1,16]{1,0:T(1,128)} %home_ref.1) | copy-start | bytes 196
  15.3 10.9 %collective-permute-start.10 = (bf16[8,8,2048]{2,1,0:T(8,128)(2,1)S(1)}, bf16[8,8,2048]{2,1,0:T(8,128)(2,1)S(1)}, u32[]{:S(2)}, u32[]{:S(2)}) collective-permute-start(bf16[8,8,2048]{2,1,0:T(8,128)(2,1)S(1)} %get-tuple-element.38), channel_id=1, source_target_pairs={{0,24},{8,16},{16,8},{24,0},{1,25},{9,17},{17,9},{25,1},{2,26},{10... | collective-permute-start | bytes 786440 | tf_op jit(solution)/shard_map/ppermute | solution.py:306
  20.0 1.5 %collective-permute-start.6 = (bf16[128,512]{1,0:T(8,128)(2,1)S(1)}, bf16[128,512]{1,0:T(8,128)(2,1)S(1)}, u32[]{:S(2)}, u32[]{:S(2)}) collective-permute-start(bf16[128,512]{1,0:T(8,128)(2,1)S(1)} %get-tuple-element.33), channel_id=1, source_target_pairs={{0,1},{1,0},{2,3},{3,2},{4,5},{5,4},{6,7},{7,6},{8,9},{9,8},{10,11... | collective-permute-start | bytes 393224 | tf_op jit(solution)/shard_map/ppermute | solution.py:283
  20.1 1.5 %collective-permute-start.7 = (bf16[128,512]{1,0:T(8,128)(2,1)S(1)}, bf16[128,512]{1,0:T(8,128)(2,1)S(1)}, u32[]{:S(2)}, u32[]{:S(2)}) collective-permute-start(bf16[128,512]{1,0:T(8,128)(2,1)S(1)} %get-tuple-element.34), channel_id=1, source_target_pairs={{0,1},{1,0},{2,3},{3,2},{4,5},{5,4},{6,7},{7,6},{8,9},{9,8},{10,11... | collective-permute-start | bytes 393224 | tf_op jit(solution)/shard_map/ppermute | solution.py:283
  20.6 9.6 %collective-permute-start.4 = (bf16[8,8,2048]{2,1,0:T(8,128)(2,1)S(1)}, bf16[8,8,2048]{2,1,0:T(8,128)(2,1)S(1)}, u32[]{:S(2)}, u32[]{:S(2)}) collective-permute-start(bf16[8,8,2048]{2,1,0:T(8,128)(2,1)S(1)} %get-tuple-element.27), channel_id=1, source_target_pairs={{0,16},{8,24},{16,0},{24,8},{1,17},{9,25},{17,1},{25,9},{2,18},{10... | collective-permute-start | bytes 786440 | tf_op jit(solution)/shard_map/ppermute | solution.py:306
  21.1 9.3 %collective-permute-start.5 = (bf16[8,8,2048]{2,1,0:T(8,128)(2,1)S(1)}, bf16[8,8,2048]{2,1,0:T(8,128)(2,1)S(1)}, u32[]{:S(2)}, u32[]{:S(2)}) collective-permute-start(bf16[8,8,2048]{2,1,0:T(8,128)(2,1)S(1)} %get-tuple-element.28), channel_id=1, source_target_pairs={{0,8},{8,0},{16,24},{24,16},{1,9},{9,1},{17,25},{25,17},{2,10},{10... | collective-permute-start | bytes 786440 | tf_op jit(solution)/shard_map/ppermute | solution.py:306
  21.7 9.6 %collective-permute-start.9 = (bf16[256,512]{1,0:T(8,128)(2,1)S(1)}, bf16[256,512]{1,0:T(8,128)(2,1)S(1)}, u32[]{:S(2)}, u32[]{:S(2)}) collective-permute-start(bf16[256,512]{1,0:T(8,128)(2,1)S(1)} %merge.1), channel_id=1, source_target_pairs={{0,2},{1,3},{2,0},{3,1},{4,6},{5,7},{6,4},{7,5},{8,10},{9,11},{10,... | collective-permute-start | bytes 786440 | tf_op jit(solution)/shard_map/ppermute | solution.py:297
  24.5 6.8 %collective-permute-start.8 = (bf16[256,512]{1,0:T(8,128)(2,1)S(1)}, bf16[256,512]{1,0:T(8,128)(2,1)S(1)}, u32[]{:S(2)}, u32[]{:S(2)}) collective-permute-start(bf16[256,512]{1,0:T(8,128)(2,1)S(1)} %merge.1), channel_id=1, source_target_pairs={{0,1},{1,0},{2,4},{3,5},{4,2},{5,3},{6,7},{7,6},{8,9},{9,8},{10,12... | collective-permute-start | bytes 786440 | tf_op jit(solution)/shard_map/ppermute | solution.py:297

commit v5 on v4

--- a/solution.py
+++ b/solution.py
@@ -283,18 +283,18 @@
     return lax.ppermute(value, "ctx", [(i, i ^ 1) for i in range(count)])
 
 
-def from_chip(value):
+def from_chip(value, colours):
     count = lax.axis_size("ctx")
 
-    def pairs(first):
+    def pairs(colour):
         found = []
         for i in range(count):
-            chip = i // 2
-            other = chip + 1 if (chip - first) % 2 == 0 else chip - 1
-            found.append((i, 2 * other + i % 2 if 0 <= other < count // 2 else i ^ 1))
+            chip, core = i // 2, i % 2
+            other = chip + 1 if chip % colours == colour else chip - 1 if (chip - 1) % colours == colour else -1
+            found.append((i, 2 * other + core if 0 <= other < count // 2 else i ^ 1))
         return found
 
-    return lax.ppermute(value, "ctx", pairs(0)), lax.ppermute(value, "ctx", pairs(1))
+    return [lax.ppermute(value, "ctx", pairs(colour)) for colour in range(colours)]
 
 
 def exchange(value, k):
@@ -326,8 +326,9 @@
         cost_estimate=cost(0, 1 << 19),
         name="bundle",
     )(*pinned(segment_ids, key_rows[0], value_rows[0]))
-    even, uneven = from_chip(own)
-    far = jnp.where(lax.rem(column // 2, 2) == 0, uneven, even)
+    moved = from_chip(own, 3)
+    colour = lax.rem(column // 2 + 2, 3)
+    far = jnp.where(colour == 2, moved[2], jnp.where(colour == 1, moved[1], moved[0]))
     beside = swap(own)
     near = jnp.where(lax.rem(column, 2) == 0, swap(far), beside)
 
@@ -399,7 +400,7 @@
         cost_estimate=cost(0, 0),
         name="merge",
     )(d2, dk1_in, dv1_in)
-    d2_even, d2_uneven = from_chip(d2_sum)
+    d2_even, d2_uneven = from_chip(d2_sum, 2)
     routed_shape = jax.ShapeDtypeStruct((1, 1, n_dp, capacity, piece_len, width), BF16)
     routed = pl.pallas_call(
         functools.partial(early_kernel, n_dp),

time: 32.3 us -> 31.9 us (0.988)
  starting transfers between devices: 10.6 us -> 9.99 us
    ppermute x4 -> x5, waiting for transfers between devices: 6.99 us -> 6.37 us  [from_chip(): lax.ppermute(value, 'ctx', pairs(colour))]
    ppermute x3, waiting for transfers between devices: 3.45 us -> 4.06 us  [exchange(): return lax.ppermute(value, 'dp', pairs)]
    ppermute x4, starting transfers between devices: 1.15 us -> 0.64 us  [swap(): return lax.ppermute(value, 'ctx', [(i, i ^ 1) for i in range(count)])]
    ppermute x4 -> x5, starting transfers between devices: 5.9 us -> 5.79 us  [from_chip(): lax.ppermute(value, 'ctx', pairs(colour))]
  transfers between devices with their start and end apart: 11 -> 12, of which waited for: 6 -> 6; matrix products, arithmetic and copies ran while one was open for 0% -> 0% of each run, Pallas kernels for 16% -> 16%
where the time goes in v5:
time: 31.9 us; the launch traced here: 31.5 us
  waiting for transfers between devices  10.9 us (34%)
  starting transfers between devices  9.99 us (31%)
  Pallas kernels  9.13 us (29%)
  between operations  0.74 us (2%)
  local copies, waits for them, and re-layouts  0.64 us (2%)
    ppermute x5, waiting for transfers between devices, from_chip(): lax.ppermute(value, 'ctx', pairs(colour))  6.37 us
    ppermute x5, starting transfers between devices, from_chip(): lax.ppermute(value, 'ctx', pairs(colour))  5.79 us
    ppermute x3, waiting for transfers between devices, exchange(): return lax.ppermute(value, 'dp', pairs)  4.06 us
    ppermute x3, starting transfers between devices, exchange(): return lax.ppermute(value, 'dp', pairs)  3.56 us
    pallas_call x1, Pallas kernels, on_device(): pl.pallas_call(functools.partial(fwd_kernel, n_dp), out_shape=[jax.ShapeD...  2.1 us
    pallas_call x1, Pallas kernels, on_device(): pl.pallas_call(sent_kernel, out_shape=[jax.ShapeDtypeStruct(weights.shape...  2.07 us
    pallas_call x1, Pallas kernels, on_device(): pl.pallas_call(kept_kernel, out_shape=[jax.ShapeDtypeStruct((block, width...  1.65 us
    pallas_call x1, Pallas kernels, on_device(): pl.pallas_call(prep_kernel, out_shape=jax.ShapeDtypeStruct((2 * block + S...  1.01 us
  transfers between devices with their start and end apart: 12, of which 6 were waited for; matrix products, arithmetic and copies ran while one was open for 0% of the time, Pallas kernels for 16%

profile of v5, /device:TPU:0, one launch (start us, length us, event | category | flops | bytes accessed | tf_op | source)
XLA Modules:
  0.0 31.5 jit_solution(18260831231736900583)
XLA Ops:
  0.6 1.0 %bundle.1.own_ref = bf16[272,512]{1,0:T(8,128)(2,1)S(1)} custom-call(s32[1,128]{1,0:T(1,128)} %seg_hbm.1, bf16[128,512]{1,0:T(8,128)(2,1)} %bitcast.13, bf16[128,512]{1,0:T(8,128)(2,1)} %bitcast.14), custom_call_target="tpu_custom_call" | custom-call | bytes 524288 | tf_op jit(solution)/shard_map/bundle/pallas_call | solution.py:319
  1.6 3.1 %collective-permute-start.2 = (bf16[272,512]{1,0:T(8,128)(2,1)S(1)}, bf16[272,512]{1,0:T(8,128)(2,1)S(1)}, u32[]{:S(2)}, u32[]{:S(2)}) collective-permute-start(bf16[272,512]{1,0:T(8,128)(2,1)S(1)} %bundle.1.own_ref), channel_id=1, source_target_pairs={{0,2},{1,3},{2,0},{3,1},{4,5},{5,4},{6,7},{7,6},{8,10},{9,11},{10,... | collective-permute-start | bytes 835592 | tf_op jit(solution)/shard_map/ppermute | solution.py:297
  4.7 0.0 collective-permute-start.1
  4.7 0.5 %collective-permute-start = (bf16[272,512]{1,0:T(8,128)(2,1)S(1)}, bf16[272,512]{1,0:T(8,128)(2,1)S(1)}, u32[]{:S(2)}, u32[]{:S(2)}) collective-permute-start(bf16[272,512]{1,0:T(8,128)(2,1)S(1)} %bundle.1.own_ref), channel_id=1, source_target_pairs={{0,1},{1,0},{2,3},{3,2},{4,6},{5,7},{6,4},{7,5},{8,9},{9,8},{10,11... | collective-permute-start | bytes 835592 | tf_op jit(solution)/shard_map/ppermute | solution.py:297
  5.2 0.0 collective-permute-start.4
  5.3 6.1 %collective-permute-done.2 = bf16[272,512]{1,0:T(8,128)(2,1)S(1)} collective-permute-done((bf16[272,512]{1,0:T(8,128)(2,1)S(1)}, bf16[272,512]{1,0:T(8,128)(2,1)S(1)}, u32[]{:S(2)}, u32[]{:S(2)}) %collective-permute-start.2) | collective-permute-done | bytes 278560 | tf_op jit(solution)/shard_map/ppermute | solution.py:297
  11.4 0.0 collective-permute-done.1
  11.4 0.0 collective-permute-done
  11.4 0.1 collective-permute-start.3
  11.5 0.0 copy-start.2
  11.6 0.6 %copy-done.2 = s32[1,16]{1,0:T(1,128)S(1)} copy-done((s32[1,16]{1,0:T(1,128)S(1)}, s32[1,16]{1,0:T(1,128)}, u32[]{:S(2)}) %copy-start.2) | copy-done | bytes 88
  12.2 0.5 %ahead.1 = (s32[1,16]{1,0:T(1,128)S(1)}, bf16[4,128,512]{2,1,0:T(8,128)(2,1)S(1)}, bf16[4,128,512]{2,1,0:T(8,128)(2,1)S(1)}, f32[4,128,512]{2,1,0:T(8,128)S(1)}, f32[4,128,512]{2,1,0:T(8,128)S(1)}) custom-call(s32[1,16]{1,0:T(1,128)S(1)} %copy-done.2, bf16[128,2048]{1,0:T(8,128)(2,1)S(1)} %bitcast.7, bf16[128,2048]{1,0:T(8,128)(2,1)S(1)} %bitcast.10, ...), custom_call_target="tpu_custom_call" | custom-call | flops 134217728 | bytes 4194304 | tf_op jit(solution)/shard_map/ahead/pallas_call | solution.py:338
  12.7 0.4 %collective-permute-done.3 = bf16[272,512]{1,0:T(8,128)(2,1)S(1)} collective-permute-done((bf16[272,512]{1,0:T(8,128)(2,1)S(1)}, bf16[272,512]{1,0:T(8,128)(2,1)S(1)}, u32[]{:S(2)}, u32[]{:S(2)}) %collective-permute-start.3) | collective-permute-done | bytes 278560 | tf_op jit(solution)/shard_map/ppermute | solution.py:283
  13.1 2.1 %attend.1 = (bf16[4,256,512]{2,1,0:T(8,128)(2,1)S(1)}, bf16[8,8,2048]{2,1,0:T(8,128)(2,1)S(1)}, bf16[8,8,2048]{2,1,0:T(8,128)(2,1)S(1)}, bf16[8,8,2048]{2,1,0:T(8,128)(2,1)S(1)}, bf16[8,8,2048]{2,1,0:T(8,128)(2,1)S(1)}) custom-call(s32[1,16]{1,0:T(1,128)S(1)} %get-tuple-element.24.home_hbm, bf16[4,128,512]{2,1,0:T(8,128)(2,1)S(1)} %get-tuple-element.25.qt_ref, ...), custom_call_target="tpu_custom_call" | custom-call | flops 402653184 | bytes 4194304 | tf_op jit(solution)/shard_map/attend/pallas_call | solution.py:349
  15.2 2.7 %collective-permute-start.11 = (bf16[8,8,2048]{2,1,0:T(8,128)(2,1)S(1)}, bf16[8,8,2048]{2,1,0:T(8,128)(2,1)S(1)}, u32[]{:S(2)}, u32[]{:S(2)}) collective-permute-start(bf16[8,8,2048]{2,1,0:T(8,128)(2,1)S(1)} %get-tuple-element.38), channel_id=1, source_target_pairs={{0,24},{8,16},{16,8},{24,0},{1,25},{9,17},{17,9},{25,1},{2,26},{10... | collective-permute-start | bytes 786440 | tf_op jit(solution)/shard_map/ppermute | solution.py:306
  17.9 2.1 %sent_terms.1 = (bf16[4,256,512]{2,1,0:T(8,128)(2,1)S(1)}, bf16[256,512]{1,0:T(8,128)(2,1)S(1)}, bf16[128,512]{1,0:T(8,128)(2,1)S(1)}, bf16[128,512]{1,0:T(8,128)(2,1)S(1)}) custom-call(bf16[128,2048]{1,0:T(8,128)(2,1)S(1)} %bitcast.8, bf16[128,2048]{1,0:T(8,128)(2,1)S(1)} %bitcast.11, bf16[4,128,512]{2,1,0:T(8,128)(2,1)S(1)} %get-tuple-element.29.gt_ref, ...), custom_call_target="tpu_custom_call" | custom-call | tf_op jit(solution)/shard_map/sent_terms/pallas_call | solution.py:371
  20.0 0.1 collective-permute-start.7
  20.0 0.5 %collective-permute-start.8 = (bf16[128,512]{1,0:T(8,128)(2,1)S(1)}, bf16[128,512]{1,0:T(8,128)(2,1)S(1)}, u32[]{:S(2)}, u32[]{:S(2)}) collective-permute-start(bf16[128,512]{1,0:T(8,128)(2,1)S(1)} %get-tuple-element.34), channel_id=1, source_target_pairs={{0,1},{1,0},{2,3},{3,2},{4,5},{5,4},{6,7},{7,6},{8,9},{9,8},{10,11... | collective-permute-start | bytes 393224 | tf_op jit(solution)/shard_map/ppermute | solution.py:283
  20.5 0.5 %collective-permute-start.5 = (bf16[8,8,2048]{2,1,0:T(8,128)(2,1)S(1)}, bf16[8,8,2048]{2,1,0:T(8,128)(2,1)S(1)}, u32[]{:S(2)}, u32[]{:S(2)}) collective-permute-start(bf16[8,8,2048]{2,1,0:T(8,128)(2,1)S(1)} %get-tuple-element.27), channel_id=1, source_target_pairs={{0,16},{8,24},{16,0},{24,8},{1,17},{9,25},{17,1},{25,9},{2,18},{10... | collective-permute-start | bytes 786440 | tf_op jit(solution)/shard_map/ppermute | solution.py:306
  21.0 0.4 %collective-permute-start.6 = (bf16[8,8,2048]{2,1,0:T(8,128)(2,1)S(1)}, bf16[8,8,2048]{2,1,0:T(8,128)(2,1)S(1)}, u32[]{:S(2)}, u32[]{:S(2)}) collective-permute-start(bf16[8,8,2048]{2,1,0:T(8,128)(2,1)S(1)} %get-tuple-element.28), channel_id=1, source_target_pairs={{0,8},{8,0},{16,24},{24,16},{1,9},{9,1},{17,25},{25,17},{2,10},{10... | collective-permute-start | bytes 786440 | tf_op jit(solution)/shard_map/ppermute | solution.py:306
  21.4 0.0 collective-permute-done.7.dk1_ref.rest_4_
  21.4 0.1 collective-permute-done.8.dv1_ref.rest_5_
  21.6 0.1 merge.1
  21.7 2.2 %collective-permute-start.10 = (bf16[256,512]{1,0:T(8,128)(2,1)S(1)}, bf16[256,512]{1,0:T(8,128)(2,1)S(1)}, u32[]{:S(2)}, u32[]{:S(2)}) collective-permute-start(bf16[256,512]{1,0:T(8,128)(2,1)S(1)} %merge.1), channel_id=1, source_target_pairs={{0,2},{1,3},{2,0},{3,1},{4,6},{5,7},{6,4},{7,5},{8,10},{9,11},{10,... | collective-permute-start | bytes 786440 | tf_op jit(solution)/shard_map/ppermute | solution.py:297
  23.8 0.0 collective-permute-start.9
  23.9 1.6 %kept_terms.1 = (bf16[128,2048]{1,0:T(8,128)(2,1)}, f32[256,512]{1,0:T(8,128)S(1)}, f32[8,128]{1,0:T(8,128)S(1)}) custom-call(bf16[128,2048]{1,0:T(8,128)(2,1)S(1)} %bitcast.9, bf16[128,2048]{1,0:T(8,128)(2,1)S(1)} %bitcast.12, bf16[272,512]{1,0:T(8,128)(2,1)S(1)} %bundle.1.own_ref, bf16[272,512]{1,0:T(8,128)(2,1)S(1)} %select_select_fusion.far_ref, ...), custom_call_target="tpu_custom_call" | custom-call | flops 1073741824 | tf_op jit(solution)/shard_map/kept_terms/pallas_call | solution.py:380
  25.5 0.8 %place_early.1.rest_7_ = bf16[1,1,4,8,8,2048]{5,4,3,2,1,0:T(8,128)(2,1)} custom-call(f32[8,128]{1,0:T(8,128)S(1)} %get-tuple-element.37.kept_ref, bf16[8,8,2048]{2,1,0:T(8,128)(2,1)S(1)} %collective-permute-done.11.far_ref, bf16[8,8,2048]{2,1,0:T(8,128)(2,1)S(1)} %get-tuple-element.39.own_ref), custom_call_target="tpu_custom_call" | custom-call | flops 2147483648 | tf_op jit(solution)/shard_map/place_early/pallas_call | solution.py:405
  26.3 3.8 %collective-permute-done.5.rest_0_ = bf16[8,8,2048]{2,1,0:T(8,128)(2,1)S(1)} collective-permute-done((bf16[8,8,2048]{2,1,0:T(8,128)(2,1)S(1)}, bf16[8,8,2048]{2,1,0:T(8,128)(2,1)S(1)}, u32[]{:S(2)}, u32[]{:S(2)}) %collective-permute-start.5) | collective-permute-done | bytes 262176 | tf_op jit(solution)/shard_map/ppermute | solution.py:306
  30.1 0.2 collective-permute-done.6.rest_1_
  30.4 0.2 collective-permute-done.10.rest_3_
  30.6 0.0 collective-permute-done.9.rest_2_
  30.6 0.9 %finish.1 = (bf16[1,1,4,8,8,2048]{5,4,3,2,1,0:T(8,128)(2,1)}, bf16[128,512]{1,0:T(8,128)(2,1)}, bf16[128,512]{1,0:T(8,128)(2,1)}) custom-call(bf16[8,8,2048]{2,1,0:T(8,128)(2,1)S(1)} %collective-permute-done.5.rest_0_, bf16[8,8,2048]{2,1,0:T(8,128)(2,1)S(1)} %collective-permute-done.6.rest_1_, ...), custom_call_target="tpu_custom_call", output_to_operand_aliasing={{0}: (7, {})} | custom-call | bytes 1048576 | tf_op jit(solution)/shard_map/finish/pallas_call | solution.py:415
  (8 shorter events, 0.1 us)
Async XLA Ops:
  1.6 9.7 %collective-permute-start.2 = (bf16[272,512]{1,0:T(8,128)(2,1)S(1)}, bf16[272,512]{1,0:T(8,128)(2,1)S(1)}, u32[]{:S(2)}, u32[]{:S(2)}) collective-permute-start(bf16[272,512]{1,0:T(8,128)(2,1)S(1)} %bundle.1.own_ref), channel_id=1, source_target_pairs={{0,2},{1,3},{2,0},{3,1},{4,5},{5,4},{6,7},{7,6},{8,10},{9,11},{10,... | collective-permute-start | bytes 835592 | tf_op jit(solution)/shard_map/ppermute | solution.py:297
  4.7 6.7 %collective-permute-start.1 = (bf16[272,512]{1,0:T(8,128)(2,1)S(1)}, bf16[272,512]{1,0:T(8,128)(2,1)S(1)}, u32[]{:S(2)}, u32[]{:S(2)}) collective-permute-start(bf16[272,512]{1,0:T(8,128)(2,1)S(1)} %bundle.1.own_ref), channel_id=1, source_target_pairs={{0,1},{1,0},{2,4},{3,5},{4,2},{5,3},{6,7},{7,6},{8,9},{9,8},{10,12... | collective-permute-start | bytes 835592 | tf_op jit(solution)/shard_map/ppermute | solution.py:297
  4.7 6.7 %collective-permute-start = (bf16[272,512]{1,0:T(8,128)(2,1)S(1)}, bf16[272,512]{1,0:T(8,128)(2,1)S(1)}, u32[]{:S(2)}, u32[]{:S(2)}) collective-permute-start(bf16[272,512]{1,0:T(8,128)(2,1)S(1)} %bundle.1.own_ref), channel_id=1, source_target_pairs={{0,1},{1,0},{2,3},{3,2},{4,6},{5,7},{6,4},{7,5},{8,9},{9,8},{10,11... | collective-permute-start | bytes 835592 | tf_op jit(solution)/shard_map/ppermute | solution.py:297
  5.2 7.4 %collective-permute-start.4 = (bf16[272,512]{1,0:T(8,128)(2,1)S(1)}, bf16[272,512]{1,0:T(8,128)(2,1)S(1)}, u32[]{:S(2)}, u32[]{:S(2)}) collective-permute-start(bf16[272,512]{1,0:T(8,128)(2,1)S(1)} %bundle.1.own_ref), channel_id=1, source_target_pairs={{0,1},{1,0},{2,3},{3,2},{4,5},{5,4},{6,7},{7,6},{8,9},{9,8},{10,11... | collective-permute-start | bytes 835592 | tf_op jit(solution)/shard_map/ppermute | solution.py:283
  5.3 6.3 %copy-start = (bf16[1,128,2048]{2,1,0:T(8,128)(2,1)S(1)}, bf16[1,128,2048]{2,1,0:T(8,128)(2,1)}, u32[]{:S(2)}) copy-start(bf16[1,128,2048]{2,1,0:T(8,128)(2,1)} %param.6) | copy-start | bytes 1572868
  5.3 6.3 %copy-start.1 = (bf16[1,128,2048]{2,1,0:T(8,128)(2,1)S(1)}, bf16[1,128,2048]{2,1,0:T(8,128)(2,1)}, u32[]{:S(2)}) copy-start(bf16[1,128,2048]{2,1,0:T(8,128)(2,1)} %param.9) | copy-start | bytes 1572868
  11.4 1.6 %collective-permute-start.3 = (bf16[272,512]{1,0:T(8,128)(2,1)S(1)}, bf16[272,512]{1,0:T(8,128)(2,1)S(1)}, u32[]{:S(2)}, u32[]{:S(2)}) collective-permute-start(bf16[272,512]{1,0:T(8,128)(2,1)S(1)} %select_select_fusion.far_ref), channel_id=1, source_target_pairs={{0,1},{1,0},{2,3},{3,2},{4,5},{5,4},{6,7},{7,6},{8,9},{9,8},{10,11... | collective-permute-start | bytes 835592 | tf_op jit(solution)/shard_map/ppermute | solution.py:283
  11.5 0.7 %copy-start.2 = (s32[1,16]{1,0:T(1,128)S(1)}, s32[1,16]{1,0:T(1,128)}, u32[]{:S(2)}) copy-start(s32[1,16]{1,0:T(1,128)} %home_ref.1) | copy-start | bytes 196
  15.2 10.3 %collective-permute-start.11 = (bf16[8,8,2048]{2,1,0:T(8,128)(2,1)S(1)}, bf16[8,8,2048]{2,1,0:T(8,128)(2,1)S(1)}, u32[]{:S(2)}, u32[]{:S(2)}) collective-permute-start(bf16[8,8,2048]{2,1,0:T(8,128)(2,1)S(1)} %get-tuple-element.38), channel_id=1, source_target_pairs={{0,24},{8,16},{16,8},{24,0},{1,25},{9,17},{17,9},{25,1},{2,26},{10... | collective-permute-start | bytes 786440 | tf_op jit(solution)/shard_map/ppermute | solution.py:306
  20.0 1.5 %collective-permute-start.7 = (bf16[128,512]{1,0:T(8,128)(2,1)S(1)}, bf16[128,512]{1,0:T(8,128)(2,1)S(1)}, u32[]{:S(2)}, u32[]{:S(2)}) collective-permute-start(bf16[128,512]{1,0:T(8,128)(2,1)S(1)} %get-tuple-element.33), channel_id=1, source_target_pairs={{0,1},{1,0},{2,3},{3,2},{4,5},{5,4},{6,7},{7,6},{8,9},{9,8},{10,11... | collective-permute-start | bytes 393224 | tf_op jit(solution)/shard_map/ppermute | solution.py:283
  20.0 1.5 %collective-permute-start.8 = (bf16[128,512]{1,0:T(8,128)(2,1)S(1)}, bf16[128,512]{1,0:T(8,128)(2,1)S(1)}, u32[]{:S(2)}, u32[]{:S(2)}) collective-permute-start(bf16[128,512]{1,0:T(8,128)(2,1)S(1)} %get-tuple-element.34), channel_id=1, source_target_pairs={{0,1},{1,0},{2,3},{3,2},{4,5},{5,4},{6,7},{7,6},{8,9},{9,8},{10,11... | collective-permute-start | bytes 393224 | tf_op jit(solution)/shard_map/ppermute | solution.py:283
  20.5 9.6 %collective-permute-start.5 = (bf16[8,8,2048]{2,1,0:T(8,128)(2,1)S(1)}, bf16[8,8,2048]{2,1,0:T(8,128)(2,1)S(1)}, u32[]{:S(2)}, u32[]{:S(2)}) collective-permute-start(bf16[8,8,2048]{2,1,0:T(8,128)(2,1)S(1)} %get-tuple-element.27), channel_id=1, source_target_pairs={{0,16},{8,24},{16,0},{24,8},{1,17},{9,25},{17,1},{25,9},{2,18},{10... | collective-permute-start | bytes 786440 | tf_op jit(solution)/shard_map/ppermute | solution.py:306
  21.0 9.3 %collective-permute-start.6 = (bf16[8,8,2048]{2,1,0:T(8,128)(2,1)S(1)}, bf16[8,8,2048]{2,1,0:T(8,128)(2,1)S(1)}, u32[]{:S(2)}, u32[]{:S(2)}) collective-permute-start(bf16[8,8,2048]{2,1,0:T(8,128)(2,1)S(1)} %get-tuple-element.28), channel_id=1, source_target_pairs={{0,8},{8,0},{16,24},{24,16},{1,9},{9,1},{17,25},{25,17},{2,10},{10... | collective-permute-start | bytes 786440 | tf_op jit(solution)/shard_map/ppermute | solution.py:306
  21.7 8.9 %collective-permute-start.10 = (bf16[256,512]{1,0:T(8,128)(2,1)S(1)}, bf16[256,512]{1,0:T(8,128)(2,1)S(1)}, u32[]{:S(2)}, u32[]{:S(2)}) collective-permute-start(bf16[256,512]{1,0:T(8,128)(2,1)S(1)} %merge.1), channel_id=1, source_target_pairs={{0,2},{1,3},{2,0},{3,1},{4,6},{5,7},{6,4},{7,5},{8,10},{9,11},{10,... | collective-permute-start | bytes 786440 | tf_op jit(solution)/shard_map/ppermute | solution.py:297
  23.8 6.8 %collective-permute-start.9 = (bf16[256,512]{1,0:T(8,128)(2,1)S(1)}, bf16[256,512]{1,0:T(8,128)(2,1)S(1)}, u32[]{:S(2)}, u32[]{:S(2)}) collective-permute-start(bf16[256,512]{1,0:T(8,128)(2,1)S(1)} %merge.1), channel_id=1, source_target_pairs={{0,1},{1,0},{2,4},{3,5},{4,2},{5,3},{6,7},{7,6},{8,9},{9,8},{10,12... | collective-permute-start | bytes 786440 | tf_op jit(solution)/shard_map/ppermute | solution.py:297

commit v6 on v5

--- a/solution.py
+++ b/solution.py
@@ -31,15 +31,9 @@
     return jnp.concatenate(heads, axis=0)
 
 
-def window(g, block, own_ref, far_ref, near_ref):
+def head_blocks(g, block, own_ref, far_ref, near_ref):
     cols = slice(g * HEAD_DIM, (g + 1) * HEAD_DIM)
-    keys = (own_ref[0:block, cols], near_ref[0:block, cols], far_ref[0:block, cols])
-    values = (
-        own_ref[block : 2 * block, cols],
-        near_ref[block : 2 * block, cols],
-        far_ref[block : 2 * block, cols],
-    )
-    return keys, values
+    return [ref[0:block, cols] for ref in (own_ref, near_ref, far_ref)]
 
 
 def triangle(block, copies):
@@ -52,21 +46,12 @@
     return home ^ row if count & (count - 1) == 0 else lax.rem(home - row + count, count)
 
 
-def fwd_kernel(n_dp, home_hbm, qt_ref, s0_ref, own_ref, far_ref, near_ref, *rest):
-    p_ref = rest[0]
-    sends = rest[1 : 1 + n_dp]
-    held, counts, filled, home_ref, sem = rest[1 + n_dp :]
-    fetch = pltpu.make_async_copy(home_hbm, home_ref, sem)
-    fetch.start()
+def weights_kernel(qt_ref, s0_ref, own_ref, far_ref, near_ref, p_ref):
     block = s0_ref.shape[1]
-    column, row = lax.axis_index("ctx"), lax.axis_index("dp")
-    pieces = home_ref.shape[1]
-    piece_len = block // pieces
-    capacity = sends[0].shape[0]
-    held[pieces] = jnp.zeros(held.shape[1:], held.dtype)
-
-    def seg_of(value):
-        return value[2 * block : 2 * block + SEG_ROWS, 0:block].astype(F32)[0:1]
+    column = lax.axis_index("ctx")
+
+    def seg_of(ref):
+        return ref[block : block + SEG_ROWS, 0:block].astype(F32)[0:1]
 
     seg_own, seg_near, seg_far = seg_of(own_ref), seg_of(near_ref), seg_of(far_ref)
     first = seg_own[:, 0:1]
@@ -85,11 +70,10 @@
     bias_n = jnp.where(near_ok, 0.0, NEG)
     bias_x = jnp.concatenate([bias_x] * GROUP, axis=1)
     bias_n = jnp.concatenate([bias_n] * GROUP, axis=1)
-    tri_g, lower = triangle(block, GROUP), lower_mask(block)
+    tri_g = triangle(block, GROUP)
     scaling = math.log2(math.e) / math.sqrt(HEAD_DIM)
-
-    for g in range(own_ref.shape[1] // HEAD_DIM):
-        keys, values = window(g, block, own_ref, far_ref, near_ref)
+    for g in range(qt_ref.shape[0]):
+        keys = head_blocks(g, block, own_ref, far_ref, near_ref)
         scores = dot(jnp.concatenate(keys[1:], axis=0), qt_ref[g], NN)
         s_x = jnp.where(tri_g, s0_ref[g], scores[block:]) * scaling + bias_x
         s_n = scores[0:block] * scaling + bias_n
@@ -97,12 +81,25 @@
         e_x = jnp.exp2(s_x - highest)
         e_n = jnp.exp2(s_n - highest)
         inverse = 1.0 / jnp.sum(e_x + e_n, axis=0, keepdims=True)
-        w_x = (e_x * inverse).astype(BF16)
-        w_n = (e_n * inverse).astype(BF16)
-        p_ref[g, 0:block] = w_x
-        p_ref[g, block : 2 * block] = w_n
-        w_0, w_2 = split(lower, w_x)
-        weights = jnp.concatenate([w_0, w_n, w_2], axis=0)
+        p_ref[g, 0:block] = (e_x * inverse).astype(BF16)
+        p_ref[g, block : 2 * block] = (e_n * inverse).astype(BF16)
+
+
+def attend_kernel(n_dp, home_hbm, p_ref, own_ref, far_ref, near_ref, *rest):
+    sends, (held, counts, filled, home_ref, sem) = rest[:n_dp], rest[n_dp:]
+    fetch = pltpu.make_async_copy(home_hbm, home_ref, sem)
+    fetch.start()
+    block = own_ref.shape[0]
+    row = lax.axis_index("dp")
+    pieces = home_ref.shape[1]
+    piece_len = block // pieces
+    capacity = sends[0].shape[0]
+    held[pieces] = jnp.zeros(held.shape[1:], held.dtype)
+    lower = lower_mask(block)
+    for g in range(p_ref.shape[0]):
+        values = head_blocks(g, block, own_ref, far_ref, near_ref)
+        w_0, w_2 = split(lower, p_ref[g, 0:block])
+        weights = jnp.concatenate([w_0, p_ref[g, block : 2 * block], w_2], axis=0)
         attended = dot(jnp.concatenate(values, axis=0), weights, TN).astype(BF16)
         for h in range(GROUP):
             cols = slice((g * GROUP + h) * HEAD_DIM, (g * GROUP + h + 1) * HEAD_DIM)
@@ -118,7 +115,7 @@
         slot = counts[step]
         counts[step] = slot + 1
         filled[step * capacity + slot] = m
-    for d in range(n_dp):
+    for d in range(n_dp - 1, -1, -1):
         for slot in range(capacity):
             sends[d][slot] = held[filled[d * capacity + slot]]
 
@@ -132,17 +129,24 @@
     return jnp.where(triangle(block, GROUP), 1.0, 0.0).astype(BF16)
 
 
-def ahead_kernel(home_ref, q_ref, do_ref, own_ref, plan_ref, qt_ref, gt_ref, s0_ref, gw0_ref):
-    plan_ref[...] = home_ref[...]
+def ahead_kernel(
+    home_hbm, q_hbm, do_hbm, v_hbm, key_ref,
+    plan_ref, qt_ref, gt_ref, s0_ref, gw0_ref, q_ref, do_ref, v_ref, sems,
+):
+    pairs = ((q_hbm, q_ref), (do_hbm, do_ref), (v_hbm, v_ref), (home_hbm, plan_ref))
+    copies = [pltpu.make_async_copy(*pair, sems.at[i]) for i, pair in enumerate(pairs)]
+    for copy in copies:
+        copy.start()
     block = q_ref.shape[0]
-    for g in range(own_ref.shape[1] // HEAD_DIM):
-        cols = slice(g * HEAD_DIM, (g + 1) * HEAD_DIM)
-        for source, turned, product, rows in (
-            (q_ref, qt_ref, s0_ref, slice(0, block)),
-            (do_ref, gt_ref, gw0_ref, slice(block, 2 * block)),
-        ):
+    for source, own_ref, turned, product, waits in (
+        (q_ref, key_ref, qt_ref, s0_ref, copies[:1]),
+        (do_ref, v_ref, gt_ref, gw0_ref, copies[1:]),
+    ):
+        for copy in waits:
+            copy.wait()
+        for g in range(qt_ref.shape[0]):
             turned[g] = stacked(source, g).T
-            product[g] = dot(own_ref[rows, cols], turned[g], NN)
+            product[g] = dot(own_ref[0:block, g * HEAD_DIM : (g + 1) * HEAD_DIM], turned[g], NN)
 
 
 def sent_kernel(q_ref, do_ref, gt_ref, gw0_ref, own_ref, far_ref, near_ref, p_ref, gs_ref, d2_ref, dk1_ref, dv1_ref):
@@ -150,7 +154,7 @@
     tri_g, lower = triangle(block, GROUP), lower_mask(block)
     scaling = 1.0 / math.sqrt(HEAD_DIM)
     for g in range(own_ref.shape[1] // HEAD_DIM):
-        _, values = window(g, block, own_ref, far_ref, near_ref)
+        values = head_blocks(g, block, own_ref, far_ref, near_ref)
         queries, grads = stacked(q_ref, g), stacked(do_ref, g)
         w_xb = p_ref[g, 0:block]
         w_x = w_xb.astype(F32)
@@ -180,7 +184,7 @@
     block = q_ref.shape[0]
     lower = lower_mask(block)
     for g in range(own_ref.shape[1] // HEAD_DIM):
-        keys, _ = window(g, block, own_ref, far_ref, near_ref)
+        keys = head_blocks(g, block, own_ref, far_ref, near_ref)
         queries, grads = stacked(q_ref, g), stacked(do_ref, g)
         gs_0, gs_2 = split(lower, gs_ref[g, 0:block])
         w_0, _ = split(lower, p_ref[g, 0:block])
@@ -194,22 +198,31 @@
             dq_ref[:, heads] = dq[h * block : (h + 1) * block].astype(dq_ref.dtype)
 
 
-def prep_kernel(seg_hbm, k_hbm, v_hbm, own_ref, seg_ref, sems):
+def bundle_kernel(seg_hbm, k_hbm, own_ref, seg_ref, sems):
     block = k_hbm.shape[0]
     copies = [
         pltpu.make_async_copy(seg_hbm, seg_ref, sems.at[0]),
         pltpu.make_async_copy(k_hbm, own_ref.at[0:block], sems.at[1]),
-        pltpu.make_async_copy(v_hbm, own_ref.at[block : 2 * block], sems.at[2]),
     ]
     for copy in copies:
         copy.start()
-    tail = slice(2 * block, 2 * block + SEG_ROWS)
+    tail = slice(block, block + SEG_ROWS)
     own_ref[tail, block:] = jnp.zeros((SEG_ROWS, own_ref.shape[1] - block), BF16)
     copies[0].wait()
     ids = jnp.broadcast_to(seg_ref[...].astype(F32), (SEG_ROWS, block))
     own_ref[tail, 0:block] = ids.astype(BF16)
-    for copy in copies[1:]:
-        copy.wait()
+    copies[1].wait()
+
+
+def pick_kernel(colours, own_ref, *rest):
+    moved_refs, (_, out_ref, crossing_ref) = rest[:colours], rest[colours:]
+    chip, core = lax.axis_index("ctx") // 2, lax.rem(lax.axis_index("ctx"), 2)
+    colour = lax.rem(chip + colours - 1, colours)
+    picked = moved_refs[0][...]
+    for i in range(1, colours):
+        picked = jnp.where(colour == colours - 1 - i, moved_refs[i][...], picked)
+    out_ref[...] = picked
+    crossing_ref[...] = jnp.where(core == 0, own_ref[...], picked)
 
 
 def merge_kernel(d2_ref, dk1_ref, dv1_ref, out_ref):
@@ -316,42 +329,69 @@
     capacity = max(2, 2 * pieces // n_dp)
     piece_len = block // pieces
     column = lax.axis_index("ctx")
-    own = pl.pallas_call(
-        prep_kernel,
-        out_shape=jax.ShapeDtypeStruct((2 * block + SEG_ROWS, kv_width), BF16),
-        in_specs=[HBM] * 3,
+    keys = pl.pallas_call(
+        bundle_kernel,
+        out_shape=jax.ShapeDtypeStruct((block + SEG_ROWS, kv_width), BF16),
+        in_specs=[HBM] * 2,
         out_specs=VMEM,
-        scratch_shapes=[pltpu.VMEM((1, block), jnp.int32), pltpu.SemaphoreType.DMA((3,))],
+        scratch_shapes=[pltpu.VMEM((1, block), jnp.int32), pltpu.SemaphoreType.DMA((2,))],
         compiler_params=params(),
         cost_estimate=cost(0, 1 << 19),
         name="bundle",
-    )(*pinned(segment_ids, key_rows[0], value_rows[0]))
-    moved = from_chip(own, 3)
-    colour = lax.rem(column // 2 + 2, 3)
-    far = jnp.where(colour == 2, moved[2], jnp.where(colour == 1, moved[1], moved[0]))
-    beside = swap(own)
-    near = jnp.where(lax.rem(column, 2) == 0, swap(far), beside)
-
-    pairs = 2 * block * block * GROUP * heads * HEAD_DIM
+    )(*pinned(segment_ids, key_rows[0]))
+    values = value_rows[0]
+    moved_keys, moved_values = from_chip(keys, 3), from_chip(values, 2)
+
     turned = jax.ShapeDtypeStruct((heads, HEAD_DIM, GROUP * block), BF16)
     product = jax.ShapeDtypeStruct((heads, block, GROUP * block), F32)
-    plan, turned_query, turned_grad, own_scores, own_terms = pl.pallas_call(
+    plan, turned_query, turned_grad, own_scores, own_terms, query, grad, own_values = pl.pallas_call(
         ahead_kernel,
         out_shape=[
-            jax.ShapeDtypeStruct(home_rows.shape, jnp.int32), turned, turned, product, product
+            jax.ShapeDtypeStruct(home_rows.shape, jnp.int32), turned, turned, product, product,
+            jax.ShapeDtypeStruct(query.shape, BF16), jax.ShapeDtypeStruct(grad.shape, BF16),
+            jax.ShapeDtypeStruct(values.shape, BF16),
         ],
-        in_specs=[VMEM] * 4,
-        out_specs=[VMEM] * 5,
-        compiler_params=params(),
-        cost_estimate=cost(2 * pairs, 4 << 20),
+        in_specs=[HBM] * 4 + [VMEM],
+        out_specs=[VMEM] * 8,
+        scratch_shapes=[pltpu.SemaphoreType.DMA((4,))],
+        compiler_params=params(),
+        cost_estimate=cost(0, 0),
         name="ahead",
-    )(home_rows, query, grad, own)
-    outs = pl.pallas_call(
-        functools.partial(fwd_kernel, n_dp),
-        out_shape=[jax.ShapeDtypeStruct((heads, 2 * block, GROUP * block), BF16)]
-        + [jax.ShapeDtypeStruct((capacity, piece_len, width), BF16)] * n_dp,
-        in_specs=[HBM] + [VMEM] * 5,
-        out_specs=[VMEM] * (1 + n_dp),
+    )(*pinned(home_rows, query, grad, values), keys)
+    far_keys, crossing = pl.pallas_call(
+        functools.partial(pick_kernel, len(moved_keys)),
+        out_shape=[jax.ShapeDtypeStruct(keys.shape, BF16)] * 2,
+        in_specs=[VMEM] * (1 + len(moved_keys)) + [HBM],
+        out_specs=[VMEM] * 2,
+        compiler_params=params(),
+        cost_estimate=cost(0, 0),
+        name="pick_keys",
+    )(keys, *moved_keys[::-1], plan)
+    near_keys = swap(crossing)
+    weights = pl.pallas_call(
+        weights_kernel,
+        out_shape=jax.ShapeDtypeStruct((heads, 2 * block, GROUP * block), BF16),
+        in_specs=[VMEM] * 5,
+        out_specs=VMEM,
+        compiler_params=params(),
+        cost_estimate=cost(0, 0),
+        name="weights",
+    )(turned_query, own_scores, keys, far_keys, near_keys)
+    far_values, crossing = pl.pallas_call(
+        functools.partial(pick_kernel, len(moved_values)),
+        out_shape=[jax.ShapeDtypeStruct(values.shape, BF16)] * 2,
+        in_specs=[VMEM] * (1 + len(moved_values)) + [HBM],
+        out_specs=[VMEM] * 2,
+        compiler_params=params(),
+        cost_estimate=cost(0, 0),
+        name="pick_values",
+    )(own_values, *moved_values[::-1], plan)
+    near_values = swap(crossing)
+    sends = pl.pallas_call(
+        functools.partial(attend_kernel, n_dp),
+        out_shape=[jax.ShapeDtypeStruct((capacity, piece_len, width), BF16)] * n_dp,
+        in_specs=[HBM] + [VMEM] * 4,
+        out_specs=[VMEM] * n_dp,
         scratch_shapes=[
             pltpu.VMEM((pieces + 1, piece_len, width), BF16),
             pltpu.SMEM((n_dp,), jnp.int32),
@@ -360,10 +400,9 @@
             pltpu.SemaphoreType.DMA,
         ],
         compiler_params=params(),
-        cost_estimate=cost(6 * pairs, 4 << 20),
+        cost_estimate=cost(0, 0),
         name="attend",
-    )(plan, turned_query, own_scores, own, far, near)
-    weights, sends = outs[0], outs[1:]
+    )(plan, weights, own_values, far_values, near_values)
     arrived = [exchange(sends[k], k) for k in range(n_dp - 1, 0, -1)] + [sends[0]]
     terms = jax.ShapeDtypeStruct((2 * block, kv_width), BF16)
     half = jax.ShapeDtypeStruct((block, kv_width), BF16)
@@ -376,7 +415,7 @@
         compiler_params=params(),
         cost_estimate=cost(0, 0),
         name="sent_terms",
-    )(query, grad, turned_grad, own_terms, own, far, near, weights)
+    )(query, grad, turned_grad, own_terms, own_values, far_values, near_values, weights)
     dq, d0, after_kept = pl.pallas_call(
         kept_kernel,
         out_shape=[
@@ -389,7 +428,7 @@
         compiler_params=params(),
         cost_estimate=cost(1073741824, 0),
         name="kept_terms",
-    )(query, grad, own, far, near, weights, score_grads)
+    )(query, grad, keys, far_keys, near_keys, weights, score_grads)
     dk1_in, dv1_in = swap(dk1), swap(dv1)
     d2_sum = pl.pallas_call(
         merge_kernel,

time: 31.9 us -> 30.3 us (0.950)
  waiting for transfers between devices: 10.9 us -> 7.52 us
  starting transfers between devices: 9.99 us -> 11.4 us
  Pallas kernels: 9.13 us -> 10.2 us
  local copies, waits for them, and re-layouts: 0.64 us -> 0.01 us
    ppermute x5 -> x7, waiting for transfers between devices: 6.37 us -> 2.92 us  [from_chip(): lax.ppermute(value, 'ctx', pairs(colour))]
    ppermute x5 -> x7, starting transfers between devices: 5.79 us -> 7.17 us  [from_chip(): lax.ppermute(value, 'ctx', pairs(colour))]
    pallas_call x1, Pallas kernels: 0.49 us -> 1.79 us  [on_device(): pl.pallas_call(ahead_kernel, out_shape=[jax.ShapeDtypeStruct(home_rows.sh...]
    unnamed x6 -> x2, local copies, waits for them, and re-layouts: 0.64 us -> 0.01 us
    pallas_call x2 -> x5, Pallas kernels: 3.11 us -> 2.85 us  [the longest x1 1.07 us: on_device(): pl.pallas_call(weights_kernel, out_shape=jax.ShapeDtypeStruct((heads, 2 *...]
  transfers between devices with their start and end apart: 12 -> 14, of which waited for: 6 -> 7; matrix products, arithmetic and copies ran while one was open for 0% -> 0% of each run, Pallas kernels for 16% -> 25%
where the time goes in v6:
time: 30.3 us; the launch traced here: 29.9 us
  starting transfers between devices  11.4 us (38%)
  Pallas kernels  10.2 us (34%)
  waiting for transfers between devices  7.52 us (25%)
  between operations  0.75 us (2%)
    ppermute x7, starting transfers between devices, from_chip(): lax.ppermute(value, 'ctx', pairs(colour))  7.17 us
    ppermute x3, waiting for transfers between devices, exchange(): return lax.ppermute(value, 'dp', pairs)  4.2 us
    ppermute x3, starting transfers between devices, exchange(): return lax.ppermute(value, 'dp', pairs)  3.55 us
    ppermute x7, waiting for transfers between devices, from_chip(): lax.ppermute(value, 'ctx', pairs(colour))  2.92 us
    pallas_call x1, Pallas kernels, on_device(): pl.pallas_call(sent_kernel, out_shape=[jax.ShapeDtypeStruct(weights.shape...  2.07 us
    pallas_call x1, Pallas kernels, on_device(): pl.pallas_call(ahead_kernel, out_shape=[jax.ShapeDtypeStruct(home_rows.sh...  1.79 us
    pallas_call x1, Pallas kernels, on_device(): pl.pallas_call(kept_kernel, out_shape=[jax.ShapeDtypeStruct((block, width...  1.65 us
    pallas_call x1, Pallas kernels, on_device(): pl.pallas_call(weights_kernel, out_shape=jax.ShapeDtypeStruct((heads, 2 *...  1.07 us
  transfers between devices with their start and end apart: 14, of which 7 were waited for; matrix products, arithmetic and copies ran while one was open for 0% of the time, Pallas kernels for 25%

profile of v6, /device:TPU:0, one launch (start us, length us, event | category | flops | bytes accessed | tf_op | source)
XLA Modules:
  0.0 29.9 jit_solution(9862897637525309128)
XLA Ops:
  0.6 0.0 copy-start
  0.6 1.0 %bundle.1.key_ref.own_ref = bf16[144,512]{1,0:T(8,128)(2,1)S(1)} custom-call(s32[1,128]{1,0:T(1,128)} %seg_hbm.1, bf16[128,512]{1,0:T(8,128)(2,1)} %bitcast.12), custom_call_target="tpu_custom_call" | custom-call | bytes 524288 | tf_op jit(solution)/shard_map/bundle/pallas_call | solution.py:332
  1.6 3.1 %collective-permute-start.2 = (bf16[144,512]{1,0:T(8,128)(2,1)S(1)}, bf16[144,512]{1,0:T(8,128)(2,1)S(1)}, u32[]{:S(2)}, u32[]{:S(2)}) collective-permute-start(bf16[144,512]{1,0:T(8,128)(2,1)S(1)} %bundle.1.key_ref.own_ref), channel_id=1, source_target_pairs={{0,2},{1,3},{2,0},{3,1},{4,5},{5,4},{6,7},{7,6},{8,10},{9,11},{10,... | collective-permute-start | bytes 442376 | tf_op jit(solution)/shard_map/ppermute | solution.py:310
  4.7 0.0 collective-permute-start.1
  4.7 0.5 %collective-permute-start = (bf16[144,512]{1,0:T(8,128)(2,1)S(1)}, bf16[144,512]{1,0:T(8,128)(2,1)S(1)}, u32[]{:S(2)}, u32[]{:S(2)}) collective-permute-start(bf16[144,512]{1,0:T(8,128)(2,1)S(1)} %bundle.1.key_ref.own_ref), channel_id=1, source_target_pairs={{0,1},{1,0},{2,3},{3,2},{4,6},{5,7},{6,4},{7,5},{8,9},{9,8},{10,11... | collective-permute-start | bytes 442376 | tf_op jit(solution)/shard_map/ppermute | solution.py:310
  5.2 1.3 %collective-permute-start.5 = (bf16[128,512]{1,0:T(8,128)(2,1)S(1)}, bf16[128,512]{1,0:T(8,128)(2,1)S(1)}, u32[]{:S(2)}, u32[]{:S(2)}) collective-permute-start(bf16[128,512]{1,0:T(8,128)(2,1)S(1)} %bitcast.10), channel_id=1, source_target_pairs={{0,2},{1,3},{2,0},{3,1},{4,6},{5,7},{6,4},{7,5},{8,10},{9,11},{10,... | collective-permute-start | bytes 393224 | tf_op jit(solution)/shard_map/ppermute | solution.py:310
  6.5 0.1 collective-permute-start.4
  6.6 1.8 %ahead.1 = (s32[1,16]{1,0:T(1,128)S(1)}, bf16[4,128,512]{2,1,0:T(8,128)(2,1)S(1)}, bf16[4,128,512]{2,1,0:T(8,128)(2,1)S(1)}, f32[4,128,512]{2,1,0:T(8,128)S(1)},...) custom-call(s32[1,16]{1,0:T(1,128)} %home_hbm.1, ...), custom_call_target="tpu_custom_call" | custom-call | tf_op jit(solution)/shard_map/ahead/pallas_call | solution.py:347
  8.4 0.8 %collective-permute-done.2.rest_2_ = bf16[144,512]{1,0:T(8,128)(2,1)S(1)} collective-permute-done((bf16[144,512]{1,0:T(8,128)(2,1)S(1)}, bf16[144,512]{1,0:T(8,128)(2,1)S(1)}, u32[]{:S(2)}, u32[]{:S(2)}) %collective-permute-start.2) | collective-permute-done | bytes 147488 | tf_op jit(solution)/shard_map/ppermute | solution.py:310
  9.3 0.1 collective-permute-start.3
  9.4 2.0 %collective-permute-done.5.rest_1_ = bf16[128,512]{1,0:T(8,128)(2,1)S(1)} collective-permute-done((bf16[128,512]{1,0:T(8,128)(2,1)S(1)}, bf16[128,512]{1,0:T(8,128)(2,1)S(1)}, u32[]{:S(2)}, u32[]{:S(2)}) %collective-permute-start.5) | collective-permute-done | bytes 131104 | tf_op jit(solution)/shard_map/ppermute | solution.py:310
  11.4 0.0 collective-permute-done.4.rest_0_
  11.4 0.1 collective-permute-start.6
  11.5 1.1 %weights.1.p_ref = bf16[4,256,512]{2,1,0:T(8,128)(2,1)S(1)} custom-call(bf16[4,128,512]{2,1,0:T(8,128)(2,1)S(1)} %get-tuple-element.31.qt_ref, f32[4,128,512]{2,1,0:T(8,128)S(1)} %get-tuple-element.32.s0_ref, bf16[144,512]{1,0:T(8,128)(2,1)S(1)} %bundle.1.key_ref.own_ref, bf16[144,512]{1,0:T(8,128)(2,1)S(1)} %get-tuple-element.33.far_ref, ...), custom_call_target="tpu_custom_call" | custom-call | tf_op jit(solution)/shard_map/weights/pallas_call | solution.py:371
  12.6 0.2 collective-permute-done.6.near_ref
  12.8 0.7 %attend.1 = (bf16[8,8,2048]{2,1,0:T(8,128)(2,1)S(1)}, bf16[8,8,2048]{2,1,0:T(8,128)(2,1)S(1)}, bf16[8,8,2048]{2,1,0:T(8,128)(2,1)S(1)}, bf16[8,8,2048]{2,1,0:T(8,128)(2,1)S(1)}) custom-call(s32[1,16]{1,0:T(1,128)S(1)} %get-tuple-element.30.rest_3_.rest_2_.home_hbm, bf16[4,256,512]{2,1,0:T(8,128)(2,1)S(1)} %weights.1.p_ref, ...), custom_call_target="tpu_custom_call" | custom-call | tf_op jit(solution)/shard_map/attend/pallas_call | solution.py:390
  13.6 2.7 %collective-permute-start.13 = (bf16[8,8,2048]{2,1,0:T(8,128)(2,1)S(1)}, bf16[8,8,2048]{2,1,0:T(8,128)(2,1)S(1)}, u32[]{:S(2)}, u32[]{:S(2)}) collective-permute-start(bf16[8,8,2048]{2,1,0:T(8,128)(2,1)S(1)} %get-tuple-element.50), channel_id=1, source_target_pairs={{0,24},{8,16},{16,8},{24,0},{1,25},{9,17},{17,9},{25,1},{2,26},{10... | collective-permute-start | bytes 786440 | tf_op jit(solution)/shard_map/ppermute | solution.py:319
  16.2 2.1 %sent_terms.1 = (bf16[4,256,512]{2,1,0:T(8,128)(2,1)S(1)}, bf16[256,512]{1,0:T(8,128)(2,1)S(1)}, bf16[128,512]{1,0:T(8,128)(2,1)S(1)}, bf16[128,512]{1,0:T(8,128)(2,1)S(1)}) custom-call(bf16[128,2048]{1,0:T(8,128)(2,1)S(1)} %get-tuple-element.40.q_ref, bf16[128,2048]{1,0:T(8,128)(2,1)S(1)} %get-tuple-element.41.do_ref, ...), custom_call_target="tpu_custom_call" | custom-call | tf_op jit(solution)/shard_map/sent_terms/pallas_call | solution.py:410
  18.3 0.1 collective-permute-start.9
  18.4 0.5 %collective-permute-start.10 = (bf16[128,512]{1,0:T(8,128)(2,1)S(1)}, bf16[128,512]{1,0:T(8,128)(2,1)S(1)}, u32[]{:S(2)}, u32[]{:S(2)}) collective-permute-start(bf16[128,512]{1,0:T(8,128)(2,1)S(1)} %get-tuple-element.46), channel_id=1, source_target_pairs={{0,1},{1,0},{2,3},{3,2},{4,5},{5,4},{6,7},{7,6},{8,9},{9,8},{10,11... | collective-permute-start | bytes 393224 | tf_op jit(solution)/shard_map/ppermute | solution.py:296
  18.9 0.5 %collective-permute-start.7 = (bf16[8,8,2048]{2,1,0:T(8,128)(2,1)S(1)}, bf16[8,8,2048]{2,1,0:T(8,128)(2,1)S(1)}, u32[]{:S(2)}, u32[]{:S(2)}) collective-permute-start(bf16[8,8,2048]{2,1,0:T(8,128)(2,1)S(1)} %get-tuple-element.38), channel_id=1, source_target_pairs={{0,16},{8,24},{16,0},{24,8},{1,17},{9,25},{17,1},{25,9},{2,18},{10... | collective-permute-start | bytes 786440 | tf_op jit(solution)/shard_map/ppermute | solution.py:319
  19.4 0.4 %collective-permute-start.8 = (bf16[8,8,2048]{2,1,0:T(8,128)(2,1)S(1)}, bf16[8,8,2048]{2,1,0:T(8,128)(2,1)S(1)}, u32[]{:S(2)}, u32[]{:S(2)}) collective-permute-start(bf16[8,8,2048]{2,1,0:T(8,128)(2,1)S(1)} %get-tuple-element.39), channel_id=1, source_target_pairs={{0,8},{8,0},{16,24},{24,16},{1,9},{9,1},{17,25},{25,17},{2,10},{10... | collective-permute-start | bytes 786440 | tf_op jit(solution)/shard_map/ppermute | solution.py:319
  19.8 0.1 collective-permute-done.10.dv1_ref.rest_5_
  19.9 0.1 merge.1
  20.0 2.2 %collective-permute-start.12 = (bf16[256,512]{1,0:T(8,128)(2,1)S(1)}, bf16[256,512]{1,0:T(8,128)(2,1)S(1)}, u32[]{:S(2)}, u32[]{:S(2)}) collective-permute-start(bf16[256,512]{1,0:T(8,128)(2,1)S(1)} %merge.1), channel_id=1, source_target_pairs={{0,2},{1,3},{2,0},{3,1},{4,6},{5,7},{6,4},{7,5},{8,10},{9,11},{10,... | collective-permute-start | bytes 786440 | tf_op jit(solution)/shard_map/ppermute | solution.py:310
  22.2 0.0 collective-permute-start.11
  22.2 1.6 %kept_terms.1 = (bf16[128,2048]{1,0:T(8,128)(2,1)}, f32[256,512]{1,0:T(8,128)S(1)}, f32[8,128]{1,0:T(8,128)S(1)}) custom-call(bf16[128,2048]{1,0:T(8,128)(2,1)S(1)} %get-tuple-element.40.q_ref, bf16[128,2048]{1,0:T(8,128)(2,1)S(1)} %get-tuple-element.41.do_ref, bf16[144,512]{1,0:T(8,128)(2,1)S(1)} %bundle.1.key_ref.own_ref, ...), custom_call_target="tpu_custom_call" | custom-call | flops 1073741824 | tf_op jit(solution)/shard_map/kept_terms/pallas_call | solution.py:419
  23.9 0.8 %place_early.1.rest_7_ = bf16[1,1,4,8,8,2048]{5,4,3,2,1,0:T(8,128)(2,1)} custom-call(f32[8,128]{1,0:T(8,128)S(1)} %get-tuple-element.49.kept_ref, bf16[8,8,2048]{2,1,0:T(8,128)(2,1)S(1)} %collective-permute-done.13.far_ref, bf16[8,8,2048]{2,1,0:T(8,128)(2,1)S(1)} %get-tuple-element.51.own_ref), custom_call_target="tpu_custom_call" | custom-call | flops 2147483648 | tf_op jit(solution)/shard_map/place_early/pallas_call | solution.py:444
  24.7 3.9 %collective-permute-done.7.rest_0_ = bf16[8,8,2048]{2,1,0:T(8,128)(2,1)S(1)} collective-permute-done((bf16[8,8,2048]{2,1,0:T(8,128)(2,1)S(1)}, bf16[8,8,2048]{2,1,0:T(8,128)(2,1)S(1)}, u32[]{:S(2)}, u32[]{:S(2)}) %collective-permute-start.7) | collective-permute-done | bytes 262176 | tf_op jit(solution)/shard_map/ppermute | solution.py:319
  28.6 0.3 collective-permute-done.8.rest_1_
  28.9 0.1 collective-permute-done.12.rest_3_
  29.0 0.9 %finish.1 = (bf16[1,1,4,8,8,2048]{5,4,3,2,1,0:T(8,128)(2,1)}, bf16[128,512]{1,0:T(8,128)(2,1)}, bf16[128,512]{1,0:T(8,128)(2,1)}) custom-call(bf16[8,8,2048]{2,1,0:T(8,128)(2,1)S(1)} %collective-permute-done.7.rest_0_, bf16[8,8,2048]{2,1,0:T(8,128)(2,1)S(1)} %collective-permute-done.8.rest_1_, ...), custom_call_target="tpu_custom_call", output_to_operand_aliasing={{0}: (7, {})} | custom-call | bytes 1048576 | tf_op jit(solution)/shard_map/finish/pallas_call | solution.py:454
  (9 shorter events, 0.1 us)
Async XLA Ops:
  0.6 4.6 %copy-start = (bf16[1,128,512]{2,1,0:T(8,128)(2,1)S(1)}, bf16[1,128,512]{2,1,0:T(8,128)(2,1)}, u32[]{:S(2)}) copy-start(bf16[1,128,512]{2,1,0:T(8,128)(2,1)} %param.8) | copy-start | bytes 393220
  1.6 7.6 %collective-permute-start.2 = (bf16[144,512]{1,0:T(8,128)(2,1)S(1)}, bf16[144,512]{1,0:T(8,128)(2,1)S(1)}, u32[]{:S(2)}, u32[]{:S(2)}) collective-permute-start(bf16[144,512]{1,0:T(8,128)(2,1)S(1)} %bundle.1.key_ref.own_ref), channel_id=1, source_target_pairs={{0,2},{1,3},{2,0},{3,1},{4,5},{5,4},{6,7},{7,6},{8,10},{9,11},{10,... | collective-permute-start | bytes 442376 | tf_op jit(solution)/shard_map/ppermute | solution.py:310
  4.7 4.5 %collective-permute-start.1 = (bf16[144,512]{1,0:T(8,128)(2,1)S(1)}, bf16[144,512]{1,0:T(8,128)(2,1)S(1)}, u32[]{:S(2)}, u32[]{:S(2)}) collective-permute-start(bf16[144,512]{1,0:T(8,128)(2,1)S(1)} %bundle.1.key_ref.own_ref), channel_id=1, source_target_pairs={{0,1},{1,0},{2,4},{3,5},{4,2},{5,3},{6,7},{7,6},{8,9},{9,8},{10,12... | collective-permute-start | bytes 442376 | tf_op jit(solution)/shard_map/ppermute | solution.py:310
  4.7 4.5 %collective-permute-start = (bf16[144,512]{1,0:T(8,128)(2,1)S(1)}, bf16[144,512]{1,0:T(8,128)(2,1)S(1)}, u32[]{:S(2)}, u32[]{:S(2)}) collective-permute-start(bf16[144,512]{1,0:T(8,128)(2,1)S(1)} %bundle.1.key_ref.own_ref), channel_id=1, source_target_pairs={{0,1},{1,0},{2,3},{3,2},{4,6},{5,7},{6,4},{7,5},{8,9},{9,8},{10,11... | collective-permute-start | bytes 442376 | tf_op jit(solution)/shard_map/ppermute | solution.py:310
  5.2 6.1 %collective-permute-start.5 = (bf16[128,512]{1,0:T(8,128)(2,1)S(1)}, bf16[128,512]{1,0:T(8,128)(2,1)S(1)}, u32[]{:S(2)}, u32[]{:S(2)}) collective-permute-start(bf16[128,512]{1,0:T(8,128)(2,1)S(1)} %bitcast.10), channel_id=1, source_target_pairs={{0,2},{1,3},{2,0},{3,1},{4,6},{5,7},{6,4},{7,5},{8,10},{9,11},{10,... | collective-permute-start | bytes 393224 | tf_op jit(solution)/shard_map/ppermute | solution.py:310
  6.5 4.8 %collective-permute-start.4 = (bf16[128,512]{1,0:T(8,128)(2,1)S(1)}, bf16[128,512]{1,0:T(8,128)(2,1)S(1)}, u32[]{:S(2)}, u32[]{:S(2)}) collective-permute-start(bf16[128,512]{1,0:T(8,128)(2,1)S(1)} %bitcast.11), channel_id=1, source_target_pairs={{0,1},{1,0},{2,4},{3,5},{4,2},{5,3},{6,7},{7,6},{8,9},{9,8},{10,12... | collective-permute-start | bytes 393224 | tf_op jit(solution)/shard_map/ppermute | solution.py:310
  9.3 2.2 %collective-permute-start.3 = (bf16[144,512]{1,0:T(8,128)(2,1)S(1)}, bf16[144,512]{1,0:T(8,128)(2,1)S(1)}, u32[]{:S(2)}, u32[]{:S(2)}) collective-permute-start(bf16[144,512]{1,0:T(8,128)(2,1)S(1)} %get-tuple-element.34), channel_id=1, source_target_pairs={{0,1},{1,0},{2,3},{3,2},{4,5},{5,4},{6,7},{7,6},{8,9},{9,8},{10,11... | collective-permute-start | bytes 442376 | tf_op jit(solution)/shard_map/ppermute | solution.py:296
  11.4 1.4 %collective-permute-start.6 = (bf16[128,512]{1,0:T(8,128)(2,1)S(1)}, bf16[128,512]{1,0:T(8,128)(2,1)S(1)}, u32[]{:S(2)}, u32[]{:S(2)}) collective-permute-start(bf16[128,512]{1,0:T(8,128)(2,1)S(1)} %get-tuple-element.37), channel_id=1, source_target_pairs={{0,1},{1,0},{2,3},{3,2},{4,5},{5,4},{6,7},{7,6},{8,9},{9,8},{10,11... | collective-permute-start | bytes 393224 | tf_op jit(solution)/shard_map/ppermute | solution.py:296
  13.6 10.3 %collective-permute-start.13 = (bf16[8,8,2048]{2,1,0:T(8,128)(2,1)S(1)}, bf16[8,8,2048]{2,1,0:T(8,128)(2,1)S(1)}, u32[]{:S(2)}, u32[]{:S(2)}) collective-permute-start(bf16[8,8,2048]{2,1,0:T(8,128)(2,1)S(1)} %get-tuple-element.50), channel_id=1, source_target_pairs={{0,24},{8,16},{16,8},{24,0},{1,25},{9,17},{17,9},{25,1},{2,26},{10... | collective-permute-start | bytes 786440 | tf_op jit(solution)/shard_map/ppermute | solution.py:319
  18.3 1.5 %collective-permute-start.9 = (bf16[128,512]{1,0:T(8,128)(2,1)S(1)}, bf16[128,512]{1,0:T(8,128)(2,1)S(1)}, u32[]{:S(2)}, u32[]{:S(2)}) collective-permute-start(bf16[128,512]{1,0:T(8,128)(2,1)S(1)} %get-tuple-element.45), channel_id=1, source_target_pairs={{0,1},{1,0},{2,3},{3,2},{4,5},{5,4},{6,7},{7,6},{8,9},{9,8},{10,11... | collective-permute-start | bytes 393224 | tf_op jit(solution)/shard_map/ppermute | solution.py:296
  18.4 1.5 %collective-permute-start.10 = (bf16[128,512]{1,0:T(8,128)(2,1)S(1)}, bf16[128,512]{1,0:T(8,128)(2,1)S(1)}, u32[]{:S(2)}, u32[]{:S(2)}) collective-permute-start(bf16[128,512]{1,0:T(8,128)(2,1)S(1)} %get-tuple-element.46), channel_id=1, source_target_pairs={{0,1},{1,0},{2,3},{3,2},{4,5},{5,4},{6,7},{7,6},{8,9},{9,8},{10,11... | collective-permute-start | bytes 393224 | tf_op jit(solution)/shard_map/ppermute | solution.py:296
  18.9 9.7 %collective-permute-start.7 = (bf16[8,8,2048]{2,1,0:T(8,128)(2,1)S(1)}, bf16[8,8,2048]{2,1,0:T(8,128)(2,1)S(1)}, u32[]{:S(2)}, u32[]{:S(2)}) collective-permute-start(bf16[8,8,2048]{2,1,0:T(8,128)(2,1)S(1)} %get-tuple-element.38), channel_id=1, source_target_pairs={{0,16},{8,24},{16,0},{24,8},{1,17},{9,25},{17,1},{25,9},{2,18},{10... | collective-permute-start | bytes 786440 | tf_op jit(solution)/shard_map/ppermute | solution.py:319
  19.4 9.5 %collective-permute-start.8 = (bf16[8,8,2048]{2,1,0:T(8,128)(2,1)S(1)}, bf16[8,8,2048]{2,1,0:T(8,128)(2,1)S(1)}, u32[]{:S(2)}, u32[]{:S(2)}) collective-permute-start(bf16[8,8,2048]{2,1,0:T(8,128)(2,1)S(1)} %get-tuple-element.39), channel_id=1, source_target_pairs={{0,8},{8,0},{16,24},{24,16},{1,9},{9,1},{17,25},{25,17},{2,10},{10... | collective-permute-start | bytes 786440 | tf_op jit(solution)/shard_map/ppermute | solution.py:319
  20.0 8.9 %collective-permute-start.12 = (bf16[256,512]{1,0:T(8,128)(2,1)S(1)}, bf16[256,512]{1,0:T(8,128)(2,1)S(1)}, u32[]{:S(2)}, u32[]{:S(2)}) collective-permute-start(bf16[256,512]{1,0:T(8,128)(2,1)S(1)} %merge.1), channel_id=1, source_target_pairs={{0,2},{1,3},{2,0},{3,1},{4,6},{5,7},{6,4},{7,5},{8,10},{9,11},{10,... | collective-permute-start | bytes 786440 | tf_op jit(solution)/shard_map/ppermute | solution.py:310
  22.2 6.8 %collective-permute-start.11 = (bf16[256,512]{1,0:T(8,128)(2,1)S(1)}, bf16[256,512]{1,0:T(8,128)(2,1)S(1)}, u32[]{:S(2)}, u32[]{:S(2)}) collective-permute-start(bf16[256,512]{1,0:T(8,128)(2,1)S(1)} %merge.1), channel_id=1, source_target_pairs={{0,1},{1,0},{2,4},{3,5},{4,2},{5,3},{6,7},{7,6},{8,9},{9,8},{10,12... | collective-permute-start | bytes 786440 | tf_op jit(solution)/shard_map/ppermute | solution.py:310

commit v7 on v6

--- a/solution.py
+++ b/solution.py
@@ -46,14 +46,18 @@
     return home ^ row if count & (count - 1) == 0 else lax.rem(home - row + count, count)
 
 
-def weights_kernel(qt_ref, s0_ref, own_ref, far_ref, near_ref, p_ref):
+def weights_kernel(qt_ref, s0_ref, own_ref, far_ref, near_ref, own_ids_ref, far_ids_ref, p_ref):
     block = s0_ref.shape[1]
     column = lax.axis_index("ctx")
 
-    def seg_of(ref):
-        return ref[block : block + SEG_ROWS, 0:block].astype(F32)[0:1]
-
-    seg_own, seg_near, seg_far = seg_of(own_ref), seg_of(near_ref), seg_of(far_ref)
+    def seg_of(ref, core):
+        cols = slice(core * block, (core + 1) * block)
+        return ref[block : block + SEG_ROWS, cols].astype(F32)[0:1]
+
+    first_core = lax.rem(column, 2) == 0
+    seg_own = jnp.where(first_core, seg_of(own_ids_ref, 0), seg_of(own_ids_ref, 1))
+    seg_near = jnp.where(first_core, seg_of(far_ids_ref, 1), seg_of(own_ids_ref, 0))
+    seg_far = jnp.where(first_core, seg_of(far_ids_ref, 0), seg_of(far_ids_ref, 1))
     first = seg_own[:, 0:1]
     reach = jnp.where(column >= 1, jnp.sum((seg_near == first).astype(F32), axis=1, keepdims=True), 0.0)
     reach = reach + jnp.where(
@@ -89,7 +93,7 @@
     sends, (held, counts, filled, home_ref, sem) = rest[:n_dp], rest[n_dp:]
     fetch = pltpu.make_async_copy(home_hbm, home_ref, sem)
     fetch.start()
-    block = own_ref.shape[0]
+    block = near_ref.shape[0]
     row = lax.axis_index("dp")
     pieces = home_ref.shape[1]
     piece_len = block // pieces
@@ -130,17 +134,17 @@
 
 
 def ahead_kernel(
-    home_hbm, q_hbm, do_hbm, v_hbm, key_ref,
-    plan_ref, qt_ref, gt_ref, s0_ref, gw0_ref, q_ref, do_ref, v_ref, sems,
+    home_hbm, q_hbm, do_hbm, k_hbm, v_ref,
+    plan_ref, qt_ref, gt_ref, s0_ref, gw0_ref, q_ref, do_ref, key_ref, sems,
 ):
-    pairs = ((q_hbm, q_ref), (do_hbm, do_ref), (v_hbm, v_ref), (home_hbm, plan_ref))
+    pairs = ((q_hbm, q_ref), (k_hbm, key_ref), (do_hbm, do_ref), (home_hbm, plan_ref))
     copies = [pltpu.make_async_copy(*pair, sems.at[i]) for i, pair in enumerate(pairs)]
     for copy in copies:
         copy.start()
     block = q_ref.shape[0]
     for source, own_ref, turned, product, waits in (
-        (q_ref, key_ref, qt_ref, s0_ref, copies[:1]),
-        (do_ref, v_ref, gt_ref, gw0_ref, copies[1:]),
+        (q_ref, key_ref, qt_ref, s0_ref, copies[:2]),
+        (do_ref, v_ref, gt_ref, gw0_ref, copies[2:]),
     ):
         for copy in waits:
             copy.wait()
@@ -198,19 +202,23 @@
             dq_ref[:, heads] = dq[h * block : (h + 1) * block].astype(dq_ref.dtype)
 
 
-def bundle_kernel(seg_hbm, k_hbm, own_ref, seg_ref, sems):
-    block = k_hbm.shape[0]
+def bundle_kernel(seg_hbm, other_ref, v_hbm, own_ref, seg_ref, sems):
+    block = v_hbm.shape[0]
     copies = [
         pltpu.make_async_copy(seg_hbm, seg_ref, sems.at[0]),
-        pltpu.make_async_copy(k_hbm, own_ref.at[0:block], sems.at[1]),
+        pltpu.make_async_copy(v_hbm, own_ref.at[0:block], sems.at[1]),
     ]
     for copy in copies:
         copy.start()
     tail = slice(block, block + SEG_ROWS)
-    own_ref[tail, block:] = jnp.zeros((SEG_ROWS, own_ref.shape[1] - block), BF16)
+    own_ref[tail, 2 * block :] = jnp.zeros((SEG_ROWS, own_ref.shape[1] - 2 * block), BF16)
+    first_core = lax.rem(lax.axis_index("ctx"), 2) == 0
     copies[0].wait()
-    ids = jnp.broadcast_to(seg_ref[...].astype(F32), (SEG_ROWS, block))
-    own_ref[tail, 0:block] = ids.astype(BF16)
+    own_ids, other_ids = seg_ref[...].astype(F32), other_ref[...].astype(F32)
+    ids = (jnp.where(first_core, own_ids, other_ids), jnp.where(first_core, other_ids, own_ids))
+    for core in range(2):
+        cols = slice(core * block, (core + 1) * block)
+        own_ref[tail, cols] = jnp.broadcast_to(ids[core], (SEG_ROWS, block)).astype(BF16)
     copies[1].wait()
 
 
@@ -222,7 +230,10 @@
     for i in range(1, colours):
         picked = jnp.where(colour == colours - 1 - i, moved_refs[i][...], picked)
     out_ref[...] = picked
-    crossing_ref[...] = jnp.where(core == 0, own_ref[...], picked)
+    block = min(own_ref.shape[0], crossing_ref.shape[0])
+    crossing_ref[0:block] = jnp.where(core == 0, own_ref[0:block], picked[0:block])
+    if crossing_ref.shape[0] > block:
+        crossing_ref[block:] = jnp.zeros((crossing_ref.shape[0] - block, own_ref.shape[1]), BF16)
 
 
 def merge_kernel(d2_ref, dk1_ref, dv1_ref, out_ref):
@@ -329,27 +340,28 @@
     capacity = max(2, 2 * pieces // n_dp)
     piece_len = block // pieces
     column = lax.axis_index("ctx")
-    keys = pl.pallas_call(
+    keys = key_rows[0]
+    moved_keys = from_chip(keys, 3)
+    values = pl.pallas_call(
         bundle_kernel,
         out_shape=jax.ShapeDtypeStruct((block + SEG_ROWS, kv_width), BF16),
-        in_specs=[HBM] * 2,
+        in_specs=[HBM, VMEM, HBM],
         out_specs=VMEM,
         scratch_shapes=[pltpu.VMEM((1, block), jnp.int32), pltpu.SemaphoreType.DMA((2,))],
         compiler_params=params(),
-        cost_estimate=cost(0, 1 << 19),
+        cost_estimate=cost(0, 0),
         name="bundle",
-    )(*pinned(segment_ids, key_rows[0]))
-    values = value_rows[0]
-    moved_keys, moved_values = from_chip(keys, 3), from_chip(values, 2)
+    )(*pinned(segment_ids), swap(segment_ids), *pinned(value_rows[0]))
+    moved_values = from_chip(values, 2)
 
     turned = jax.ShapeDtypeStruct((heads, HEAD_DIM, GROUP * block), BF16)
     product = jax.ShapeDtypeStruct((heads, block, GROUP * block), F32)
-    plan, turned_query, turned_grad, own_scores, own_terms, query, grad, own_values = pl.pallas_call(
+    plan, turned_query, turned_grad, own_scores, own_terms, query, grad, own_keys = pl.pallas_call(
         ahead_kernel,
         out_shape=[
             jax.ShapeDtypeStruct(home_rows.shape, jnp.int32), turned, turned, product, product,
             jax.ShapeDtypeStruct(query.shape, BF16), jax.ShapeDtypeStruct(grad.shape, BF16),
-            jax.ShapeDtypeStruct(values.shape, BF16),
+            jax.ShapeDtypeStruct(keys.shape, BF16),
         ],
         in_specs=[HBM] * 4 + [VMEM],
         out_specs=[VMEM] * 8,
@@ -357,36 +369,40 @@
         compiler_params=params(),
         cost_estimate=cost(0, 0),
         name="ahead",
-    )(*pinned(home_rows, query, grad, values), keys)
+    )(*pinned(home_rows, query, grad, keys), values)
     far_keys, crossing = pl.pallas_call(
         functools.partial(pick_kernel, len(moved_keys)),
-        out_shape=[jax.ShapeDtypeStruct(keys.shape, BF16)] * 2,
+        out_shape=[
+            jax.ShapeDtypeStruct(keys.shape, BF16), jax.ShapeDtypeStruct(values.shape, BF16)
+        ],
         in_specs=[VMEM] * (1 + len(moved_keys)) + [HBM],
         out_specs=[VMEM] * 2,
         compiler_params=params(),
         cost_estimate=cost(0, 0),
         name="pick_keys",
-    )(keys, *moved_keys[::-1], plan)
+    )(own_keys, *moved_keys[::-1], plan)
     near_keys = swap(crossing)
+    far_values, crossing = pl.pallas_call(
+        functools.partial(pick_kernel, len(moved_values)),
+        out_shape=[
+            jax.ShapeDtypeStruct(values.shape, BF16), jax.ShapeDtypeStruct(keys.shape, BF16)
+        ],
+        in_specs=[VMEM] * (1 + len(moved_values)) + [HBM],
+        out_specs=[VMEM] * 2,
+        compiler_params=params(),
+        cost_estimate=cost(0, 0),
+        name="pick_values",
+    )(values, *moved_values[::-1], plan)
+    near_values = swap(crossing)
     weights = pl.pallas_call(
         weights_kernel,
         out_shape=jax.ShapeDtypeStruct((heads, 2 * block, GROUP * block), BF16),
-        in_specs=[VMEM] * 5,
+        in_specs=[VMEM] * 7,
         out_specs=VMEM,
         compiler_params=params(),
         cost_estimate=cost(0, 0),
         name="weights",
-    )(turned_query, own_scores, keys, far_keys, near_keys)
-    far_values, crossing = pl.pallas_call(
-        functools.partial(pick_kernel, len(moved_values)),
-        out_shape=[jax.ShapeDtypeStruct(values.shape, BF16)] * 2,
-        in_specs=[VMEM] * (1 + len(moved_values)) + [HBM],
-        out_specs=[VMEM] * 2,
-        compiler_params=params(),
-        cost_estimate=cost(0, 0),
-        name="pick_values",
-    )(own_values, *moved_values[::-1], plan)
-    near_values = swap(crossing)
+    )(turned_query, own_scores, own_keys, far_keys, near_keys, values, far_values)
     sends = pl.pallas_call(
         functools.partial(attend_kernel, n_dp),
         out_shape=[jax.ShapeDtypeStruct((capacity, piece_len, width), BF16)] * n_dp,
@@ -402,7 +418,7 @@
         compiler_params=params(),
         cost_estimate=cost(0, 0),
         name="attend",
-    )(plan, weights, own_values, far_values, near_values)
+    )(plan, weights, values, far_values, near_values)
     arrived = [exchange(sends[k], k) for k in range(n_dp - 1, 0, -1)] + [sends[0]]
     terms = jax.ShapeDtypeStruct((2 * block, kv_width), BF16)
     half = jax.ShapeDtypeStruct((block, kv_width), BF16)
@@ -415,7 +431,7 @@
         compiler_params=params(),
         cost_estimate=cost(0, 0),
         name="sent_terms",
-    )(query, grad, turned_grad, own_terms, own_values, far_values, near_values, weights)
+    )(query, grad, turned_grad, own_terms, values, far_values, near_values, weights)
     dq, d0, after_kept = pl.pallas_call(
         kept_kernel,
         out_shape=[
@@ -428,7 +444,7 @@
         compiler_params=params(),
         cost_estimate=cost(1073741824, 0),
         name="kept_terms",
-    )(query, grad, keys, far_keys, near_keys, weights, score_grads)
+    )(query, grad, own_keys, far_keys, near_keys, weights, score_grads)
     dk1_in, dv1_in = swap(dk1), swap(dv1)
     d2_sum = pl.pallas_call(
         merge_kernel,

time: 30.3 us -> 29.9 us (0.987)
  waiting for transfers between devices: 7.52 us -> 6.9 us
  starting transfers between devices: 11.4 us -> 11.9 us
    ppermute x7, waiting for transfers between devices: 2.92 us -> 2.05 us  [from_chip(): lax.ppermute(value, 'ctx', pairs(colour))]
    ppermute x4 -> x5, starting transfers between devices: 0.71 us -> 1.51 us  [swap(): return lax.ppermute(value, 'ctx', [(i, i ^ 1) for i in range(count)])]
    ppermute x7, starting transfers between devices: 7.17 us -> 6.82 us  [from_chip(): lax.ppermute(value, 'ctx', pairs(colour))]
    ppermute x3, waiting for transfers between devices: 4.2 us -> 4.52 us  [exchange(): return lax.ppermute(value, 'dp', pairs)]
  transfers between devices with their start and end apart: 14 -> 15, of which waited for: 7 -> 5; matrix products, arithmetic and copies ran while one was open for 0% -> 0% of each run, Pallas kernels for 25% -> 29%
where the time goes in v7:
time: 29.9 us; the launch traced here: 29.7 us
  starting transfers between devices  11.9 us (40%)
  Pallas kernels  10.2 us (34%)
  waiting for transfers between devices  6.9 us (23%)
  between operations  0.75 us (3%)
    ppermute x7, starting transfers between devices, from_chip(): lax.ppermute(value, 'ctx', pairs(colour))  6.82 us
    ppermute x3, waiting for transfers between devices, exchange(): return lax.ppermute(value, 'dp', pairs)  4.52 us
    ppermute x3, starting transfers between devices, exchange(): return lax.ppermute(value, 'dp', pairs)  3.56 us
    pallas_call x1, Pallas kernels, on_device(): pl.pallas_call(sent_kernel, out_shape=[jax.ShapeDtypeStruct(weights.shape...  2.07 us
    ppermute x7, waiting for transfers between devices, from_chip(): lax.ppermute(value, 'ctx', pairs(colour))  2.05 us
    pallas_call x1, Pallas kernels, on_device(): pl.pallas_call(ahead_kernel, out_shape=[jax.ShapeDtypeStruct(home_rows.sh...  1.81 us
    pallas_call x1, Pallas kernels, on_device(): pl.pallas_call(kept_kernel, out_shape=[jax.ShapeDtypeStruct((block, width...  1.67 us
    ppermute x5, starting transfers between devices, swap(): return lax.ppermute(value, 'ctx', [(i, i ^ 1) for i in range(count)])  1.51 us
  transfers between devices with their start and end apart: 15, of which 5 were waited for; matrix products, arithmetic and copies ran while one was open for 0% of the time, Pallas kernels for 29%

profile of v7, /device:TPU:0, one launch (start us, length us, event | category | flops | bytes accessed | tf_op | source)
XLA Modules:
  0.0 29.7 jit_solution(11089222591565368147)
XLA Ops:
  0.6 0.5 %collective-permute-start = (s32[1,128]{1,0:T(1,128)}, s32[1,128]{1,0:T(1,128)S(1)}, u32[]{:S(2)}, u32[]{:S(2)}) collective-permute-start(s32[1,128]{1,0:T(1,128)} %seg_hbm.1), channel_id=1, source_target_pairs={{0,1},{1,0},{2,3},{3,2},{4,5},{5,4},{6,7},{7,6},{8,9},{9,8},{10,11... | collective-permute-start | bytes 1544 | tf_op jit(solution)/shard_map/ppermute | solution.py:307
  1.1 2.6 %collective-permute-start.3 = (bf16[128,512]{1,0:T(8,128)(2,1)}, bf16[128,512]{1,0:T(8,128)(2,1)S(1)}, u32[]{:S(2)}, u32[]{:S(2)}) collective-permute-start(bf16[128,512]{1,0:T(8,128)(2,1)} %bitcast.9), channel_id=1, source_target_pairs={{0,2},{1,3},{2,0},{3,1},{4,5},{5,4},{6,7},{7,6},{8,10},{9,11},{10,... | collective-permute-start | bytes 393224 | tf_op jit(solution)/shard_map/ppermute | solution.py:321
  3.8 0.2 collective-permute-start.2
  4.0 0.3 %collective-permute-start.1 = (bf16[128,512]{1,0:T(8,128)(2,1)}, bf16[128,512]{1,0:T(8,128)(2,1)S(1)}, u32[]{:S(2)}, u32[]{:S(2)}) collective-permute-start(bf16[128,512]{1,0:T(8,128)(2,1)} %bitcast.11), channel_id=1, source_target_pairs={{0,1},{1,0},{2,3},{3,2},{4,6},{5,7},{6,4},{7,5},{8,9},{9,8},{10,11... | collective-permute-start | bytes 393224 | tf_op jit(solution)/shard_map/ppermute | solution.py:321
  4.3 0.0 collective-permute-done.other_ref
  4.3 0.9 %bundle.1.v_ref.own_ref.own_ids_ref = bf16[144,512]{1,0:T(8,128)(2,1)S(1)} custom-call(s32[1,128]{1,0:T(1,128)} %seg_hbm.1, s32[1,128]{1,0:T(1,128)S(1)} %collective-permute-done.other_ref, bf16[128,512]{1,0:T(8,128)(2,1)} %bitcast.13), custom_call_target="tpu_custom_call" | custom-call | tf_op jit(solution)/shard_map/bundle/pallas_call | solution.py:345
  5.3 1.6 %collective-permute-start.6 = (bf16[144,512]{1,0:T(8,128)(2,1)S(1)}, bf16[144,512]{1,0:T(8,128)(2,1)S(1)}, u32[]{:S(2)}, u32[]{:S(2)}) collective-permute-start(bf16[144,512]{1,0:T(8,128)(2,1)S(1)} %bundle.1.v_ref.own_ref.own_ids_ref), channel_id=1, source_target_pairs={{0,2},{1,3},{2,0},{3,1},{4,6},{5,7},{6,4},{7,5},{8,10},{9,11},{10,... | collective-permute-start | bytes 442376 | tf_op jit(solution)/shard_map/ppermute | solution.py:321
  6.8 0.2 collective-permute-start.5
  7.1 1.8 %ahead.1 = (s32[1,16]{1,0:T(1,128)S(1)}, bf16[4,128,512]{2,1,0:T(8,128)(2,1)S(1)}, bf16[4,128,512]{2,1,0:T(8,128)(2,1)S(1)}, f32[4,128,512]{2,1,0:T(8,128)S(1)},...) custom-call(s32[1,16]{1,0:T(1,128)} %home_hbm.1, ...), custom_call_target="tpu_custom_call" | custom-call | tf_op jit(solution)/shard_map/ahead/pallas_call | solution.py:359
  8.9 0.0 collective-permute-done.3.rest_2_
  8.9 0.1 pick_keys.1
  9.0 0.3 %collective-permute-start.4 = (bf16[144,512]{1,0:T(8,128)(2,1)S(1)}, bf16[144,512]{1,0:T(8,128)(2,1)S(1)}, u32[]{:S(2)}, u32[]{:S(2)}) collective-permute-start(bf16[144,512]{1,0:T(8,128)(2,1)S(1)} %get-tuple-element.35), channel_id=1, source_target_pairs={{0,1},{1,0},{2,3},{3,2},{4,5},{5,4},{6,7},{7,6},{8,9},{9,8},{10,11... | collective-permute-start | bytes 442376 | tf_op jit(solution)/shard_map/ppermute | solution.py:307
  9.3 2.0 %collective-permute-done.6.rest_1_ = bf16[144,512]{1,0:T(8,128)(2,1)S(1)} collective-permute-done((bf16[144,512]{1,0:T(8,128)(2,1)S(1)}, bf16[144,512]{1,0:T(8,128)(2,1)S(1)}, u32[]{:S(2)}, u32[]{:S(2)}) %collective-permute-start.6) | collective-permute-done | bytes 147488 | tf_op jit(solution)/shard_map/ppermute | solution.py:321
  11.4 0.1 collective-permute-start.7
  11.5 1.1 %weights.1.p_ref = bf16[4,256,512]{2,1,0:T(8,128)(2,1)S(1)} custom-call(bf16[4,128,512]{2,1,0:T(8,128)(2,1)S(1)} %get-tuple-element.31.qt_ref, f32[4,128,512]{2,1,0:T(8,128)S(1)} %get-tuple-element.32.s0_ref, bf16[128,512]{1,0:T(8,128)(2,1)S(1)} %get-tuple-element.33.own_ref, bf16[128,512]{1,0:T(8,128)(2,1)S(1)} %get-tuple-element.34.far_ref, ...), custom_call_target="tpu_custom_call" | custom-call | tf_op jit(solution)/shard_map/weights/pallas_call | solution.py:397
  12.6 0.2 collective-permute-done.7.near_ref
  12.8 0.7 %attend.1 = (bf16[8,8,2048]{2,1,0:T(8,128)(2,1)S(1)}, bf16[8,8,2048]{2,1,0:T(8,128)(2,1)S(1)}, bf16[8,8,2048]{2,1,0:T(8,128)(2,1)S(1)}, bf16[8,8,2048]{2,1,0:T(8,128)(2,1)S(1)}) custom-call(s32[1,16]{1,0:T(1,128)S(1)} %get-tuple-element.30.rest_3_.rest_2_.home_hbm, bf16[4,256,512]{2,1,0:T(8,128)(2,1)S(1)} %weights.1.p_ref, ...), custom_call_target="tpu_custom_call" | custom-call | tf_op jit(solution)/shard_map/attend/pallas_call | solution.py:406
  13.5 2.6 %collective-permute-start.14 = (bf16[8,8,2048]{2,1,0:T(8,128)(2,1)S(1)}, bf16[8,8,2048]{2,1,0:T(8,128)(2,1)S(1)}, u32[]{:S(2)}, u32[]{:S(2)}) collective-permute-start(bf16[8,8,2048]{2,1,0:T(8,128)(2,1)S(1)} %get-tuple-element.50), channel_id=1, source_target_pairs={{0,24},{8,16},{16,8},{24,0},{1,25},{9,17},{17,9},{25,1},{2,26},{10... | collective-permute-start | bytes 786440 | tf_op jit(solution)/shard_map/ppermute | solution.py:330
  16.1 2.1 %sent_terms.1 = (bf16[4,256,512]{2,1,0:T(8,128)(2,1)S(1)}, bf16[256,512]{1,0:T(8,128)(2,1)S(1)}, bf16[128,512]{1,0:T(8,128)(2,1)S(1)}, bf16[128,512]{1,0:T(8,128)(2,1)S(1)}) custom-call(bf16[128,2048]{1,0:T(8,128)(2,1)S(1)} %get-tuple-element.40.q_ref, bf16[128,2048]{1,0:T(8,128)(2,1)S(1)} %get-tuple-element.41.do_ref, ...), custom_call_target="tpu_custom_call" | custom-call | tf_op jit(solution)/shard_map/sent_terms/pallas_call | solution.py:426
  18.2 0.1 collective-permute-start.10
  18.3 0.5 %collective-permute-start.11 = (bf16[128,512]{1,0:T(8,128)(2,1)S(1)}, bf16[128,512]{1,0:T(8,128)(2,1)S(1)}, u32[]{:S(2)}, u32[]{:S(2)}) collective-permute-start(bf16[128,512]{1,0:T(8,128)(2,1)S(1)} %get-tuple-element.46), channel_id=1, source_target_pairs={{0,1},{1,0},{2,3},{3,2},{4,5},{5,4},{6,7},{7,6},{8,9},{9,8},{10,11... | collective-permute-start | bytes 393224 | tf_op jit(solution)/shard_map/ppermute | solution.py:307
  18.8 0.5 %collective-permute-start.8 = (bf16[8,8,2048]{2,1,0:T(8,128)(2,1)S(1)}, bf16[8,8,2048]{2,1,0:T(8,128)(2,1)S(1)}, u32[]{:S(2)}, u32[]{:S(2)}) collective-permute-start(bf16[8,8,2048]{2,1,0:T(8,128)(2,1)S(1)} %get-tuple-element.38), channel_id=1, source_target_pairs={{0,16},{8,24},{16,0},{24,8},{1,17},{9,25},{17,1},{25,9},{2,18},{10... | collective-permute-start | bytes 786440 | tf_op jit(solution)/shard_map/ppermute | solution.py:330
  19.3 0.4 %collective-permute-start.9 = (bf16[8,8,2048]{2,1,0:T(8,128)(2,1)S(1)}, bf16[8,8,2048]{2,1,0:T(8,128)(2,1)S(1)}, u32[]{:S(2)}, u32[]{:S(2)}) collective-permute-start(bf16[8,8,2048]{2,1,0:T(8,128)(2,1)S(1)} %get-tuple-element.39), channel_id=1, source_target_pairs={{0,8},{8,0},{16,24},{24,16},{1,9},{9,1},{17,25},{25,17},{2,10},{10... | collective-permute-start | bytes 786440 | tf_op jit(solution)/shard_map/ppermute | solution.py:330
  19.8 0.1 collective-permute-done.11.dv1_ref.rest_5_
  19.8 0.1 merge.1
  19.9 1.8 %collective-permute-start.13 = (bf16[256,512]{1,0:T(8,128)(2,1)S(1)}, bf16[256,512]{1,0:T(8,128)(2,1)S(1)}, u32[]{:S(2)}, u32[]{:S(2)}) collective-permute-start(bf16[256,512]{1,0:T(8,128)(2,1)S(1)} %merge.1), channel_id=1, source_target_pairs={{0,2},{1,3},{2,0},{3,1},{4,6},{5,7},{6,4},{7,5},{8,10},{9,11},{10,... | collective-permute-start | bytes 786440 | tf_op jit(solution)/shard_map/ppermute | solution.py:321
  21.7 0.0 collective-permute-start.12
  21.8 1.7 %kept_terms.1 = (bf16[128,2048]{1,0:T(8,128)(2,1)}, f32[256,512]{1,0:T(8,128)S(1)}, f32[8,128]{1,0:T(8,128)S(1)}) custom-call(bf16[128,2048]{1,0:T(8,128)(2,1)S(1)} %get-tuple-element.40.q_ref, bf16[128,2048]{1,0:T(8,128)(2,1)S(1)} %get-tuple-element.41.do_ref, bf16[128,512]{1,0:T(8,128)(2,1)S(1)} %get-tuple-element.33.own_ref, ...), custom_call_target="tpu_custom_call" | custom-call | flops 1073741824 | tf_op jit(solution)/shard_map/kept_terms/pallas_call | solution.py:435
  23.5 0.8 %place_early.1.rest_7_ = bf16[1,1,4,8,8,2048]{5,4,3,2,1,0:T(8,128)(2,1)} custom-call(f32[8,128]{1,0:T(8,128)S(1)} %get-tuple-element.49.kept_ref, bf16[8,8,2048]{2,1,0:T(8,128)(2,1)S(1)} %collective-permute-done.14.far_ref, bf16[8,8,2048]{2,1,0:T(8,128)(2,1)S(1)} %get-tuple-element.51.own_ref), custom_call_target="tpu_custom_call" | custom-call | flops 2147483648 | tf_op jit(solution)/shard_map/place_early/pallas_call | solution.py:460
  24.3 4.3 %collective-permute-done.8.rest_0_ = bf16[8,8,2048]{2,1,0:T(8,128)(2,1)S(1)} collective-permute-done((bf16[8,8,2048]{2,1,0:T(8,128)(2,1)S(1)}, bf16[8,8,2048]{2,1,0:T(8,128)(2,1)S(1)}, u32[]{:S(2)}, u32[]{:S(2)}) %collective-permute-start.8) | collective-permute-done | bytes 262176 | tf_op jit(solution)/shard_map/ppermute | solution.py:330
  28.6 0.2 collective-permute-done.9.rest_1_
  28.8 0.9 %finish.1 = (bf16[1,1,4,8,8,2048]{5,4,3,2,1,0:T(8,128)(2,1)}, bf16[128,512]{1,0:T(8,128)(2,1)}, bf16[128,512]{1,0:T(8,128)(2,1)}) custom-call(bf16[8,8,2048]{2,1,0:T(8,128)(2,1)S(1)} %collective-permute-done.8.rest_0_, bf16[8,8,2048]{2,1,0:T(8,128)(2,1)S(1)} %collective-permute-done.9.rest_1_, ...), custom_call_target="tpu_custom_call", output_to_operand_aliasing={{0}: (7, {})} | custom-call | bytes 1048576 | tf_op jit(solution)/shard_map/finish/pallas_call | solution.py:470
  (9 shorter events, 0.1 us)
Async XLA Ops:
  0.6 3.7 %collective-permute-start = (s32[1,128]{1,0:T(1,128)}, s32[1,128]{1,0:T(1,128)S(1)}, u32[]{:S(2)}, u32[]{:S(2)}) collective-permute-start(s32[1,128]{1,0:T(1,128)} %seg_hbm.1), channel_id=1, source_target_pairs={{0,1},{1,0},{2,3},{3,2},{4,5},{5,4},{6,7},{7,6},{8,9},{9,8},{10,11... | collective-permute-start | bytes 1544 | tf_op jit(solution)/shard_map/ppermute | solution.py:307
  1.1 7.7 %collective-permute-start.3 = (bf16[128,512]{1,0:T(8,128)(2,1)}, bf16[128,512]{1,0:T(8,128)(2,1)S(1)}, u32[]{:S(2)}, u32[]{:S(2)}) collective-permute-start(bf16[128,512]{1,0:T(8,128)(2,1)} %bitcast.9), channel_id=1, source_target_pairs={{0,2},{1,3},{2,0},{3,1},{4,5},{5,4},{6,7},{7,6},{8,10},{9,11},{10,... | collective-permute-start | bytes 393224 | tf_op jit(solution)/shard_map/ppermute | solution.py:321
  3.8 5.1 %collective-permute-start.2 = (bf16[128,512]{1,0:T(8,128)(2,1)}, bf16[128,512]{1,0:T(8,128)(2,1)S(1)}, u32[]{:S(2)}, u32[]{:S(2)}) collective-permute-start(bf16[128,512]{1,0:T(8,128)(2,1)} %bitcast.10), channel_id=1, source_target_pairs={{0,1},{1,0},{2,4},{3,5},{4,2},{5,3},{6,7},{7,6},{8,9},{9,8},{10,12... | collective-permute-start | bytes 393224 | tf_op jit(solution)/shard_map/ppermute | solution.py:321
  4.0 4.9 %collective-permute-start.1 = (bf16[128,512]{1,0:T(8,128)(2,1)}, bf16[128,512]{1,0:T(8,128)(2,1)S(1)}, u32[]{:S(2)}, u32[]{:S(2)}) collective-permute-start(bf16[128,512]{1,0:T(8,128)(2,1)} %bitcast.11), channel_id=1, source_target_pairs={{0,1},{1,0},{2,3},{3,2},{4,6},{5,7},{6,4},{7,5},{8,9},{9,8},{10,11... | collective-permute-start | bytes 393224 | tf_op jit(solution)/shard_map/ppermute | solution.py:321
  5.3 6.1 %collective-permute-start.6 = (bf16[144,512]{1,0:T(8,128)(2,1)S(1)}, bf16[144,512]{1,0:T(8,128)(2,1)S(1)}, u32[]{:S(2)}, u32[]{:S(2)}) collective-permute-start(bf16[144,512]{1,0:T(8,128)(2,1)S(1)} %bundle.1.v_ref.own_ref.own_ids_ref), channel_id=1, source_target_pairs={{0,2},{1,3},{2,0},{3,1},{4,6},{5,7},{6,4},{7,5},{8,10},{9,11},{10,... | collective-permute-start | bytes 442376 | tf_op jit(solution)/shard_map/ppermute | solution.py:321
  6.8 4.5 %collective-permute-start.5 = (bf16[144,512]{1,0:T(8,128)(2,1)S(1)}, bf16[144,512]{1,0:T(8,128)(2,1)S(1)}, u32[]{:S(2)}, u32[]{:S(2)}) collective-permute-start(bf16[144,512]{1,0:T(8,128)(2,1)S(1)} %bundle.1.v_ref.own_ref.own_ids_ref), channel_id=1, source_target_pairs={{0,1},{1,0},{2,4},{3,5},{4,2},{5,3},{6,7},{7,6},{8,9},{9,8},{10,12... | collective-permute-start | bytes 442376 | tf_op jit(solution)/shard_map/ppermute | solution.py:321
  9.0 2.5 %collective-permute-start.4 = (bf16[144,512]{1,0:T(8,128)(2,1)S(1)}, bf16[144,512]{1,0:T(8,128)(2,1)S(1)}, u32[]{:S(2)}, u32[]{:S(2)}) collective-permute-start(bf16[144,512]{1,0:T(8,128)(2,1)S(1)} %get-tuple-element.35), channel_id=1, source_target_pairs={{0,1},{1,0},{2,3},{3,2},{4,5},{5,4},{6,7},{7,6},{8,9},{9,8},{10,11... | collective-permute-start | bytes 442376 | tf_op jit(solution)/shard_map/ppermute | solution.py:307
  11.4 1.4 %collective-permute-start.7 = (bf16[128,512]{1,0:T(8,128)(2,1)S(1)}, bf16[128,512]{1,0:T(8,128)(2,1)S(1)}, u32[]{:S(2)}, u32[]{:S(2)}) collective-permute-start(bf16[128,512]{1,0:T(8,128)(2,1)S(1)} %get-tuple-element.37), channel_id=1, source_target_pairs={{0,1},{1,0},{2,3},{3,2},{4,5},{5,4},{6,7},{7,6},{8,9},{9,8},{10,11... | collective-permute-start | bytes 393224 | tf_op jit(solution)/shard_map/ppermute | solution.py:307
  13.5 9.9 %collective-permute-start.14 = (bf16[8,8,2048]{2,1,0:T(8,128)(2,1)S(1)}, bf16[8,8,2048]{2,1,0:T(8,128)(2,1)S(1)}, u32[]{:S(2)}, u32[]{:S(2)}) collective-permute-start(bf16[8,8,2048]{2,1,0:T(8,128)(2,1)S(1)} %get-tuple-element.50), channel_id=1, source_target_pairs={{0,24},{8,16},{16,8},{24,0},{1,25},{9,17},{17,9},{25,1},{2,26},{10... | collective-permute-start | bytes 786440 | tf_op jit(solution)/shard_map/ppermute | solution.py:330
  18.2 1.5 %collective-permute-start.10 = (bf16[128,512]{1,0:T(8,128)(2,1)S(1)}, bf16[128,512]{1,0:T(8,128)(2,1)S(1)}, u32[]{:S(2)}, u32[]{:S(2)}) collective-permute-start(bf16[128,512]{1,0:T(8,128)(2,1)S(1)} %get-tuple-element.45), channel_id=1, source_target_pairs={{0,1},{1,0},{2,3},{3,2},{4,5},{5,4},{6,7},{7,6},{8,9},{9,8},{10,11... | collective-permute-start | bytes 393224 | tf_op jit(solution)/shard_map/ppermute | solution.py:307
  18.3 1.5 %collective-permute-start.11 = (bf16[128,512]{1,0:T(8,128)(2,1)S(1)}, bf16[128,512]{1,0:T(8,128)(2,1)S(1)}, u32[]{:S(2)}, u32[]{:S(2)}) collective-permute-start(bf16[128,512]{1,0:T(8,128)(2,1)S(1)} %get-tuple-element.46), channel_id=1, source_target_pairs={{0,1},{1,0},{2,3},{3,2},{4,5},{5,4},{6,7},{7,6},{8,9},{9,8},{10,11... | collective-permute-start | bytes 393224 | tf_op jit(solution)/shard_map/ppermute | solution.py:307
  18.8 9.8 %collective-permute-start.8 = (bf16[8,8,2048]{2,1,0:T(8,128)(2,1)S(1)}, bf16[8,8,2048]{2,1,0:T(8,128)(2,1)S(1)}, u32[]{:S(2)}, u32[]{:S(2)}) collective-permute-start(bf16[8,8,2048]{2,1,0:T(8,128)(2,1)S(1)} %get-tuple-element.38), channel_id=1, source_target_pairs={{0,16},{8,24},{16,0},{24,8},{1,17},{9,25},{17,1},{25,9},{2,18},{10... | collective-permute-start | bytes 786440 | tf_op jit(solution)/shard_map/ppermute | solution.py:330
  19.3 9.5 %collective-permute-start.9 = (bf16[8,8,2048]{2,1,0:T(8,128)(2,1)S(1)}, bf16[8,8,2048]{2,1,0:T(8,128)(2,1)S(1)}, u32[]{:S(2)}, u32[]{:S(2)}) collective-permute-start(bf16[8,8,2048]{2,1,0:T(8,128)(2,1)S(1)} %get-tuple-element.39), channel_id=1, source_target_pairs={{0,8},{8,0},{16,24},{24,16},{1,9},{9,1},{17,25},{25,17},{2,10},{10... | collective-permute-start | bytes 786440 | tf_op jit(solution)/shard_map/ppermute | solution.py:330
  19.9 8.9 %collective-permute-start.13 = (bf16[256,512]{1,0:T(8,128)(2,1)S(1)}, bf16[256,512]{1,0:T(8,128)(2,1)S(1)}, u32[]{:S(2)}, u32[]{:S(2)}) collective-permute-start(bf16[256,512]{1,0:T(8,128)(2,1)S(1)} %merge.1), channel_id=1, source_target_pairs={{0,2},{1,3},{2,0},{3,1},{4,6},{5,7},{6,4},{7,5},{8,10},{9,11},{10,... | collective-permute-start | bytes 786440 | tf_op jit(solution)/shard_map/ppermute | solution.py:321
  21.7 7.1 %collective-permute-start.12 = (bf16[256,512]{1,0:T(8,128)(2,1)S(1)}, bf16[256,512]{1,0:T(8,128)(2,1)S(1)}, u32[]{:S(2)}, u32[]{:S(2)}) collective-permute-start(bf16[256,512]{1,0:T(8,128)(2,1)S(1)} %merge.1), channel_id=1, source_target_pairs={{0,1},{1,0},{2,4},{3,5},{4,2},{5,3},{6,7},{7,6},{8,9},{9,8},{10,12... | collective-permute-start | bytes 786440 | tf_op jit(solution)/shard_map/ppermute | solution.py:321

commit v8 on v7

--- a/solution.py
+++ b/solution.py
@@ -46,39 +46,36 @@
     return home ^ row if count & (count - 1) == 0 else lax.rem(home - row + count, count)
 
 
-def weights_kernel(qt_ref, s0_ref, own_ref, far_ref, near_ref, own_ids_ref, far_ids_ref, p_ref):
+def weights_kernel(
+    qt_ref, s0_ref, own_ref, far_ref, near_ref, own_ids_ref, far_ids_ref, bias_ref, joined_ref, p_ref
+):
     block = s0_ref.shape[1]
     column = lax.axis_index("ctx")
 
-    def seg_of(ref, core):
-        cols = slice(core * block, (core + 1) * block)
-        return ref[block : block + SEG_ROWS, cols].astype(F32)[0:1]
-
     first_core = lax.rem(column, 2) == 0
-    seg_own = jnp.where(first_core, seg_of(own_ids_ref, 0), seg_of(own_ids_ref, 1))
-    seg_near = jnp.where(first_core, seg_of(far_ids_ref, 1), seg_of(own_ids_ref, 0))
-    seg_far = jnp.where(first_core, seg_of(far_ids_ref, 0), seg_of(far_ids_ref, 1))
-    first = seg_own[:, 0:1]
-    reach = jnp.where(column >= 1, jnp.sum((seg_near == first).astype(F32), axis=1, keepdims=True), 0.0)
-    reach = reach + jnp.where(
-        column >= 2, jnp.sum((seg_far == first).astype(F32), axis=1, keepdims=True), 0.0
-    )
+    first = own_ids(own_ids_ref, block)[:, 0:1]
+    seg_near = jnp.where(first_core, ids_of(far_ids_ref, block, 1), ids_of(own_ids_ref, block, 0))
+    seg_far = jnp.where(first_core, ids_of(far_ids_ref, block, 0), ids_of(far_ids_ref, block, 1))
+    seen = jnp.where((seg_near == first) & (column >= 1), 1.0, 0.0)
+    seen = seen + jnp.where((seg_far == first) & (column >= 2), 1.0, 0.0)
+    reach = jnp.sum(seen, axis=1, keepdims=True)
     key_pos = lax.broadcasted_iota(jnp.int32, (block, block), 0).astype(F32)
-    tri = triangle(block, 1)
-    seg_rows = jnp.broadcast_to(seg_own, (block, block))
-    joined = seg_rows == first
-    own_ok = seg_rows == seg_rows.T
-    far_ok = (key_pos >= 2 * block - reach) & joined
-    near_ok = (key_pos >= block - reach) & joined
-    bias_x = jnp.where((tri & own_ok) | (~tri & far_ok), 0.0, NEG)
-    bias_n = jnp.where(near_ok, 0.0, NEG)
+    joined = joined_ref[...]
+    far_bias = jnp.where(key_pos >= 2 * block - reach, joined, NEG)
+    bias_n = jnp.where(key_pos >= block - reach, joined, NEG)
+    bias_x = jnp.where(triangle(block, 1), bias_ref[...], far_bias)
     bias_x = jnp.concatenate([bias_x] * GROUP, axis=1)
     bias_n = jnp.concatenate([bias_n] * GROUP, axis=1)
     tri_g = triangle(block, GROUP)
     scaling = math.log2(math.e) / math.sqrt(HEAD_DIM)
-    for g in range(qt_ref.shape[0]):
+    def products(g):
         keys = head_blocks(g, block, own_ref, far_ref, near_ref)
-        scores = dot(jnp.concatenate(keys[1:], axis=0), qt_ref[g], NN)
+        return dot(jnp.concatenate(keys[1:], axis=0), qt_ref[g], NN)
+
+    heads = qt_ref.shape[0]
+    upcoming = products(0)
+    for g in range(heads):
+        scores, upcoming = upcoming, products(g + 1) if g + 1 < heads else None
         s_x = jnp.where(tri_g, s0_ref[g], scores[block:]) * scaling + bias_x
         s_n = scores[0:block] * scaling + bias_n
         highest = jnp.max(jnp.maximum(s_x, s_n), axis=0, keepdims=True)
@@ -133,15 +130,30 @@
     return jnp.where(triangle(block, GROUP), 1.0, 0.0).astype(BF16)
 
 
+def ids_of(ref, block, core):
+    cols = slice(core * block, (core + 1) * block)
+    return ref[block : block + SEG_ROWS, cols].astype(F32)[0:1]
+
+
+def own_ids(ref, block):
+    first_core = lax.rem(lax.axis_index("ctx"), 2) == 0
+    return jnp.where(first_core, ids_of(ref, block, 0), ids_of(ref, block, 1))
+
+
 def ahead_kernel(
     home_hbm, q_hbm, do_hbm, k_hbm, v_ref,
-    plan_ref, qt_ref, gt_ref, s0_ref, gw0_ref, q_ref, do_ref, key_ref, sems,
+    plan_ref, qt_ref, gt_ref, s0_ref, gw0_ref, q_ref, do_ref, key_ref, bias_ref, joined_ref, sems,
 ):
     pairs = ((q_hbm, q_ref), (k_hbm, key_ref), (do_hbm, do_ref), (home_hbm, plan_ref))
     copies = [pltpu.make_async_copy(*pair, sems.at[i]) for i, pair in enumerate(pairs)]
     for copy in copies:
         copy.start()
     block = q_ref.shape[0]
+    seg_own = own_ids(v_ref, block)
+    seg_rows = jnp.broadcast_to(seg_own, (block, block))
+    own_ok = triangle(block, 1) & (seg_rows == seg_rows.T)
+    bias_ref[...] = jnp.where(own_ok, 0.0, NEG)
+    joined_ref[...] = jnp.where(seg_rows == seg_own[:, 0:1], 0.0, NEG)
     for source, own_ref, turned, product, waits in (
         (q_ref, key_ref, qt_ref, s0_ref, copies[:2]),
         (do_ref, v_ref, gt_ref, gw0_ref, copies[2:]),
@@ -157,25 +169,30 @@
     block = q_ref.shape[0]
     tri_g, lower = triangle(block, GROUP), lower_mask(block)
     scaling = 1.0 / math.sqrt(HEAD_DIM)
-    for g in range(own_ref.shape[1] // HEAD_DIM):
+    def products(g):
         values = head_blocks(g, block, own_ref, far_ref, near_ref)
+        return dot(jnp.concatenate(values[1:], axis=0), gt_ref[g], NN)
+
+    heads = gt_ref.shape[0]
+    upcoming = products(0)
+    for g in range(heads):
+        score_terms, upcoming = upcoming, products(g + 1) if g + 1 < heads else None
         queries, grads = stacked(q_ref, g), stacked(do_ref, g)
         w_xb = p_ref[g, 0:block]
         w_x = w_xb.astype(F32)
         w_n = p_ref[g, block : 2 * block]
         w_nf = w_n.astype(F32)
-        score_terms = dot(jnp.concatenate(values[1:], axis=0), gt_ref[g], NN)
         gw_x = jnp.where(tri_g, gw0_ref[g], score_terms[block:])
         gw_n = score_terms[0:block]
         delta = jnp.sum(w_x * gw_x + w_nf * gw_n, axis=0, keepdims=True)
-        gs_x = (w_x * (gw_x - delta) * scaling).astype(BF16)
-        gs_n = (w_nf * (gw_n - delta) * scaling).astype(BF16)
+        gs_x = (w_x * (gw_x - delta)).astype(BF16)
+        gs_n = (w_nf * (gw_n - delta)).astype(BF16)
         gs_ref[g, 0:block] = gs_x
         gs_ref[g, block : 2 * block] = gs_n
         _, gs_2 = split(lower, gs_x)
         _, w_2 = split(lower, w_xb)
         cols = slice(g * HEAD_DIM, (g + 1) * HEAD_DIM)
-        dk = dot(jnp.concatenate([gs_n, gs_2], axis=0), queries, NN).astype(d2_ref.dtype)
+        dk = (dot(jnp.concatenate([gs_n, gs_2], axis=0), queries, NN) * scaling).astype(d2_ref.dtype)
         dv = dot(jnp.concatenate([w_n, w_2], axis=0), grads, NN).astype(d2_ref.dtype)
         dk1_ref[:, cols] = dk[0:block]
         dv1_ref[:, cols] = dv[0:block]
@@ -187,6 +204,7 @@
     mark_ref[...] = jnp.zeros_like(mark_ref)
     block = q_ref.shape[0]
     lower = lower_mask(block)
+    scaling = 1.0 / math.sqrt(HEAD_DIM)
     for g in range(own_ref.shape[1] // HEAD_DIM):
         keys = head_blocks(g, block, own_ref, far_ref, near_ref)
         queries, grads = stacked(q_ref, g), stacked(do_ref, g)
@@ -194,12 +212,12 @@
         w_0, _ = split(lower, p_ref[g, 0:block])
         gs_n = gs_ref[g, block : 2 * block]
         cols = slice(g * HEAD_DIM, (g + 1) * HEAD_DIM)
-        d0_ref[0:block, cols] = dot(gs_0, queries, NN)
+        d0_ref[0:block, cols] = dot(gs_0, queries, NN) * scaling
         d0_ref[block : 2 * block, cols] = dot(w_0, grads, NN)
         dq = dot(jnp.concatenate([gs_0, gs_n, gs_2], axis=0), jnp.concatenate(keys, axis=0), TN)
         for h in range(GROUP):
             heads = slice((g * GROUP + h) * HEAD_DIM, (g * GROUP + h + 1) * HEAD_DIM)
-            dq_ref[:, heads] = dq[h * block : (h + 1) * block].astype(dq_ref.dtype)
+            dq_ref[:, heads] = (dq[h * block : (h + 1) * block] * scaling).astype(dq_ref.dtype)
 
 
 def bundle_kernel(seg_hbm, other_ref, v_hbm, own_ref, seg_ref, sems):
@@ -356,15 +374,16 @@
 
     turned = jax.ShapeDtypeStruct((heads, HEAD_DIM, GROUP * block), BF16)
     product = jax.ShapeDtypeStruct((heads, block, GROUP * block), F32)
-    plan, turned_query, turned_grad, own_scores, own_terms, query, grad, own_keys = pl.pallas_call(
+    plan, turned_query, turned_grad, own_scores, own_terms, query, grad, own_keys, *masks = pl.pallas_call(
         ahead_kernel,
         out_shape=[
             jax.ShapeDtypeStruct(home_rows.shape, jnp.int32), turned, turned, product, product,
             jax.ShapeDtypeStruct(query.shape, BF16), jax.ShapeDtypeStruct(grad.shape, BF16),
             jax.ShapeDtypeStruct(keys.shape, BF16),
+            jax.ShapeDtypeStruct((block, block), F32), jax.ShapeDtypeStruct((block, block), F32),
         ],
         in_specs=[HBM] * 4 + [VMEM],
-        out_specs=[VMEM] * 8,
+        out_specs=[VMEM] * 10,
         scratch_shapes=[pltpu.SemaphoreType.DMA((4,))],
         compiler_params=params(),
         cost_estimate=cost(0, 0),
@@ -397,12 +416,12 @@
     weights = pl.pallas_call(
         weights_kernel,
         out_shape=jax.ShapeDtypeStruct((heads, 2 * block, GROUP * block), BF16),
-        in_specs=[VMEM] * 7,
+        in_specs=[VMEM] * 9,
         out_specs=VMEM,
         compiler_params=params(),
         cost_estimate=cost(0, 0),
         name="weights",
-    )(turned_query, own_scores, own_keys, far_keys, near_keys, values, far_values)
+    )(turned_query, own_scores, own_keys, far_keys, near_keys, values, far_values, *masks)
     sends = pl.pallas_call(
         functools.partial(attend_kernel, n_dp),
         out_shape=[jax.ShapeDtypeStruct((capacity, piece_len, width), BF16)] * n_dp,

time: 29.9 us -> 29.9 us (level)
  Pallas kernels: 10.2 us -> 9.75 us
  waiting for transfers between devices: 6.9 us -> 7.33 us
    ppermute x3, waiting for transfers between devices: 4.52 us -> 4.96 us  [exchange(): return lax.ppermute(value, 'dp', pairs)]
    pallas_call x1, Pallas kernels: 2.07 us -> 1.64 us  [on_device(): pl.pallas_call(sent_kernel, out_shape=[jax.ShapeDtypeStruct(weights.shape...]
  transfers between devices with their start and end apart: 15 -> 15, of which waited for: 5 -> 6; matrix products, arithmetic and copies ran while one was open for 0% -> 0% of each run, Pallas kernels for 29% -> 27%
where the time goes in v8:
time: 29.9 us; the launch traced here: 29.7 us
  starting transfers between devices  11.9 us (40%)
  Pallas kernels  9.75 us (33%)
  waiting for transfers between devices  7.33 us (25%)
  between operations  0.76 us (3%)
    ppermute x7, starting transfers between devices, from_chip(): lax.ppermute(value, 'ctx', pairs(colour))  6.81 us
    ppermute x3, waiting for transfers between devices, exchange(): return lax.ppermute(value, 'dp', pairs)  4.96 us
    ppermute x3, starting transfers between devices, exchange(): return lax.ppermute(value, 'dp', pairs)  3.56 us
    ppermute x7, waiting for transfers between devices, from_chip(): lax.ppermute(value, 'ctx', pairs(colour))  2.05 us
    pallas_call x1, Pallas kernels, on_device(): pl.pallas_call(ahead_kernel, out_shape=[jax.ShapeDtypeStruct(home_rows.sh...  1.81 us
    pallas_call x1, Pallas kernels, on_device(): pl.pallas_call(kept_kernel, out_shape=[jax.ShapeDtypeStruct((block, width...  1.68 us
    pallas_call x1, Pallas kernels, on_device(): pl.pallas_call(sent_kernel, out_shape=[jax.ShapeDtypeStruct(weights.shape...  1.64 us
    ppermute x5, starting transfers between devices, swap(): return lax.ppermute(value, 'ctx', [(i, i ^ 1) for i in range(count)])  1.5 us
  transfers between devices with their start and end apart: 15, of which 6 were waited for; matrix products, arithmetic and copies ran while one was open for 0% of the time, Pallas kernels for 27%

profile of v8, /device:TPU:0, one launch (start us, length us, event | category | flops | bytes accessed | tf_op | source)
XLA Modules:
  0.0 29.7 jit_solution(471331102107332580)
XLA Ops:
  0.6 0.5 %collective-permute-start = (s32[1,128]{1,0:T(1,128)}, s32[1,128]{1,0:T(1,128)S(1)}, u32[]{:S(2)}, u32[]{:S(2)}) collective-permute-start(s32[1,128]{1,0:T(1,128)} %seg_hbm.1), channel_id=1, source_target_pairs={{0,1},{1,0},{2,3},{3,2},{4,5},{5,4},{6,7},{7,6},{8,9},{9,8},{10,11... | collective-permute-start | bytes 1544 | tf_op jit(solution)/shard_map/ppermute | solution.py:325
  1.1 2.6 %collective-permute-start.3 = (bf16[128,512]{1,0:T(8,128)(2,1)}, bf16[128,512]{1,0:T(8,128)(2,1)S(1)}, u32[]{:S(2)}, u32[]{:S(2)}) collective-permute-start(bf16[128,512]{1,0:T(8,128)(2,1)} %bitcast.9), channel_id=1, source_target_pairs={{0,2},{1,3},{2,0},{3,1},{4,5},{5,4},{6,7},{7,6},{8,10},{9,11},{10,... | collective-permute-start | bytes 393224 | tf_op jit(solution)/shard_map/ppermute | solution.py:339
  3.8 0.2 collective-permute-start.2
  4.0 0.3 %collective-permute-start.1 = (bf16[128,512]{1,0:T(8,128)(2,1)}, bf16[128,512]{1,0:T(8,128)(2,1)S(1)}, u32[]{:S(2)}, u32[]{:S(2)}) collective-permute-start(bf16[128,512]{1,0:T(8,128)(2,1)} %bitcast.11), channel_id=1, source_target_pairs={{0,1},{1,0},{2,3},{3,2},{4,6},{5,7},{6,4},{7,5},{8,9},{9,8},{10,11... | collective-permute-start | bytes 393224 | tf_op jit(solution)/shard_map/ppermute | solution.py:339
  4.3 0.0 collective-permute-done.other_ref
  4.3 0.9 %bundle.1.v_ref.own_ref.own_ids_ref = bf16[144,512]{1,0:T(8,128)(2,1)S(1)} custom-call(s32[1,128]{1,0:T(1,128)} %seg_hbm.1, s32[1,128]{1,0:T(1,128)S(1)} %collective-permute-done.other_ref, bf16[128,512]{1,0:T(8,128)(2,1)} %bitcast.13), custom_call_target="tpu_custom_call" | custom-call | tf_op jit(solution)/shard_map/bundle/pallas_call | solution.py:363
  5.3 1.6 %collective-permute-start.6 = (bf16[144,512]{1,0:T(8,128)(2,1)S(1)}, bf16[144,512]{1,0:T(8,128)(2,1)S(1)}, u32[]{:S(2)}, u32[]{:S(2)}) collective-permute-start(bf16[144,512]{1,0:T(8,128)(2,1)S(1)} %bundle.1.v_ref.own_ref.own_ids_ref), channel_id=1, source_target_pairs={{0,2},{1,3},{2,0},{3,1},{4,6},{5,7},{6,4},{7,5},{8,10},{9,11},{10,... | collective-permute-start | bytes 442376 | tf_op jit(solution)/shard_map/ppermute | solution.py:339
  6.8 0.2 collective-permute-start.5
  7.1 1.8 %ahead.1 = (s32[1,16]{1,0:T(1,128)S(1)}, bf16[4,128,512]{2,1,0:T(8,128)(2,1)S(1)}, bf16[4,128,512]{2,1,0:T(8,128)(2,1)S(1)}, f32[4,128,512]{2,1,0:T(8,128)S(1)},...) custom-call(s32[1,16]{1,0:T(1,128)} %home_hbm.1, ...), custom_call_target="tpu_custom_call" | custom-call | tf_op jit(solution)/shard_map/ahead/pallas_call | solution.py:377
  8.9 0.0 collective-permute-done.3.rest_2_
  9.0 0.3 %collective-permute-start.4 = (bf16[144,512]{1,0:T(8,128)(2,1)S(1)}, bf16[144,512]{1,0:T(8,128)(2,1)S(1)}, u32[]{:S(2)}, u32[]{:S(2)}) collective-permute-start(bf16[144,512]{1,0:T(8,128)(2,1)S(1)} %get-tuple-element.37), channel_id=1, source_target_pairs={{0,1},{1,0},{2,3},{3,2},{4,5},{5,4},{6,7},{7,6},{8,9},{9,8},{10,11... | collective-permute-start | bytes 442376 | tf_op jit(solution)/shard_map/ppermute | solution.py:325
  9.3 2.0 %collective-permute-done.6.rest_1_ = bf16[144,512]{1,0:T(8,128)(2,1)S(1)} collective-permute-done((bf16[144,512]{1,0:T(8,128)(2,1)S(1)}, bf16[144,512]{1,0:T(8,128)(2,1)S(1)}, u32[]{:S(2)}, u32[]{:S(2)}) %collective-permute-start.6) | collective-permute-done | bytes 147488 | tf_op jit(solution)/shard_map/ppermute | solution.py:339
  11.4 0.1 collective-permute-start.7
  11.5 1.1 %weights.1.p_ref = bf16[4,256,512]{2,1,0:T(8,128)(2,1)S(1)} custom-call(bf16[4,128,512]{2,1,0:T(8,128)(2,1)S(1)} %get-tuple-element.33.qt_ref, f32[4,128,512]{2,1,0:T(8,128)S(1)} %get-tuple-element.34.s0_ref, bf16[128,512]{1,0:T(8,128)(2,1)S(1)} %get-tuple-element.35.own_ref, bf16[128,512]{1,0:T(8,128)(2,1)S(1)} %get-tuple-element.36.far_ref, ...), custom_call_target="tpu_custom_call" | custom-call | tf_op jit(solution)/shard_map/weights/pallas_call | solution.py:416
  12.6 0.2 collective-permute-done.7.near_ref
  12.8 0.7 %attend.1 = (bf16[8,8,2048]{2,1,0:T(8,128)(2,1)S(1)}, bf16[8,8,2048]{2,1,0:T(8,128)(2,1)S(1)}, bf16[8,8,2048]{2,1,0:T(8,128)(2,1)S(1)}, bf16[8,8,2048]{2,1,0:T(8,128)(2,1)S(1)}) custom-call(s32[1,16]{1,0:T(1,128)S(1)} %get-tuple-element.32.rest_3_.rest_2_.home_hbm, bf16[4,256,512]{2,1,0:T(8,128)(2,1)S(1)} %weights.1.p_ref, ...), custom_call_target="tpu_custom_call" | custom-call | tf_op jit(solution)/shard_map/attend/pallas_call | solution.py:425
  13.5 2.6 %collective-permute-start.14 = (bf16[8,8,2048]{2,1,0:T(8,128)(2,1)S(1)}, bf16[8,8,2048]{2,1,0:T(8,128)(2,1)S(1)}, u32[]{:S(2)}, u32[]{:S(2)}) collective-permute-start(bf16[8,8,2048]{2,1,0:T(8,128)(2,1)S(1)} %get-tuple-element.54), channel_id=1, source_target_pairs={{0,24},{8,16},{16,8},{24,0},{1,25},{9,17},{17,9},{25,1},{2,26},{10... | collective-permute-start | bytes 786440 | tf_op jit(solution)/shard_map/ppermute | solution.py:348
  16.1 1.6 %sent_terms.1 = (bf16[4,256,512]{2,1,0:T(8,128)(2,1)S(1)}, bf16[256,512]{1,0:T(8,128)(2,1)S(1)}, bf16[128,512]{1,0:T(8,128)(2,1)S(1)}, bf16[128,512]{1,0:T(8,128)(2,1)S(1)}) custom-call(bf16[128,2048]{1,0:T(8,128)(2,1)S(1)} %get-tuple-element.44.q_ref, bf16[128,2048]{1,0:T(8,128)(2,1)S(1)} %get-tuple-element.45.do_ref, ...), custom_call_target="tpu_custom_call" | custom-call | tf_op jit(solution)/shard_map/sent_terms/pallas_call | solution.py:445
  17.8 0.1 collective-permute-start.10
  17.9 0.5 %collective-permute-start.11 = (bf16[128,512]{1,0:T(8,128)(2,1)S(1)}, bf16[128,512]{1,0:T(8,128)(2,1)S(1)}, u32[]{:S(2)}, u32[]{:S(2)}) collective-permute-start(bf16[128,512]{1,0:T(8,128)(2,1)S(1)} %get-tuple-element.50), channel_id=1, source_target_pairs={{0,1},{1,0},{2,3},{3,2},{4,5},{5,4},{6,7},{7,6},{8,9},{9,8},{10,11... | collective-permute-start | bytes 393224 | tf_op jit(solution)/shard_map/ppermute | solution.py:325
  18.4 0.5 %collective-permute-start.8 = (bf16[8,8,2048]{2,1,0:T(8,128)(2,1)S(1)}, bf16[8,8,2048]{2,1,0:T(8,128)(2,1)S(1)}, u32[]{:S(2)}, u32[]{:S(2)}) collective-permute-start(bf16[8,8,2048]{2,1,0:T(8,128)(2,1)S(1)} %get-tuple-element.42), channel_id=1, source_target_pairs={{0,16},{8,24},{16,0},{24,8},{1,17},{9,25},{17,1},{25,9},{2,18},{10... | collective-permute-start | bytes 786440 | tf_op jit(solution)/shard_map/ppermute | solution.py:348
  18.9 0.4 %collective-permute-start.9 = (bf16[8,8,2048]{2,1,0:T(8,128)(2,1)S(1)}, bf16[8,8,2048]{2,1,0:T(8,128)(2,1)S(1)}, u32[]{:S(2)}, u32[]{:S(2)}) collective-permute-start(bf16[8,8,2048]{2,1,0:T(8,128)(2,1)S(1)} %get-tuple-element.43), channel_id=1, source_target_pairs={{0,8},{8,0},{16,24},{24,16},{1,9},{9,1},{17,25},{25,17},{2,10},{10... | collective-permute-start | bytes 786440 | tf_op jit(solution)/shard_map/ppermute | solution.py:348
  19.3 0.1 collective-permute-done.11.dv1_ref.rest_5_
  19.4 0.1 merge.1
  19.5 1.8 %collective-permute-start.13 = (bf16[256,512]{1,0:T(8,128)(2,1)S(1)}, bf16[256,512]{1,0:T(8,128)(2,1)S(1)}, u32[]{:S(2)}, u32[]{:S(2)}) collective-permute-start(bf16[256,512]{1,0:T(8,128)(2,1)S(1)} %merge.1), channel_id=1, source_target_pairs={{0,2},{1,3},{2,0},{3,1},{4,6},{5,7},{6,4},{7,5},{8,10},{9,11},{10,... | collective-permute-start | bytes 786440 | tf_op jit(solution)/shard_map/ppermute | solution.py:339
  21.3 0.0 collective-permute-start.12
  21.3 1.7 %kept_terms.1 = (bf16[128,2048]{1,0:T(8,128)(2,1)}, f32[256,512]{1,0:T(8,128)S(1)}, f32[8,128]{1,0:T(8,128)S(1)}) custom-call(bf16[128,2048]{1,0:T(8,128)(2,1)S(1)} %get-tuple-element.44.q_ref, bf16[128,2048]{1,0:T(8,128)(2,1)S(1)} %get-tuple-element.45.do_ref, bf16[128,512]{1,0:T(8,128)(2,1)S(1)} %get-tuple-element.35.own_ref, ...), custom_call_target="tpu_custom_call" | custom-call | flops 1073741824 | tf_op jit(solution)/shard_map/kept_terms/pallas_call | solution.py:454
  23.0 0.6 %collective-permute-done.14.far_ref = bf16[8,8,2048]{2,1,0:T(8,128)(2,1)S(1)} collective-permute-done((bf16[8,8,2048]{2,1,0:T(8,128)(2,1)S(1)}, bf16[8,8,2048]{2,1,0:T(8,128)(2,1)S(1)}, u32[]{:S(2)}, u32[]{:S(2)}) %collective-permute-start.14) | collective-permute-done | bytes 262176 | tf_op jit(solution)/shard_map/ppermute | solution.py:348
  23.6 0.8 %place_early.1.rest_7_ = bf16[1,1,4,8,8,2048]{5,4,3,2,1,0:T(8,128)(2,1)} custom-call(f32[8,128]{1,0:T(8,128)S(1)} %get-tuple-element.53.kept_ref, bf16[8,8,2048]{2,1,0:T(8,128)(2,1)S(1)} %collective-permute-done.14.far_ref, bf16[8,8,2048]{2,1,0:T(8,128)(2,1)S(1)} %get-tuple-element.55.own_ref), custom_call_target="tpu_custom_call" | custom-call | flops 2147483648 | tf_op jit(solution)/shard_map/place_early/pallas_call | solution.py:479
  24.5 4.1 %collective-permute-done.8.rest_0_ = bf16[8,8,2048]{2,1,0:T(8,128)(2,1)S(1)} collective-permute-done((bf16[8,8,2048]{2,1,0:T(8,128)(2,1)S(1)}, bf16[8,8,2048]{2,1,0:T(8,128)(2,1)S(1)}, u32[]{:S(2)}, u32[]{:S(2)}) %collective-permute-start.8) | collective-permute-done | bytes 262176 | tf_op jit(solution)/shard_map/ppermute | solution.py:348
  28.6 0.2 collective-permute-done.9.rest_1_
  28.8 0.9 %finish.1 = (bf16[1,1,4,8,8,2048]{5,4,3,2,1,0:T(8,128)(2,1)}, bf16[128,512]{1,0:T(8,128)(2,1)}, bf16[128,512]{1,0:T(8,128)(2,1)}) custom-call(bf16[8,8,2048]{2,1,0:T(8,128)(2,1)S(1)} %collective-permute-done.8.rest_0_, bf16[8,8,2048]{2,1,0:T(8,128)(2,1)S(1)} %collective-permute-done.9.rest_1_, ...), custom_call_target="tpu_custom_call", output_to_operand_aliasing={{0}: (7, {})} | custom-call | bytes 1048576 | tf_op jit(solution)/shard_map/finish/pallas_call | solution.py:489
  (9 shorter events, 0.1 us)
Async XLA Ops:
  0.6 3.7 %collective-permute-start = (s32[1,128]{1,0:T(1,128)}, s32[1,128]{1,0:T(1,128)S(1)}, u32[]{:S(2)}, u32[]{:S(2)}) collective-permute-start(s32[1,128]{1,0:T(1,128)} %seg_hbm.1), channel_id=1, source_target_pairs={{0,1},{1,0},{2,3},{3,2},{4,5},{5,4},{6,7},{7,6},{8,9},{9,8},{10,11... | collective-permute-start | bytes 1544 | tf_op jit(solution)/shard_map/ppermute | solution.py:325
  1.1 7.7 %collective-permute-start.3 = (bf16[128,512]{1,0:T(8,128)(2,1)}, bf16[128,512]{1,0:T(8,128)(2,1)S(1)}, u32[]{:S(2)}, u32[]{:S(2)}) collective-permute-start(bf16[128,512]{1,0:T(8,128)(2,1)} %bitcast.9), channel_id=1, source_target_pairs={{0,2},{1,3},{2,0},{3,1},{4,5},{5,4},{6,7},{7,6},{8,10},{9,11},{10,... | collective-permute-start | bytes 393224 | tf_op jit(solution)/shard_map/ppermute | solution.py:339
  3.8 5.1 %collective-permute-start.2 = (bf16[128,512]{1,0:T(8,128)(2,1)}, bf16[128,512]{1,0:T(8,128)(2,1)S(1)}, u32[]{:S(2)}, u32[]{:S(2)}) collective-permute-start(bf16[128,512]{1,0:T(8,128)(2,1)} %bitcast.10), channel_id=1, source_target_pairs={{0,1},{1,0},{2,4},{3,5},{4,2},{5,3},{6,7},{7,6},{8,9},{9,8},{10,12... | collective-permute-start | bytes 393224 | tf_op jit(solution)/shard_map/ppermute | solution.py:339
  4.0 4.9 %collective-permute-start.1 = (bf16[128,512]{1,0:T(8,128)(2,1)}, bf16[128,512]{1,0:T(8,128)(2,1)S(1)}, u32[]{:S(2)}, u32[]{:S(2)}) collective-permute-start(bf16[128,512]{1,0:T(8,128)(2,1)} %bitcast.11), channel_id=1, source_target_pairs={{0,1},{1,0},{2,3},{3,2},{4,6},{5,7},{6,4},{7,5},{8,9},{9,8},{10,11... | collective-permute-start | bytes 393224 | tf_op jit(solution)/shard_map/ppermute | solution.py:339
  5.3 6.1 %collective-permute-start.6 = (bf16[144,512]{1,0:T(8,128)(2,1)S(1)}, bf16[144,512]{1,0:T(8,128)(2,1)S(1)}, u32[]{:S(2)}, u32[]{:S(2)}) collective-permute-start(bf16[144,512]{1,0:T(8,128)(2,1)S(1)} %bundle.1.v_ref.own_ref.own_ids_ref), channel_id=1, source_target_pairs={{0,2},{1,3},{2,0},{3,1},{4,6},{5,7},{6,4},{7,5},{8,10},{9,11},{10,... | collective-permute-start | bytes 442376 | tf_op jit(solution)/shard_map/ppermute | solution.py:339
  6.8 4.5 %collective-permute-start.5 = (bf16[144,512]{1,0:T(8,128)(2,1)S(1)}, bf16[144,512]{1,0:T(8,128)(2,1)S(1)}, u32[]{:S(2)}, u32[]{:S(2)}) collective-permute-start(bf16[144,512]{1,0:T(8,128)(2,1)S(1)} %bundle.1.v_ref.own_ref.own_ids_ref), channel_id=1, source_target_pairs={{0,1},{1,0},{2,4},{3,5},{4,2},{5,3},{6,7},{7,6},{8,9},{9,8},{10,12... | collective-permute-start | bytes 442376 | tf_op jit(solution)/shard_map/ppermute | solution.py:339
  9.0 2.5 %collective-permute-start.4 = (bf16[144,512]{1,0:T(8,128)(2,1)S(1)}, bf16[144,512]{1,0:T(8,128)(2,1)S(1)}, u32[]{:S(2)}, u32[]{:S(2)}) collective-permute-start(bf16[144,512]{1,0:T(8,128)(2,1)S(1)} %get-tuple-element.37), channel_id=1, source_target_pairs={{0,1},{1,0},{2,3},{3,2},{4,5},{5,4},{6,7},{7,6},{8,9},{9,8},{10,11... | collective-permute-start | bytes 442376 | tf_op jit(solution)/shard_map/ppermute | solution.py:325
  11.4 1.4 %collective-permute-start.7 = (bf16[128,512]{1,0:T(8,128)(2,1)S(1)}, bf16[128,512]{1,0:T(8,128)(2,1)S(1)}, u32[]{:S(2)}, u32[]{:S(2)}) collective-permute-start(bf16[128,512]{1,0:T(8,128)(2,1)S(1)} %get-tuple-element.41), channel_id=1, source_target_pairs={{0,1},{1,0},{2,3},{3,2},{4,5},{5,4},{6,7},{7,6},{8,9},{9,8},{10,11... | collective-permute-start | bytes 393224 | tf_op jit(solution)/shard_map/ppermute | solution.py:325
  13.5 10.1 %collective-permute-start.14 = (bf16[8,8,2048]{2,1,0:T(8,128)(2,1)S(1)}, bf16[8,8,2048]{2,1,0:T(8,128)(2,1)S(1)}, u32[]{:S(2)}, u32[]{:S(2)}) collective-permute-start(bf16[8,8,2048]{2,1,0:T(8,128)(2,1)S(1)} %get-tuple-element.54), channel_id=1, source_target_pairs={{0,24},{8,16},{16,8},{24,0},{1,25},{9,17},{17,9},{25,1},{2,26},{10... | collective-permute-start | bytes 786440 | tf_op jit(solution)/shard_map/ppermute | solution.py:348
  17.8 1.5 %collective-permute-start.10 = (bf16[128,512]{1,0:T(8,128)(2,1)S(1)}, bf16[128,512]{1,0:T(8,128)(2,1)S(1)}, u32[]{:S(2)}, u32[]{:S(2)}) collective-permute-start(bf16[128,512]{1,0:T(8,128)(2,1)S(1)} %get-tuple-element.49), channel_id=1, source_target_pairs={{0,1},{1,0},{2,3},{3,2},{4,5},{5,4},{6,7},{7,6},{8,9},{9,8},{10,11... | collective-permute-start | bytes 393224 | tf_op jit(solution)/shard_map/ppermute | solution.py:325
  17.9 1.5 %collective-permute-start.11 = (bf16[128,512]{1,0:T(8,128)(2,1)S(1)}, bf16[128,512]{1,0:T(8,128)(2,1)S(1)}, u32[]{:S(2)}, u32[]{:S(2)}) collective-permute-start(bf16[128,512]{1,0:T(8,128)(2,1)S(1)} %get-tuple-element.50), channel_id=1, source_target_pairs={{0,1},{1,0},{2,3},{3,2},{4,5},{5,4},{6,7},{7,6},{8,9},{9,8},{10,11... | collective-permute-start | bytes 393224 | tf_op jit(solution)/shard_map/ppermute | solution.py:325
  18.4 10.2 %collective-permute-start.8 = (bf16[8,8,2048]{2,1,0:T(8,128)(2,1)S(1)}, bf16[8,8,2048]{2,1,0:T(8,128)(2,1)S(1)}, u32[]{:S(2)}, u32[]{:S(2)}) collective-permute-start(bf16[8,8,2048]{2,1,0:T(8,128)(2,1)S(1)} %get-tuple-element.42), channel_id=1, source_target_pairs={{0,16},{8,24},{16,0},{24,8},{1,17},{9,25},{17,1},{25,9},{2,18},{10... | collective-permute-start | bytes 786440 | tf_op jit(solution)/shard_map/ppermute | solution.py:348
  18.9 9.9 %collective-permute-start.9 = (bf16[8,8,2048]{2,1,0:T(8,128)(2,1)S(1)}, bf16[8,8,2048]{2,1,0:T(8,128)(2,1)S(1)}, u32[]{:S(2)}, u32[]{:S(2)}) collective-permute-start(bf16[8,8,2048]{2,1,0:T(8,128)(2,1)S(1)} %get-tuple-element.43), channel_id=1, source_target_pairs={{0,8},{8,0},{16,24},{24,16},{1,9},{9,1},{17,25},{25,17},{2,10},{10... | collective-permute-start | bytes 786440 | tf_op jit(solution)/shard_map/ppermute | solution.py:348
  19.5 9.3 %collective-permute-start.13 = (bf16[256,512]{1,0:T(8,128)(2,1)S(1)}, bf16[256,512]{1,0:T(8,128)(2,1)S(1)}, u32[]{:S(2)}, u32[]{:S(2)}) collective-permute-start(bf16[256,512]{1,0:T(8,128)(2,1)S(1)} %merge.1), channel_id=1, source_target_pairs={{0,2},{1,3},{2,0},{3,1},{4,6},{5,7},{6,4},{7,5},{8,10},{9,11},{10,... | collective-permute-start | bytes 786440 | tf_op jit(solution)/shard_map/ppermute | solution.py:339
  21.3 7.5 %collective-permute-start.12 = (bf16[256,512]{1,0:T(8,128)(2,1)S(1)}, bf16[256,512]{1,0:T(8,128)(2,1)S(1)}, u32[]{:S(2)}, u32[]{:S(2)}) collective-permute-start(bf16[256,512]{1,0:T(8,128)(2,1)S(1)} %merge.1), channel_id=1, source_target_pairs={{0,1},{1,0},{2,4},{3,5},{4,2},{5,3},{6,7},{7,6},{8,9},{9,8},{10,12... | collective-permute-start | bytes 786440 | tf_op jit(solution)/shard_map/ppermute | solution.py:339

commit v9 on v8

--- a/solution.py
+++ b/solution.py
@@ -64,9 +64,7 @@
     far_bias = jnp.where(key_pos >= 2 * block - reach, joined, NEG)
     bias_n = jnp.where(key_pos >= block - reach, joined, NEG)
     bias_x = jnp.where(triangle(block, 1), bias_ref[...], far_bias)
-    bias_x = jnp.concatenate([bias_x] * GROUP, axis=1)
-    bias_n = jnp.concatenate([bias_n] * GROUP, axis=1)
-    tri_g = triangle(block, GROUP)
+    tri = triangle(block, 1)
     scaling = math.log2(math.e) / math.sqrt(HEAD_DIM)
     def products(g):
         keys = head_blocks(g, block, own_ref, far_ref, near_ref)
@@ -76,14 +74,16 @@
     upcoming = products(0)
     for g in range(heads):
         scores, upcoming = upcoming, products(g + 1) if g + 1 < heads else None
-        s_x = jnp.where(tri_g, s0_ref[g], scores[block:]) * scaling + bias_x
-        s_n = scores[0:block] * scaling + bias_n
-        highest = jnp.max(jnp.maximum(s_x, s_n), axis=0, keepdims=True)
-        e_x = jnp.exp2(s_x - highest)
-        e_n = jnp.exp2(s_n - highest)
-        inverse = 1.0 / jnp.sum(e_x + e_n, axis=0, keepdims=True)
-        p_ref[g, 0:block] = (e_x * inverse).astype(BF16)
-        p_ref[g, block : 2 * block] = (e_n * inverse).astype(BF16)
+        for h in range(GROUP):
+            cols = slice(h * block, (h + 1) * block)
+            s_x = jnp.where(tri, s0_ref[g, :, cols], scores[block:, cols]) * scaling + bias_x
+            s_n = scores[0:block, cols] * scaling + bias_n
+            highest = jnp.max(jnp.maximum(s_x, s_n), axis=0, keepdims=True)
+            e_x = jnp.exp2(s_x - highest)
+            e_n = jnp.exp2(s_n - highest)
+            inverse = 1.0 / jnp.sum(e_x + e_n, axis=0, keepdims=True)
+            p_ref[g, 0:block, cols] = (e_x * inverse).astype(BF16)
+            p_ref[g, block : 2 * block, cols] = (e_n * inverse).astype(BF16)
 
 
 def attend_kernel(n_dp, home_hbm, p_ref, own_ref, far_ref, near_ref, *rest):

time: 29.9 us -> 29.8 us (level)
  no operation moved by 1% of the time
where the time goes in v9:
time: 29.8 us; the launch traced here: 29.7 us
  starting transfers between devices  11.9 us (40%)
  Pallas kernels  9.7 us (33%)
  waiting for transfers between devices  7.33 us (25%)
  between operations  0.76 us (3%)
    ppermute x7, starting transfers between devices, from_chip(): lax.ppermute(value, 'ctx', pairs(colour))  6.81 us
    ppermute x3, waiting for transfers between devices, exchange(): return lax.ppermute(value, 'dp', pairs)  4.91 us
    ppermute x3, starting transfers between devices, exchange(): return lax.ppermute(value, 'dp', pairs)  3.56 us
    ppermute x7, waiting for transfers between devices, from_chip(): lax.ppermute(value, 'ctx', pairs(colour))  2.05 us
    pallas_call x1, Pallas kernels, on_device(): pl.pallas_call(ahead_kernel, out_shape=[jax.ShapeDtypeStruct(home_rows.sh...  1.81 us
    pallas_call x1, Pallas kernels, on_device(): pl.pallas_call(kept_kernel, out_shape=[jax.ShapeDtypeStruct((block, width...  1.68 us
    pallas_call x1, Pallas kernels, on_device(): pl.pallas_call(sent_kernel, out_shape=[jax.ShapeDtypeStruct(weights.shape...  1.64 us
    ppermute x5, starting transfers between devices, swap(): return lax.ppermute(value, 'ctx', [(i, i ^ 1) for i in range(count)])  1.5 us
  transfers between devices with their start and end apart: 15, of which 6 were waited for; matrix products, arithmetic and copies ran while one was open for 0% of the time, Pallas kernels for 27%

profile of v9, /device:TPU:0, one launch (start us, length us, event | category | flops | bytes accessed | tf_op | source)
XLA Modules:
  0.0 29.7 jit_solution(2972196641490160066)
XLA Ops:
  0.6 0.5 %collective-permute-start = (s32[1,128]{1,0:T(1,128)}, s32[1,128]{1,0:T(1,128)S(1)}, u32[]{:S(2)}, u32[]{:S(2)}) collective-permute-start(s32[1,128]{1,0:T(1,128)} %seg_hbm.1), channel_id=1, source_target_pairs={{0,1},{1,0},{2,3},{3,2},{4,5},{5,4},{6,7},{7,6},{8,9},{9,8},{10,11... | collective-permute-start | bytes 1544 | tf_op jit(solution)/shard_map/ppermute | solution.py:325
  1.1 2.6 %collective-permute-start.3 = (bf16[128,512]{1,0:T(8,128)(2,1)}, bf16[128,512]{1,0:T(8,128)(2,1)S(1)}, u32[]{:S(2)}, u32[]{:S(2)}) collective-permute-start(bf16[128,512]{1,0:T(8,128)(2,1)} %bitcast.9), channel_id=1, source_target_pairs={{0,2},{1,3},{2,0},{3,1},{4,5},{5,4},{6,7},{7,6},{8,10},{9,11},{10,... | collective-permute-start | bytes 393224 | tf_op jit(solution)/shard_map/ppermute | solution.py:339
  3.8 0.2 collective-permute-start.2
  4.0 0.3 %collective-permute-start.1 = (bf16[128,512]{1,0:T(8,128)(2,1)}, bf16[128,512]{1,0:T(8,128)(2,1)S(1)}, u32[]{:S(2)}, u32[]{:S(2)}) collective-permute-start(bf16[128,512]{1,0:T(8,128)(2,1)} %bitcast.11), channel_id=1, source_target_pairs={{0,1},{1,0},{2,3},{3,2},{4,6},{5,7},{6,4},{7,5},{8,9},{9,8},{10,11... | collective-permute-start | bytes 393224 | tf_op jit(solution)/shard_map/ppermute | solution.py:339
  4.3 0.0 collective-permute-done.other_ref
  4.3 0.9 %bundle.1.v_ref.own_ref.own_ids_ref = bf16[144,512]{1,0:T(8,128)(2,1)S(1)} custom-call(s32[1,128]{1,0:T(1,128)} %seg_hbm.1, s32[1,128]{1,0:T(1,128)S(1)} %collective-permute-done.other_ref, bf16[128,512]{1,0:T(8,128)(2,1)} %bitcast.13), custom_call_target="tpu_custom_call" | custom-call | tf_op jit(solution)/shard_map/bundle/pallas_call | solution.py:363
  5.3 1.6 %collective-permute-start.6 = (bf16[144,512]{1,0:T(8,128)(2,1)S(1)}, bf16[144,512]{1,0:T(8,128)(2,1)S(1)}, u32[]{:S(2)}, u32[]{:S(2)}) collective-permute-start(bf16[144,512]{1,0:T(8,128)(2,1)S(1)} %bundle.1.v_ref.own_ref.own_ids_ref), channel_id=1, source_target_pairs={{0,2},{1,3},{2,0},{3,1},{4,6},{5,7},{6,4},{7,5},{8,10},{9,11},{10,... | collective-permute-start | bytes 442376 | tf_op jit(solution)/shard_map/ppermute | solution.py:339
  6.8 0.2 collective-permute-start.5
  7.1 1.8 %ahead.1 = (s32[1,16]{1,0:T(1,128)S(1)}, bf16[4,128,512]{2,1,0:T(8,128)(2,1)S(1)}, bf16[4,128,512]{2,1,0:T(8,128)(2,1)S(1)}, f32[4,128,512]{2,1,0:T(8,128)S(1)},...) custom-call(s32[1,16]{1,0:T(1,128)} %home_hbm.1, ...), custom_call_target="tpu_custom_call" | custom-call | tf_op jit(solution)/shard_map/ahead/pallas_call | solution.py:377
  8.9 0.0 collective-permute-done.3.rest_2_
  9.0 0.3 %collective-permute-start.4 = (bf16[144,512]{1,0:T(8,128)(2,1)S(1)}, bf16[144,512]{1,0:T(8,128)(2,1)S(1)}, u32[]{:S(2)}, u32[]{:S(2)}) collective-permute-start(bf16[144,512]{1,0:T(8,128)(2,1)S(1)} %get-tuple-element.37), channel_id=1, source_target_pairs={{0,1},{1,0},{2,3},{3,2},{4,5},{5,4},{6,7},{7,6},{8,9},{9,8},{10,11... | collective-permute-start | bytes 442376 | tf_op jit(solution)/shard_map/ppermute | solution.py:325
  9.3 2.0 %collective-permute-done.6.rest_1_ = bf16[144,512]{1,0:T(8,128)(2,1)S(1)} collective-permute-done((bf16[144,512]{1,0:T(8,128)(2,1)S(1)}, bf16[144,512]{1,0:T(8,128)(2,1)S(1)}, u32[]{:S(2)}, u32[]{:S(2)}) %collective-permute-start.6) | collective-permute-done | bytes 147488 | tf_op jit(solution)/shard_map/ppermute | solution.py:339
  11.4 0.1 collective-permute-start.7
  11.5 1.0 %weights.1.p_ref = bf16[4,256,512]{2,1,0:T(8,128)(2,1)S(1)} custom-call(bf16[4,128,512]{2,1,0:T(8,128)(2,1)S(1)} %get-tuple-element.33.qt_ref, f32[4,128,512]{2,1,0:T(8,128)S(1)} %get-tuple-element.34.s0_ref, bf16[128,512]{1,0:T(8,128)(2,1)S(1)} %get-tuple-element.35.own_ref, bf16[128,512]{1,0:T(8,128)(2,1)S(1)} %get-tuple-element.36.far_ref, ...), custom_call_target="tpu_custom_call" | custom-call | tf_op jit(solution)/shard_map/weights/pallas_call | solution.py:416
  12.5 0.3 %collective-permute-done.7.near_ref = bf16[128,512]{1,0:T(8,128)(2,1)S(1)} collective-permute-done((bf16[128,512]{1,0:T(8,128)(2,1)S(1)}, bf16[128,512]{1,0:T(8,128)(2,1)S(1)}, u32[]{:S(2)}, u32[]{:S(2)}) %collective-permute-start.7) | collective-permute-done | bytes 131104 | tf_op jit(solution)/shard_map/ppermute | solution.py:325
  12.8 0.7 %attend.1 = (bf16[8,8,2048]{2,1,0:T(8,128)(2,1)S(1)}, bf16[8,8,2048]{2,1,0:T(8,128)(2,1)S(1)}, bf16[8,8,2048]{2,1,0:T(8,128)(2,1)S(1)}, bf16[8,8,2048]{2,1,0:T(8,128)(2,1)S(1)}) custom-call(s32[1,16]{1,0:T(1,128)S(1)} %get-tuple-element.32.rest_3_.rest_2_.home_hbm, bf16[4,256,512]{2,1,0:T(8,128)(2,1)S(1)} %weights.1.p_ref, ...), custom_call_target="tpu_custom_call" | custom-call | tf_op jit(solution)/shard_map/attend/pallas_call | solution.py:425
  13.5 2.6 %collective-permute-start.14 = (bf16[8,8,2048]{2,1,0:T(8,128)(2,1)S(1)}, bf16[8,8,2048]{2,1,0:T(8,128)(2,1)S(1)}, u32[]{:S(2)}, u32[]{:S(2)}) collective-permute-start(bf16[8,8,2048]{2,1,0:T(8,128)(2,1)S(1)} %get-tuple-element.54), channel_id=1, source_target_pairs={{0,24},{8,16},{16,8},{24,0},{1,25},{9,17},{17,9},{25,1},{2,26},{10... | collective-permute-start | bytes 786440 | tf_op jit(solution)/shard_map/ppermute | solution.py:348
  16.1 1.6 %sent_terms.1 = (bf16[4,256,512]{2,1,0:T(8,128)(2,1)S(1)}, bf16[256,512]{1,0:T(8,128)(2,1)S(1)}, bf16[128,512]{1,0:T(8,128)(2,1)S(1)}, bf16[128,512]{1,0:T(8,128)(2,1)S(1)}) custom-call(bf16[128,2048]{1,0:T(8,128)(2,1)S(1)} %get-tuple-element.44.q_ref, bf16[128,2048]{1,0:T(8,128)(2,1)S(1)} %get-tuple-element.45.do_ref, ...), custom_call_target="tpu_custom_call" | custom-call | tf_op jit(solution)/shard_map/sent_terms/pallas_call | solution.py:445
  17.8 0.1 collective-permute-start.10
  17.9 0.5 %collective-permute-start.11 = (bf16[128,512]{1,0:T(8,128)(2,1)S(1)}, bf16[128,512]{1,0:T(8,128)(2,1)S(1)}, u32[]{:S(2)}, u32[]{:S(2)}) collective-permute-start(bf16[128,512]{1,0:T(8,128)(2,1)S(1)} %get-tuple-element.50), channel_id=1, source_target_pairs={{0,1},{1,0},{2,3},{3,2},{4,5},{5,4},{6,7},{7,6},{8,9},{9,8},{10,11... | collective-permute-start | bytes 393224 | tf_op jit(solution)/shard_map/ppermute | solution.py:325
  18.4 0.5 %collective-permute-start.8 = (bf16[8,8,2048]{2,1,0:T(8,128)(2,1)S(1)}, bf16[8,8,2048]{2,1,0:T(8,128)(2,1)S(1)}, u32[]{:S(2)}, u32[]{:S(2)}) collective-permute-start(bf16[8,8,2048]{2,1,0:T(8,128)(2,1)S(1)} %get-tuple-element.42), channel_id=1, source_target_pairs={{0,16},{8,24},{16,0},{24,8},{1,17},{9,25},{17,1},{25,9},{2,18},{10... | collective-permute-start | bytes 786440 | tf_op jit(solution)/shard_map/ppermute | solution.py:348
  18.9 0.4 %collective-permute-start.9 = (bf16[8,8,2048]{2,1,0:T(8,128)(2,1)S(1)}, bf16[8,8,2048]{2,1,0:T(8,128)(2,1)S(1)}, u32[]{:S(2)}, u32[]{:S(2)}) collective-permute-start(bf16[8,8,2048]{2,1,0:T(8,128)(2,1)S(1)} %get-tuple-element.43), channel_id=1, source_target_pairs={{0,8},{8,0},{16,24},{24,16},{1,9},{9,1},{17,25},{25,17},{2,10},{10... | collective-permute-start | bytes 786440 | tf_op jit(solution)/shard_map/ppermute | solution.py:348
  19.3 0.1 collective-permute-done.11.dv1_ref.rest_5_
  19.4 0.1 merge.1
  19.5 1.8 %collective-permute-start.13 = (bf16[256,512]{1,0:T(8,128)(2,1)S(1)}, bf16[256,512]{1,0:T(8,128)(2,1)S(1)}, u32[]{:S(2)}, u32[]{:S(2)}) collective-permute-start(bf16[256,512]{1,0:T(8,128)(2,1)S(1)} %merge.1), channel_id=1, source_target_pairs={{0,2},{1,3},{2,0},{3,1},{4,6},{5,7},{6,4},{7,5},{8,10},{9,11},{10,... | collective-permute-start | bytes 786440 | tf_op jit(solution)/shard_map/ppermute | solution.py:339
  21.3 0.0 collective-permute-start.12
  21.3 1.7 %kept_terms.1 = (bf16[128,2048]{1,0:T(8,128)(2,1)}, f32[256,512]{1,0:T(8,128)S(1)}, f32[8,128]{1,0:T(8,128)S(1)}) custom-call(bf16[128,2048]{1,0:T(8,128)(2,1)S(1)} %get-tuple-element.44.q_ref, bf16[128,2048]{1,0:T(8,128)(2,1)S(1)} %get-tuple-element.45.do_ref, bf16[128,512]{1,0:T(8,128)(2,1)S(1)} %get-tuple-element.35.own_ref, ...), custom_call_target="tpu_custom_call" | custom-call | flops 1073741824 | tf_op jit(solution)/shard_map/kept_terms/pallas_call | solution.py:454
  23.0 0.5 %collective-permute-done.14.far_ref = bf16[8,8,2048]{2,1,0:T(8,128)(2,1)S(1)} collective-permute-done((bf16[8,8,2048]{2,1,0:T(8,128)(2,1)S(1)}, bf16[8,8,2048]{2,1,0:T(8,128)(2,1)S(1)}, u32[]{:S(2)}, u32[]{:S(2)}) %collective-permute-start.14) | collective-permute-done | bytes 262176 | tf_op jit(solution)/shard_map/ppermute | solution.py:348
  23.5 0.8 %place_early.1.rest_7_ = bf16[1,1,4,8,8,2048]{5,4,3,2,1,0:T(8,128)(2,1)} custom-call(f32[8,128]{1,0:T(8,128)S(1)} %get-tuple-element.53.kept_ref, bf16[8,8,2048]{2,1,0:T(8,128)(2,1)S(1)} %collective-permute-done.14.far_ref, bf16[8,8,2048]{2,1,0:T(8,128)(2,1)S(1)} %get-tuple-element.55.own_ref), custom_call_target="tpu_custom_call" | custom-call | flops 2147483648 | tf_op jit(solution)/shard_map/place_early/pallas_call | solution.py:479
  24.4 4.2 %collective-permute-done.8.rest_0_ = bf16[8,8,2048]{2,1,0:T(8,128)(2,1)S(1)} collective-permute-done((bf16[8,8,2048]{2,1,0:T(8,128)(2,1)S(1)}, bf16[8,8,2048]{2,1,0:T(8,128)(2,1)S(1)}, u32[]{:S(2)}, u32[]{:S(2)}) %collective-permute-start.8) | collective-permute-done | bytes 262176 | tf_op jit(solution)/shard_map/ppermute | solution.py:348
  28.5 0.2 collective-permute-done.9.rest_1_
  28.7 0.9 %finish.1 = (bf16[1,1,4,8,8,2048]{5,4,3,2,1,0:T(8,128)(2,1)}, bf16[128,512]{1,0:T(8,128)(2,1)}, bf16[128,512]{1,0:T(8,128)(2,1)}) custom-call(bf16[8,8,2048]{2,1,0:T(8,128)(2,1)S(1)} %collective-permute-done.8.rest_0_, bf16[8,8,2048]{2,1,0:T(8,128)(2,1)S(1)} %collective-permute-done.9.rest_1_, ...), custom_call_target="tpu_custom_call", output_to_operand_aliasing={{0}: (7, {})} | custom-call | bytes 1048576 | tf_op jit(solution)/shard_map/finish/pallas_call | solution.py:489
  (9 shorter events, 0.1 us)
Async XLA Ops:
  0.6 3.7 %collective-permute-start = (s32[1,128]{1,0:T(1,128)}, s32[1,128]{1,0:T(1,128)S(1)}, u32[]{:S(2)}, u32[]{:S(2)}) collective-permute-start(s32[1,128]{1,0:T(1,128)} %seg_hbm.1), channel_id=1, source_target_pairs={{0,1},{1,0},{2,3},{3,2},{4,5},{5,4},{6,7},{7,6},{8,9},{9,8},{10,11... | collective-permute-start | bytes 1544 | tf_op jit(solution)/shard_map/ppermute | solution.py:325
  1.1 7.7 %collective-permute-start.3 = (bf16[128,512]{1,0:T(8,128)(2,1)}, bf16[128,512]{1,0:T(8,128)(2,1)S(1)}, u32[]{:S(2)}, u32[]{:S(2)}) collective-permute-start(bf16[128,512]{1,0:T(8,128)(2,1)} %bitcast.9), channel_id=1, source_target_pairs={{0,2},{1,3},{2,0},{3,1},{4,5},{5,4},{6,7},{7,6},{8,10},{9,11},{10,... | collective-permute-start | bytes 393224 | tf_op jit(solution)/shard_map/ppermute | solution.py:339
  3.8 5.1 %collective-permute-start.2 = (bf16[128,512]{1,0:T(8,128)(2,1)}, bf16[128,512]{1,0:T(8,128)(2,1)S(1)}, u32[]{:S(2)}, u32[]{:S(2)}) collective-permute-start(bf16[128,512]{1,0:T(8,128)(2,1)} %bitcast.10), channel_id=1, source_target_pairs={{0,1},{1,0},{2,4},{3,5},{4,2},{5,3},{6,7},{7,6},{8,9},{9,8},{10,12... | collective-permute-start | bytes 393224 | tf_op jit(solution)/shard_map/ppermute | solution.py:339
  4.0 4.9 %collective-permute-start.1 = (bf16[128,512]{1,0:T(8,128)(2,1)}, bf16[128,512]{1,0:T(8,128)(2,1)S(1)}, u32[]{:S(2)}, u32[]{:S(2)}) collective-permute-start(bf16[128,512]{1,0:T(8,128)(2,1)} %bitcast.11), channel_id=1, source_target_pairs={{0,1},{1,0},{2,3},{3,2},{4,6},{5,7},{6,4},{7,5},{8,9},{9,8},{10,11... | collective-permute-start | bytes 393224 | tf_op jit(solution)/shard_map/ppermute | solution.py:339
  5.3 6.1 %collective-permute-start.6 = (bf16[144,512]{1,0:T(8,128)(2,1)S(1)}, bf16[144,512]{1,0:T(8,128)(2,1)S(1)}, u32[]{:S(2)}, u32[]{:S(2)}) collective-permute-start(bf16[144,512]{1,0:T(8,128)(2,1)S(1)} %bundle.1.v_ref.own_ref.own_ids_ref), channel_id=1, source_target_pairs={{0,2},{1,3},{2,0},{3,1},{4,6},{5,7},{6,4},{7,5},{8,10},{9,11},{10,... | collective-permute-start | bytes 442376 | tf_op jit(solution)/shard_map/ppermute | solution.py:339
  6.8 4.5 %collective-permute-start.5 = (bf16[144,512]{1,0:T(8,128)(2,1)S(1)}, bf16[144,512]{1,0:T(8,128)(2,1)S(1)}, u32[]{:S(2)}, u32[]{:S(2)}) collective-permute-start(bf16[144,512]{1,0:T(8,128)(2,1)S(1)} %bundle.1.v_ref.own_ref.own_ids_ref), channel_id=1, source_target_pairs={{0,1},{1,0},{2,4},{3,5},{4,2},{5,3},{6,7},{7,6},{8,9},{9,8},{10,12... | collective-permute-start | bytes 442376 | tf_op jit(solution)/shard_map/ppermute | solution.py:339
  9.0 2.5 %collective-permute-start.4 = (bf16[144,512]{1,0:T(8,128)(2,1)S(1)}, bf16[144,512]{1,0:T(8,128)(2,1)S(1)}, u32[]{:S(2)}, u32[]{:S(2)}) collective-permute-start(bf16[144,512]{1,0:T(8,128)(2,1)S(1)} %get-tuple-element.37), channel_id=1, source_target_pairs={{0,1},{1,0},{2,3},{3,2},{4,5},{5,4},{6,7},{7,6},{8,9},{9,8},{10,11... | collective-permute-start | bytes 442376 | tf_op jit(solution)/shard_map/ppermute | solution.py:325
  11.4 1.4 %collective-permute-start.7 = (bf16[128,512]{1,0:T(8,128)(2,1)S(1)}, bf16[128,512]{1,0:T(8,128)(2,1)S(1)}, u32[]{:S(2)}, u32[]{:S(2)}) collective-permute-start(bf16[128,512]{1,0:T(8,128)(2,1)S(1)} %get-tuple-element.41), channel_id=1, source_target_pairs={{0,1},{1,0},{2,3},{3,2},{4,5},{5,4},{6,7},{7,6},{8,9},{9,8},{10,11... | collective-permute-start | bytes 393224 | tf_op jit(solution)/shard_map/ppermute | solution.py:325
  13.5 10.0 %collective-permute-start.14 = (bf16[8,8,2048]{2,1,0:T(8,128)(2,1)S(1)}, bf16[8,8,2048]{2,1,0:T(8,128)(2,1)S(1)}, u32[]{:S(2)}, u32[]{:S(2)}) collective-permute-start(bf16[8,8,2048]{2,1,0:T(8,128)(2,1)S(1)} %get-tuple-element.54), channel_id=1, source_target_pairs={{0,24},{8,16},{16,8},{24,0},{1,25},{9,17},{17,9},{25,1},{2,26},{10... | collective-permute-start | bytes 786440 | tf_op jit(solution)/shard_map/ppermute | solution.py:348
  17.8 1.5 %collective-permute-start.10 = (bf16[128,512]{1,0:T(8,128)(2,1)S(1)}, bf16[128,512]{1,0:T(8,128)(2,1)S(1)}, u32[]{:S(2)}, u32[]{:S(2)}) collective-permute-start(bf16[128,512]{1,0:T(8,128)(2,1)S(1)} %get-tuple-element.49), channel_id=1, source_target_pairs={{0,1},{1,0},{2,3},{3,2},{4,5},{5,4},{6,7},{7,6},{8,9},{9,8},{10,11... | collective-permute-start | bytes 393224 | tf_op jit(solution)/shard_map/ppermute | solution.py:325
  17.9 1.5 %collective-permute-start.11 = (bf16[128,512]{1,0:T(8,128)(2,1)S(1)}, bf16[128,512]{1,0:T(8,128)(2,1)S(1)}, u32[]{:S(2)}, u32[]{:S(2)}) collective-permute-start(bf16[128,512]{1,0:T(8,128)(2,1)S(1)} %get-tuple-element.50), channel_id=1, source_target_pairs={{0,1},{1,0},{2,3},{3,2},{4,5},{5,4},{6,7},{7,6},{8,9},{9,8},{10,11... | collective-permute-start | bytes 393224 | tf_op jit(solution)/shard_map/ppermute | solution.py:325
  18.4 10.2 %collective-permute-start.8 = (bf16[8,8,2048]{2,1,0:T(8,128)(2,1)S(1)}, bf16[8,8,2048]{2,1,0:T(8,128)(2,1)S(1)}, u32[]{:S(2)}, u32[]{:S(2)}) collective-permute-start(bf16[8,8,2048]{2,1,0:T(8,128)(2,1)S(1)} %get-tuple-element.42), channel_id=1, source_target_pairs={{0,16},{8,24},{16,0},{24,8},{1,17},{9,25},{17,1},{25,9},{2,18},{10... | collective-permute-start | bytes 786440 | tf_op jit(solution)/shard_map/ppermute | solution.py:348
  18.9 9.9 %collective-permute-start.9 = (bf16[8,8,2048]{2,1,0:T(8,128)(2,1)S(1)}, bf16[8,8,2048]{2,1,0:T(8,128)(2,1)S(1)}, u32[]{:S(2)}, u32[]{:S(2)}) collective-permute-start(bf16[8,8,2048]{2,1,0:T(8,128)(2,1)S(1)} %get-tuple-element.43), channel_id=1, source_target_pairs={{0,8},{8,0},{16,24},{24,16},{1,9},{9,1},{17,25},{25,17},{2,10},{10... | collective-permute-start | bytes 786440 | tf_op jit(solution)/shard_map/ppermute | solution.py:348
  19.5 9.3 %collective-permute-start.13 = (bf16[256,512]{1,0:T(8,128)(2,1)S(1)}, bf16[256,512]{1,0:T(8,128)(2,1)S(1)}, u32[]{:S(2)}, u32[]{:S(2)}) collective-permute-start(bf16[256,512]{1,0:T(8,128)(2,1)S(1)} %merge.1), channel_id=1, source_target_pairs={{0,2},{1,3},{2,0},{3,1},{4,6},{5,7},{6,4},{7,5},{8,10},{9,11},{10,... | collective-permute-start | bytes 786440 | tf_op jit(solution)/shard_map/ppermute | solution.py:339
  21.3 7.4 %collective-permute-start.12 = (bf16[256,512]{1,0:T(8,128)(2,1)S(1)}, bf16[256,512]{1,0:T(8,128)(2,1)S(1)}, u32[]{:S(2)}, u32[]{:S(2)}) collective-permute-start(bf16[256,512]{1,0:T(8,128)(2,1)S(1)} %merge.1), channel_id=1, source_target_pairs={{0,1},{1,0},{2,4},{3,5},{4,2},{5,3},{6,7},{7,6},{8,9},{9,8},{10,12... | collective-permute-start | bytes 786440 | tf_op jit(solution)/shard_map/ppermute | solution.py:339
